TPU v7x, 32 devices: a whole 2x2x4 slice. The times are simulated.
32 devices in a mesh: dp: 4 (over z), fsdp: 8 (over y, x, core).
Axes of the slice: x: 2, y: 2, z: 4, core: 2. Of those that a mesh axis runs over, the one named last changes fastest.
Arguments:
- decoder_in: bfloat16 [256, 256, 512], P(('dp', 'fsdp')), may hold values from -6 to 6
- memory: bfloat16 [256, 256, 512], P(('dp', 'fsdp')), may hold values from -6 to 6
- out_grad: bfloat16 [256, 256, 512], P(('dp', 'fsdp')), may hold values from -6 to 6
- tgt_len: int32 [256, 24], P(('dp', 'fsdp')), may hold values from 0 to 250, as said below
- src_len: int32 [256, 24], P(('dp', 'fsdp')), may hold values from 0 to 250, as said below
- self_qkv: bfloat16 [3, 512, 512], P(None, None, ('dp', 'fsdp')), may hold values from -0.25 to 0.25
- self_bias: bfloat16 [3, 512], P(None, ('dp', 'fsdp')), may hold values from -2 to 2
- self_out: bfloat16 [512, 512], P(None, ('dp', 'fsdp')), may hold values from -0.75 to 0.75
- self_norm: bfloat16 [2, 512], P(None, ('dp', 'fsdp')), may hold values from -0.5 to 1.4, as said below
- cross_q: bfloat16 [512, 512], P(None, ('dp', 'fsdp')), may hold values from -0.25 to 0.25
- cross_kv: bfloat16 [2, 512, 512], P(None, None, ('dp', 'fsdp')), may hold values from -0.25 to 0.25
- cross_bias: bfloat16 [3, 512], P(None, ('dp', 'fsdp')), may hold values from -2 to 2
- cross_out: bfloat16 [512, 512], P(None, ('dp', 'fsdp')), may hold values from -0.5 to 0.5
- cross_norm: bfloat16 [2, 512], P(None, ('dp', 'fsdp')), may hold values from -0.5 to 1.4, as said below
- ffn_in: bfloat16 [512, 2048], P(None, ('dp', 'fsdp')), may hold values from -0.25 to 0.25
- ffn_in_bias: bfloat16 [2048], P(('dp', 'fsdp')), may hold values from -2 to 2
- ffn_out: bfloat16 [2048, 512], P(None, ('dp', 'fsdp')), may hold values from -0.1875 to 0.1875
- ffn_out_bias: bfloat16 [512], P(('dp', 'fsdp')), may hold values from -2 to 2
- ffn_norm: bfloat16 [2, 512], P(None, ('dp', 'fsdp')), may hold values from -0.5 to 1.4, as said below
Outputs:
- decoder_out: bfloat16 [256, 256, 512], P(('dp', 'fsdp'))
- grad_decoder_in: bfloat16 [256, 256, 512], P(('dp', 'fsdp'))
- grad_memory: bfloat16 [256, 256, 512], P(('dp', 'fsdp'))
- grad_self_qkv: float32 [3, 512, 512], P(None, None, ('dp', 'fsdp'))
- grad_self_bias: float32 [3, 512], P(None, ('dp', 'fsdp'))
- grad_self_out: float32 [512, 512], P(None, ('dp', 'fsdp'))
- grad_self_norm: float32 [2, 512], P(None, ('dp', 'fsdp'))
- grad_cross_q: float32 [512, 512], P(None, ('dp', 'fsdp'))
- grad_cross_kv: float32 [2, 512, 512], P(None, None, ('dp', 'fsdp'))
- grad_cross_bias: float32 [3, 512], P(None, ('dp', 'fsdp'))
- grad_cross_out: float32 [512, 512], P(None, ('dp', 'fsdp'))
- grad_cross_norm: float32 [2, 512], P(None, ('dp', 'fsdp'))
- grad_ffn_in: float32 [512, 2048], P(None, ('dp', 'fsdp'))
- grad_ffn_in_bias: float32 [2048], P(('dp', 'fsdp'))
- grad_ffn_out: float32 [2048, 512], P(None, ('dp', 'fsdp'))
- grad_ffn_out_bias: float32 [512], P(('dp', 'fsdp'))
- grad_ffn_norm: float32 [2, 512], P(None, ('dp', 'fsdp'))
Inputs may be any that keep to these rules, and one draw needn't show every extreme that they name: `tgt_len`: sentence lengths in order; a row's entries sum to 256; zero marks an unused sentence slot. `src_len`: zero exactly where tgt_len is zero, otherwise from 1 to the tgt_len entry of the same slot; a row's entries sum to at most 256. `self_norm`: row 0 holds gains, row 1 shifts. `cross_norm`: row 0 holds gains, row 1 shifts. `ffn_norm`: row 0 holds gains, row 1 shifts.
All inputs are finite; a program needn't handle non-finite values.
Results may differ from a plain program's by a relative error of at most 0.018.
Values may be sent and summed in bfloat16 or wider, within the bound.
A program may use at most 320 MiB of HBM per device.

v0:
```python
import jax
import jax.numpy as jnp
from jax import lax
from jax.sharding import PartitionSpec as P

HEADS = 8
MICRO = 4


epsilon = 1e-05
masked_score = -1e30


def dense(left, right):
    return jnp.dot(left, right, preferred_element_type=jnp.float32)


def dense_back(left, right):
    return lax.dot_general(
        left, right, (((1,), (1,)), ((), ())), preferred_element_type=jnp.float32
    )


def outer_sum(left, right):
    return lax.dot_general(
        left, right, (((0,), (0,)), ((), ())), preferred_element_type=jnp.float32
    )


def column_sum(values):
    return jnp.sum(values.astype(jnp.float32), axis=0)


def gelu_tanh(values):
    return jax.nn.gelu(values, approximate=True)


def segment_ids(lengths, slot_count):
    places = jnp.arange(slot_count, dtype=jnp.int32)
    finish = jnp.cumsum(lengths, axis=-1)
    return jnp.sum((finish[:, None, :] <= places[None, :, None]).astype(jnp.int32), axis=-1)


def norm_forward(summed, table):
    gain_row = table[0].astype(jnp.float32)
    centred = summed - jnp.mean(summed, axis=-1, keepdims=True)
    inverse = lax.rsqrt(jnp.mean(centred * centred, axis=-1, keepdims=True) + epsilon)
    normed = centred * inverse
    return (normed * gain_row + table[1].astype(jnp.float32), normed, inverse)


def norm_backward(upstream, normed, inverse, table):
    scaled = upstream * table[0].astype(jnp.float32)
    adjusted = (
        scaled
        - jnp.mean(scaled, axis=-1, keepdims=True)
        - normed * jnp.mean(scaled * normed, axis=-1, keepdims=True)
    )
    return (
        adjusted * inverse,
        jnp.stack([jnp.sum(upstream * normed, axis=0), jnp.sum(upstream, axis=0)]),
    )


def split_heads(values, row_count, head_count):
    return values.reshape(row_count, -1, head_count, values.shape[-1] // head_count)


def masked_scores(query4, keys4, allowed):
    factor = query4.shape[-1] ** (-0.5)
    scores = (
        jnp.einsum("rqhe,rkhe->rhqk", query4, keys4, preferred_element_type=jnp.float32) * factor
    )
    return (jnp.where(allowed[:, None], scores, masked_score), factor)


def attend_forward(query, keys, values, allowed, row_count, head_count):
    query4 = split_heads(query, row_count, head_count)
    keys4 = split_heads(keys, row_count, head_count)
    values4 = split_heads(values, row_count, head_count)
    scores, factor = masked_scores(query4, keys4, allowed)
    ceiling = jnp.max(scores, axis=-1, keepdims=True)
    logsum = ceiling + jnp.log(jnp.sum(jnp.exp(scores - ceiling), axis=-1, keepdims=True))
    shares = jnp.exp(scores - logsum).astype(jnp.bfloat16)
    mixture = jnp.einsum("rhqk,rkhe->rqhe", shares, values4, preferred_element_type=jnp.float32)
    return (mixture.reshape(query.shape).astype(jnp.bfloat16), logsum)


def attend_backward(upstream, query, keys, values, allowed, logsum, row_count, head_count):
    query4 = split_heads(query, row_count, head_count)
    keys4 = split_heads(keys, row_count, head_count)
    values4 = split_heads(values, row_count, head_count)
    upstream4 = split_heads(upstream, row_count, head_count)
    scores, factor = masked_scores(query4, keys4, allowed)
    shares = jnp.exp(scores - logsum)
    grad_values = jnp.einsum(
        "rhqk,rqhe->rkhe",
        shares.astype(jnp.bfloat16),
        upstream4,
        preferred_element_type=jnp.float32,
    )
    grad_shares = jnp.einsum(
        "rqhe,rkhe->rhqk", upstream4, values4, preferred_element_type=jnp.float32
    )
    centre = jnp.sum(grad_shares * shares, axis=-1, keepdims=True)
    grad_scores = (shares * (grad_shares - centre)).astype(jnp.bfloat16)
    grad_query = (
        jnp.einsum("rhqk,rkhe->rqhe", grad_scores, keys4, preferred_element_type=jnp.float32)
        * factor
    )
    grad_keys = (
        jnp.einsum("rhqk,rqhe->rkhe", grad_scores, query4, preferred_element_type=jnp.float32)
        * factor
    )
    return (
        grad_query.reshape(query.shape).astype(jnp.bfloat16),
        grad_keys.reshape(keys.shape).astype(jnp.bfloat16),
        grad_values.reshape(values.shape).astype(jnp.bfloat16),
    )


def on_device(
    decoder_in,
    memory,
    out_grad,
    tgt_len,
    src_len,
    self_qkv,
    self_bias,
    self_out,
    self_norm,
    cross_q,
    cross_kv,
    cross_bias,
    cross_out,
    cross_norm,
    ffn_in,
    ffn_in_bias,
    ffn_out,
    ffn_out_bias,
    ffn_norm,
):
    attn_whole = (
        lax.all_gather(self_qkv, ("dp", "fsdp"), axis=2, tiled=True),
        lax.all_gather(self_bias, ("dp", "fsdp"), axis=1, tiled=True),
        lax.all_gather(self_out, ("dp", "fsdp"), axis=1, tiled=True),
        lax.all_gather(self_norm, ("dp", "fsdp"), axis=1, tiled=True),
        lax.all_gather(cross_q, ("dp", "fsdp"), axis=1, tiled=True),
        lax.all_gather(cross_kv, ("dp", "fsdp"), axis=2, tiled=True),
        lax.all_gather(cross_bias, ("dp", "fsdp"), axis=1, tiled=True),
        lax.all_gather(cross_out, ("dp", "fsdp"), axis=1, tiled=True),
        lax.all_gather(cross_norm, ("dp", "fsdp"), axis=1, tiled=True),
    )
    ffn_whole = (
        lax.all_gather(ffn_in, ("dp", "fsdp"), axis=1, tiled=True),
        lax.all_gather(ffn_in_bias, ("dp", "fsdp"), axis=0, tiled=True),
        lax.all_gather(ffn_out, ("dp", "fsdp"), axis=1, tiled=True),
        lax.all_gather(ffn_out_bias, ("dp", "fsdp"), axis=0, tiled=True),
        lax.all_gather(ffn_norm, ("dp", "fsdp"), axis=1, tiled=True),
    )
    head_count = HEADS
    micro_count = MICRO
    row_count = decoder_in.shape[0] // micro_count
    slot_count = decoder_in.shape[1]
    model_width = decoder_in.shape[2]
    places = jnp.arange(slot_count, dtype=jnp.int32)
    causal = places[None, :] <= places[:, None]
    target_ids = segment_ids(tgt_len, slot_count)
    source_ids = segment_ids(src_len, slot_count)
    self_allowed_all = (target_ids[:, :, None] == target_ids[:, None, :]) & causal[None]
    cross_allowed_all = target_ids[:, :, None] == source_ids[:, None, :]
    (
        qkv_self,
        bias_self,
        out_self,
        norm_self,
        query_cross,
        pair_cross,
        bias_cross,
        out_cross,
        norm_cross,
    ) = attn_whole
    weight_in, bias_in, weight_out, bias_out, norm_ffn = ffn_whole
    outputs = []
    stored = []
    for micro_step in range(micro_count):
        row_start = micro_step * row_count
        source = decoder_in[row_start : row_start + row_count].reshape(-1, model_width)
        remote = memory[row_start : row_start + row_count].reshape(-1, model_width)
        self_allowed = self_allowed_all[row_start : row_start + row_count]
        cross_allowed = cross_allowed_all[row_start : row_start + row_count]
        triple_proj = jnp.einsum(
            "td,cde->cte", source, qkv_self, preferred_element_type=jnp.float32
        )
        query_one = (triple_proj[0] + bias_self[0]).astype(jnp.bfloat16)
        keys_one = triple_proj[1].astype(jnp.bfloat16)
        values_one = (triple_proj[2] + bias_self[1]).astype(jnp.bfloat16)
        mixture_one, logsum_one = attend_forward(
            query_one, keys_one, values_one, self_allowed, row_count, head_count
        )
        summed_one = source.astype(jnp.float32) + dense(mixture_one, out_self) + bias_self[2]
        hidden_one, normed_one, inverse_one = norm_forward(summed_one, norm_self)
        hidden_low = hidden_one.astype(jnp.bfloat16)
        query_two = (dense(hidden_low, query_cross) + bias_cross[0]).astype(jnp.bfloat16)
        pair_proj = jnp.einsum(
            "td,cde->cte", remote, pair_cross, preferred_element_type=jnp.float32
        )
        keys_two = pair_proj[0].astype(jnp.bfloat16)
        values_two = (pair_proj[1] + bias_cross[1]).astype(jnp.bfloat16)
        mixture_two, logsum_two = attend_forward(
            query_two, keys_two, values_two, cross_allowed, row_count, head_count
        )
        summed_two = hidden_one + dense(mixture_two, out_cross) + bias_cross[2]
        hidden_two, normed_two, inverse_two = norm_forward(summed_two, norm_cross)
        second_low = hidden_two.astype(jnp.bfloat16)
        expanded = dense(second_low, weight_in) + bias_in
        activated = gelu_tanh(expanded).astype(jnp.bfloat16)
        summed_three = hidden_two + dense(activated, weight_out) + bias_out
        result, normed_three, inverse_three = norm_forward(summed_three, norm_ffn)
        outputs.append(result.astype(jnp.bfloat16).reshape(row_count, slot_count, model_width))
        stored.append(
            (
                source,
                remote,
                query_one,
                keys_one,
                values_one,
                mixture_one,
                logsum_one,
                normed_one,
                inverse_one,
                hidden_low,
                query_two,
                keys_two,
                values_two,
                mixture_two,
                logsum_two,
                normed_two,
                inverse_two,
                second_low,
                expanded,
                activated,
                normed_three,
                inverse_three,
            )
        )
    ffn_back = (
        lax.all_gather(ffn_in, ("dp", "fsdp"), axis=1, tiled=True),
        lax.all_gather(ffn_in_bias, ("dp", "fsdp"), axis=0, tiled=True),
        lax.all_gather(ffn_out, ("dp", "fsdp"), axis=1, tiled=True),
        lax.all_gather(ffn_out_bias, ("dp", "fsdp"), axis=0, tiled=True),
        lax.all_gather(ffn_norm, ("dp", "fsdp"), axis=1, tiled=True),
    )
    attn_back = (
        lax.all_gather(self_qkv, ("dp", "fsdp"), axis=2, tiled=True),
        lax.all_gather(self_bias, ("dp", "fsdp"), axis=1, tiled=True),
        lax.all_gather(self_out, ("dp", "fsdp"), axis=1, tiled=True),
        lax.all_gather(self_norm, ("dp", "fsdp"), axis=1, tiled=True),
        lax.all_gather(cross_q, ("dp", "fsdp"), axis=1, tiled=True),
        lax.all_gather(cross_kv, ("dp", "fsdp"), axis=2, tiled=True),
        lax.all_gather(cross_bias, ("dp", "fsdp"), axis=1, tiled=True),
        lax.all_gather(cross_out, ("dp", "fsdp"), axis=1, tiled=True),
        lax.all_gather(cross_norm, ("dp", "fsdp"), axis=1, tiled=True),
    )
    (
        qkv_self,
        bias_self,
        out_self,
        norm_self,
        query_cross,
        pair_cross,
        bias_cross,
        out_cross,
        norm_cross,
    ) = attn_back
    weight_in, bias_in, weight_out, bias_out, norm_ffn = ffn_back
    grad_totals = [
        jnp.zeros(part.shape, jnp.float32) for part in tuple(attn_back) + tuple(ffn_back)
    ]
    grad_inputs = [None] * micro_count
    grad_remote = [None] * micro_count
    for micro_step in reversed(range(micro_count)):
        (
            source,
            remote,
            query_one,
            keys_one,
            values_one,
            mixture_one,
            logsum_one,
            normed_one,
            inverse_one,
            hidden_low,
            query_two,
            keys_two,
            values_two,
            mixture_two,
            logsum_two,
            normed_two,
            inverse_two,
            second_low,
            expanded,
            activated,
            normed_three,
            inverse_three,
        ) = stored[micro_step]
        row_start = micro_step * row_count
        self_allowed = self_allowed_all[row_start : row_start + row_count]
        cross_allowed = cross_allowed_all[row_start : row_start + row_count]
        upstream = (
            out_grad[row_start : row_start + row_count].reshape(-1, model_width).astype(jnp.float32)
        )
        sum_three, grad_norm_three = norm_backward(upstream, normed_three, inverse_three, norm_ffn)
        grad_three = sum_three.astype(jnp.bfloat16)
        grad_totals[13] = grad_totals[13] + grad_norm_three
        grad_totals[12] = grad_totals[12] + column_sum(grad_three)
        grad_totals[11] = grad_totals[11] + outer_sum(activated, grad_three)
        grad_active = dense_back(grad_three, weight_out)
        grad_expanded = jax.vjp(gelu_tanh, expanded)[1](grad_active)[0].astype(jnp.bfloat16)
        grad_totals[10] = grad_totals[10] + column_sum(grad_expanded)
        grad_totals[9] = grad_totals[9] + outer_sum(second_low, grad_expanded)
        grad_hidden_two = sum_three + dense_back(grad_expanded, weight_in)
        sum_two, grad_norm_two = norm_backward(grad_hidden_two, normed_two, inverse_two, norm_cross)
        grad_two = sum_two.astype(jnp.bfloat16)
        grad_totals[8] = grad_totals[8] + grad_norm_two
        grad_totals[7] = grad_totals[7] + outer_sum(mixture_two, grad_two)
        grad_mixture_two = dense_back(grad_two, out_cross).astype(jnp.bfloat16)
        cross_grad_query, cross_grad_keys, cross_grad_values = attend_backward(
            grad_mixture_two,
            query_two,
            keys_two,
            values_two,
            cross_allowed,
            logsum_two,
            row_count,
            head_count,
        )
        grad_totals[6] = grad_totals[6] + jnp.stack(
            [column_sum(cross_grad_query), column_sum(cross_grad_values), column_sum(grad_two)]
        )
        grad_totals[4] = grad_totals[4] + outer_sum(hidden_low, cross_grad_query)
        pair_grads = jnp.stack([cross_grad_keys, cross_grad_values])
        grad_totals[5] = grad_totals[5] + jnp.einsum(
            "td,cte->cde", remote, pair_grads, preferred_element_type=jnp.float32
        )
        grad_remote[micro_step] = (
            jnp.einsum("cte,cde->td", pair_grads, pair_cross, preferred_element_type=jnp.float32)
            .astype(jnp.bfloat16)
            .reshape(row_count, slot_count, model_width)
        )
        grad_hidden_one = sum_two + dense_back(cross_grad_query, query_cross)
        sum_one, grad_norm_one = norm_backward(grad_hidden_one, normed_one, inverse_one, norm_self)
        grad_one = sum_one.astype(jnp.bfloat16)
        grad_totals[3] = grad_totals[3] + grad_norm_one
        grad_totals[2] = grad_totals[2] + outer_sum(mixture_one, grad_one)
        grad_mixture_one = dense_back(grad_one, out_self).astype(jnp.bfloat16)
        self_grad_query, self_grad_keys, self_grad_values = attend_backward(
            grad_mixture_one,
            query_one,
            keys_one,
            values_one,
            self_allowed,
            logsum_one,
            row_count,
            head_count,
        )
        grad_totals[1] = grad_totals[1] + jnp.stack(
            [column_sum(self_grad_query), column_sum(self_grad_values), column_sum(grad_one)]
        )
        triple_grads = jnp.stack([self_grad_query, self_grad_keys, self_grad_values])
        grad_totals[0] = grad_totals[0] + jnp.einsum(
            "td,cte->cde", source, triple_grads, preferred_element_type=jnp.float32
        )
        grad_inputs[micro_step] = (
            (
                sum_one
                + jnp.einsum(
                    "cte,cde->td", triple_grads, qkv_self, preferred_element_type=jnp.float32
                )
            )
            .astype(jnp.bfloat16)
            .reshape(row_count, slot_count, model_width)
        )
    summed = tuple(
        (
            lax.psum_scatter(grad_totals[0], ("dp", "fsdp"), scatter_dimension=2, tiled=True),
            lax.psum_scatter(grad_totals[1], ("dp", "fsdp"), scatter_dimension=1, tiled=True),
            lax.psum_scatter(grad_totals[2], ("dp", "fsdp"), scatter_dimension=1, tiled=True),
            lax.psum_scatter(grad_totals[3], ("dp", "fsdp"), scatter_dimension=1, tiled=True),
            lax.psum_scatter(grad_totals[4], ("dp", "fsdp"), scatter_dimension=1, tiled=True),
            lax.psum_scatter(grad_totals[5], ("dp", "fsdp"), scatter_dimension=2, tiled=True),
            lax.psum_scatter(grad_totals[6], ("dp", "fsdp"), scatter_dimension=1, tiled=True),
            lax.psum_scatter(grad_totals[7], ("dp", "fsdp"), scatter_dimension=1, tiled=True),
            lax.psum_scatter(grad_totals[8], ("dp", "fsdp"), scatter_dimension=1, tiled=True),
            lax.psum_scatter(grad_totals[9], ("dp", "fsdp"), scatter_dimension=1, tiled=True),
            lax.psum_scatter(grad_totals[10], ("dp", "fsdp"), scatter_dimension=0, tiled=True),
            lax.psum_scatter(grad_totals[11], ("dp", "fsdp"), scatter_dimension=1, tiled=True),
            lax.psum_scatter(grad_totals[12], ("dp", "fsdp"), scatter_dimension=0, tiled=True),
            lax.psum_scatter(grad_totals[13], ("dp", "fsdp"), scatter_dimension=1, tiled=True),
        )
    )
    return (
        jnp.concatenate(outputs, axis=0),
        jnp.concatenate(grad_inputs, axis=0),
        jnp.concatenate(grad_remote, axis=0),
        summed[0],
        summed[1],
        summed[2],
        summed[3],
        summed[4],
        summed[5],
        summed[6],
        summed[7],
        summed[8],
        summed[9],
        summed[10],
        summed[11],
        summed[12],
        summed[13],
    )


def solution(mesh):
    return jax.shard_map(
        on_device,
        mesh=mesh,
        in_specs=(
            P(("dp", "fsdp"), None, None),
            P(("dp", "fsdp"), None, None),
            P(("dp", "fsdp"), None, None),
            P(("dp", "fsdp"), None),
            P(("dp", "fsdp"), None),
            P(None, None, ("dp", "fsdp")),
            P(None, ("dp", "fsdp")),
            P(None, ("dp", "fsdp")),
            P(None, ("dp", "fsdp")),
            P(None, ("dp", "fsdp")),
            P(None, None, ("dp", "fsdp")),
            P(None, ("dp", "fsdp")),
            P(None, ("dp", "fsdp")),
            P(None, ("dp", "fsdp")),
            P(None, ("dp", "fsdp")),
            P(("dp", "fsdp")),
            P(None, ("dp", "fsdp")),
            P(("dp", "fsdp")),
            P(None, ("dp", "fsdp")),
        ),
        out_specs=(
            P(("dp", "fsdp"), None, None),
            P(("dp", "fsdp"), None, None),
            P(("dp", "fsdp"), None, None),
            P(None, None, ("dp", "fsdp")),
            P(None, ("dp", "fsdp")),
            P(None, ("dp", "fsdp")),
            P(None, ("dp", "fsdp")),
            P(None, ("dp", "fsdp")),
            P(None, None, ("dp", "fsdp")),
            P(None, ("dp", "fsdp")),
            P(None, ("dp", "fsdp")),
            P(None, ("dp", "fsdp")),
            P(None, ("dp", "fsdp")),
            P(("dp", "fsdp")),
            P(None, ("dp", "fsdp")),
            P(("dp", "fsdp")),
            P(None, ("dp", "fsdp")),
        ),
        check_vma=False,
    )
```

profile of v0, /device:TPU:0, one launch (start us, length us, event | category | flops | bytes accessed | tf_op | source)
XLA Modules:
  0.0 2392.9 jit_solution(1314293803268356788)
XLA Ops:
  10.1 43.5 %all-gather = bf16[32,16,3]{1,2,0:T(4,128)(2,1)S(1)} all-gather(bf16[1,16,3]{1,2,0:T(4,128)(2,1)} %bitcast.783), channel_id=1, replica_groups=mesh['dp'=4,'fsdp'=8] {'dp','fsdp'}, dimensions={0}, use_global_device_ids=true | all-gather | bytes 3168 | tf_op jit(solution)/shard_map/all_gather | solution.py:145
  54.3 36.9 %all-gather.2 = bf16[32,16,3]{1,2,0:T(4,128)(2,1)S(1)} all-gather(bf16[1,16,3]{1,2,0:T(4,128)(2,1)} %bitcast.784), channel_id=1, replica_groups=mesh['dp'=4,'fsdp'=8] {'dp','fsdp'}, dimensions={0}, use_global_device_ids=true | all-gather | bytes 3168 | tf_op jit(solution)/shard_map/all_gather | solution.py:150
  97.8 39.9 %all_gather.54 = bf16[512,512]{0,1:T(8,128)(2,1)S(1)} all-gather(bf16[512,16]{0,1:T(8,128)(2,1)} %param.26), channel_id=1, replica_groups=mesh['dp'=4,'fsdp'=8] {'dp','fsdp'}, dimensions={1}, use_global_device_ids=true | all-gather | bytes 540672 | tf_op jit(solution)/shard_map/all_gather | solution.py:146
  137.7 36.5 %all-gather.1 = bf16[32,16,2]{1,2,0:T(2,128)(2,1)S(1)} all-gather(bf16[1,16,2]{1,2,0:T(2,128)(2,1)S(1)} %bitcast.785), channel_id=1, replica_groups=mesh['dp'=4,'fsdp'=8] {'dp','fsdp'}, dimensions={0}, use_global_device_ids=true | all-gather | bytes 2112 | tf_op jit(solution)/shard_map/all_gather | solution.py:147
  176.2 42.5 %all_gather.58 = bf16[512,512]{0,1:T(8,128)(2,1)} all-gather(bf16[512,16]{0,1:T(8,128)(2,1)} %param.28), channel_id=1, replica_groups=mesh['dp'=4,'fsdp'=8] {'dp','fsdp'}, dimensions={1}, use_global_device_ids=true | all-gather | bytes 540672 | tf_op jit(solution)/shard_map/all_gather | solution.py:148
  223.3 38.9 %all_gather.59 = bf16[512,512]{0,1:T(8,128)(2,1)S(1)} all-gather(bf16[512,16]{0,1:T(8,128)(2,1)} %param.31), channel_id=1, replica_groups=mesh['dp'=4,'fsdp'=8] {'dp','fsdp'}, dimensions={1}, use_global_device_ids=true | all-gather | bytes 540672 | tf_op jit(solution)/shard_map/all_gather | solution.py:151
  262.2 37.4 %all-gather.3 = bf16[32,16,2]{1,2,0:T(2,128)(2,1)S(1)} all-gather(bf16[1,16,2]{1,2,0:T(2,128)(2,1)} %bitcast.786), channel_id=1, replica_groups=mesh['dp'=4,'fsdp'=8] {'dp','fsdp'}, dimensions={0}, use_global_device_ids=true | all-gather | bytes 2112 | tf_op jit(solution)/shard_map/all_gather | solution.py:152
  306.9 37.3 %all-reduce.5 = (bf16[512]{0:T(512)(128)(2,1)}, bf16[2048]{0:T(1024)(128)(2,1)}) all-reduce(bf16[512]{0:T(512)(128)(2,1)} %dynamic-update-slice.1, bf16[2048]{0:T(1024)(128)(2,1)} %dynamic-update-slice), channel_id=1, replica_groups=mesh['dp'=4,'fsdp'=8] {'dp','fsdp'}, use_global_device_ids=true, to_apply=%add.1 | all-reduce | flops 2560 | bytes 10240
  346.7 40.9 %all-gather.4 = bf16[32,16,2]{1,2,0:T(2,128)(2,1)S(1)} all-gather(bf16[1,16,2]{1,2,0:T(2,128)(2,1)} %bitcast.787), channel_id=1, replica_groups=mesh['dp'=4,'fsdp'=8] {'dp','fsdp'}, dimensions={0}, use_global_device_ids=true | all-gather | bytes 2112 | tf_op jit(solution)/shard_map/all_gather | solution.py:159
  446.2 3.7 fusion.100
  473.8 4.1 fusion.98
  502.3 3.6 fusion.96
  530.4 3.7 fusion.102
  559.7 5.3 fusion.284
  565.0 5.6 fusion.325
  594.4 4.5 convert_reduce_fusion
  598.8 4.4 convert_reduce_fusion.1
  607.8 4.5 convert_reduce_fusion.3
  612.2 4.6 convert_reduce_fusion.2
  618.9 4.2 convert_reduce_fusion.12
  634.2 5.0 convert_reduce_fusion.22
  649.3 5.0 convert_reduce_fusion.19
  664.0 5.0 convert_reduce_fusion.13
  669.0 3.5 multiply_reduce_fusion.7
  678.1 4.9 convert_reduce_fusion.16
  683.0 3.6 multiply_reduce_fusion.5
  718.6 5.0 convert_reduce_fusion.25
  723.7 4.1 multiply_reduce_fusion.6
  738.2 5.0 convert_reduce_fusion.28
  743.2 4.0 multiply_reduce_fusion.4
  753.3 5.0 convert_reduce_fusion.31
  758.3 4.1 multiply_reduce_fusion.2
  767.8 4.8 convert_reduce_fusion.34
  772.7 4.0 multiply_reduce_fusion
  954.9 4.3 fusion.237
  964.3 3.9 add_add_fusion
  977.3 4.6 add_add_fusion.1
  982.6 37.1 %all-reduce.4 = (f32[2048]{0:T(1024)S(1)}, f32[512]{0:T(512)S(1)}) all-reduce(f32[2048]{0:T(1024)S(1)} %add_add_fusion.2, f32[512]{0:T(512)S(1)} %add_add_fusion.3), channel_id=12, replica_groups=mesh['dp'=4,'fsdp'=8] {'dp','fsdp'}, use_global_device_ids=true, to_apply=%region_130.131.clone | all-reduce | flops 2560 | bytes 20480
  1040.3 130.3 %reduce-scatter.39.cloned.1.call-done = f32[16,2]{1,0:T(8,128)} async-done(((f32[512,2]{1,0:T(8,128)}), f32[16,2]{1,0:T(8,128)}) %reduce-scatter.39.cloned.1.call-update) | async-done | bytes 144
  1171.9 130.3 %reduce-scatter.41.cloned.1.call-done = f32[16,3]{1,0:T(8,128)} async-done(((f32[512,3]{1,0:T(8,128)}), f32[16,3]{1,0:T(8,128)}) %reduce-scatter.41.cloned.1.call-update) | async-done | bytes 208
  1303.6 130.2 %reduce-scatter.37.cloned.1.call-done = f32[16,3]{1,0:T(8,128)} async-done(((f32[512,3]{1,0:T(8,128)}), f32[16,3]{1,0:T(8,128)}) %reduce-scatter.37.cloned.1.call-update) | async-done | bytes 208
  1435.2 132.1 %reduce-scatter.31.cloned.1.call-done = f32[512,16]{0,1:T(8,128)} async-done(((f32[512,512]{0,1:T(8,128)}), f32[512,16]{0,1:T(8,128)}) %reduce-scatter.31.cloned.1.call-update) | async-done | bytes 32784 | tf_op jit(solution)/shard_map/reduce_scatter | solution.py:393
  1567.3 133.6 %reduce-scatter.27.cloned.1.call-done = f32[512,16]{0,1:T(8,128)} async-done(((f32[512,512]{0,1:T(8,128)}), f32[512,16]{0,1:T(8,128)}) %reduce-scatter.27.cloned.1.call-update) | async-done | bytes 32784 | tf_op jit(solution)/shard_map/reduce_scatter | solution.py:390
  1700.9 133.5 %reduce-scatter.25.cloned.1.call-done = f32[512,16]{0,1:T(8,128)} async-done(((f32[512,512]{0,1:T(8,128)}), f32[512,16]{0,1:T(8,128)}) %reduce-scatter.25.cloned.1.call-update) | async-done | bytes 32784 | tf_op jit(solution)/shard_map/reduce_scatter | solution.py:388
  1834.4 135.5 %reduce-scatter.29.cloned.1.call-done = f32[2,512,16]{1,2,0:T(8,128)} async-done(((f32[2,512,512]{1,2,0:T(8,128)}), f32[2,512,16]{1,2,0:T(8,128)}) %reduce-scatter.29.cloned.1.call-update) | async-done | bytes 65552 | tf_op jit(solution)/shard_map/reduce_scatter | solution.py:391
  1969.9 137.2 %reduce-scatter.23.cloned.1.call-done = f32[3,512,16]{1,2,0:T(8,128)} async-done(((f32[3,512,512]{1,2,0:T(8,128)}), f32[3,512,16]{1,2,0:T(8,128)}) %reduce-scatter.23.cloned.1.call-update) | async-done | bytes 98320 | tf_op jit(solution)/shard_map/reduce_scatter | solution.py:386
  2107.1 139.5 %reduce-scatter.35.cloned.1.call-done = f32[2048,16]{0,1:T(8,128)} async-done(((f32[2048,512]{0,1:T(8,128)}), f32[2048,16]{0,1:T(8,128)}) %reduce-scatter.35.cloned.1.call-update) | async-done | bytes 131088 | tf_op jit(solution)/shard_map/reduce_scatter | solution.py:397
  2246.6 139.6 %reduce-scatter.33.cloned.1.call-done = f32[512,64]{0,1:T(8,128)} async-done(((f32[512,2048]{0,1:T(8,128)}), f32[512,64]{0,1:T(8,128)}) %reduce-scatter.33.cloned.1.call-update) | async-done | bytes 131088 | tf_op jit(solution)/shard_map/reduce_scatter | solution.py:395
  (1248 shorter events, 517.4 us)
Async XLA Ops:
  7.2 88.3 %copy-start.371 = (s32[8,24]{1,0:T(8,128)S(1)}, s32[8,24]{1,0:T(8,128)}, u32[]{:S(2)}) copy-start(s32[8,24]{1,0:T(8,128)} %param.22) | copy-start | bytes 2308
  7.2 88.4 %copy-start.372 = (s32[8,24]{1,0:T(8,128)S(1)}, s32[8,24]{1,0:T(8,128)}, u32[]{:S(2)}) copy-start(s32[8,24]{1,0:T(8,128)} %param.23) | copy-start | bytes 2308
  7.2 130.5 %copy-start.390 = (bf16[2,16]{1,0:T(2,128)(2,1)S(1)}, bf16[2,16]{1,0:T(2,128)(2,1)}, u32[]{:S(2)}) copy-start(bf16[2,16]{1,0:T(2,128)(2,1)} %param.27) | copy-start | bytes 196
  7.2 387.5 %all-gather.12.cloned.1.call-start = ((), (), s32[]{:S(2)}) async-start(), calls=%async_computation.13 | async-start | bytes 1081344 | tf_op jit(solution)/shard_map/all_gather | solution.py:149
  8.0 412.9 %all-gather.10.cloned.1.call-start = ((), (), s32[]{:S(2)}) async-start(), calls=%async_computation.12 | async-start | bytes 1622016 | tf_op jit(solution)/shard_map/all_gather | solution.py:144
  8.7 551.0 %all-gather.14.cloned.1.call-start = ((), (), s32[]{:S(2)}) async-start(), calls=%async_computation.14 | async-start | bytes 2162688 | tf_op jit(solution)/shard_map/all_gather | solution.py:155
  9.4 555.5 %all-gather.16.cloned.1.call-start = ((), (), s32[]{:S(2)}) async-start(), calls=%async_computation.15 | async-start | bytes 2162688 | tf_op jit(solution)/shard_map/all_gather | solution.py:157
  10.0 1026.6 %reduce-scatter.45.cloned.1.call-start = ((), (), s32[]{:S(2)}) async-start(), calls=%async_computation.27 | async-start | bytes 270336
  96.8 294.1 %copy-start.44 = (bf16[8,256,512]{2,1,0:T(8,128)(2,1)S(1)}, bf16[8,256,512]{2,1,0:T(8,128)(2,1)}, u32[]{:S(2)}) copy-start(bf16[8,256,512]{2,1,0:T(8,128)(2,1)} %param.21) | copy-start | bytes 6291460
  97.6 348.6 %copy-start.174 = (pred[2,256,256]{1,2,0:T(8,128)(4,1)}, pred[2,256,256]{1,2,0:T(8,128)(4,1)S(1)}, u32[]{:S(2)}) copy-start(pred[2,256,256]{1,2,0:T(8,128)(4,1)S(1)} %get-tuple-element.131) | copy-start | bytes 393220
  97.6 376.2 %copy-start.176 = (pred[2,256,256]{1,2,0:T(8,128)(4,1)}, pred[2,256,256]{1,2,0:T(8,128)(4,1)S(1)}, u32[]{:S(2)}) copy-start(pred[2,256,256]{1,2,0:T(8,128)(4,1)S(1)} %get-tuple-element.132) | copy-start | bytes 393220
  97.6 432.7 %copy-start.172 = (pred[2,256,256]{1,2,0:T(8,128)(4,1)}, pred[2,256,256]{1,2,0:T(8,128)(4,1)S(1)}, u32[]{:S(2)}) copy-start(pred[2,256,256]{1,2,0:T(8,128)(4,1)S(1)} %get-tuple-element.130) | copy-start | bytes 393220
  97.7 425.1 %copy-start.245 = (f32[8,64]{1,0:T(8,128)}, f32[8,64]{1,0:T(8,128)S(1)}, u32[]{:S(2)}) copy-start(f32[8,64]{1,0:T(8,128)S(1)} %reshape.1001) | copy-start | bytes 6148
  97.8 432.6 %copy-start.247 = (f32[8,64]{1,0:T(8,128)}, f32[8,64]{1,0:T(8,128)S(1)}, u32[]{:S(2)}) copy-start(f32[8,64]{1,0:T(8,128)S(1)} %reshape.1000) | copy-start | bytes 6148
  137.7 397.1 %copy-start.26 = (bf16[512,512]{0,1:T(8,128)(2,1)}, bf16[512,512]{0,1:T(8,128)(2,1)S(1)}, u32[]{:S(2)}) copy-start(bf16[512,512]{0,1:T(8,128)(2,1)S(1)} %all_gather.54) | copy-start | bytes 1572868
  554.6 68.5 %copy-start.276 = (f32[512]{0:T(512)}, f32[512]{0:T(512)S(1)}, u32[]{:S(2)}) copy-start(f32[512]{0:T(512)S(1)} %broadcast_multiply_fusion.24) | copy-start | bytes 6148
  555.6 67.5 %copy-start.278 = (f32[512]{0:T(512)}, f32[512]{0:T(512)S(1)}, u32[]{:S(2)}) copy-start(f32[512]{0:T(512)S(1)} %broadcast_multiply_fusion.27) | copy-start | bytes 6148
  556.6 61.5 %copy-start.315 = (f32[512]{0:T(512)}, f32[512]{0:T(512)S(1)}, u32[]{:S(2)}) copy-start(f32[512]{0:T(512)S(1)} %broadcast_multiply_fusion.30) | copy-start | bytes 6148
  558.3 64.8 %copy-start.280 = (f32[512]{0:T(512)}, f32[512]{0:T(512)S(1)}, u32[]{:S(2)}) copy-start(f32[512]{0:T(512)S(1)} %broadcast_multiply_fusion.21) | copy-start | bytes 6148
  559.6 63.5 %copy-start.309 = (f32[512]{0:T(512)}, f32[512]{0:T(512)S(1)}, u32[]{:S(2)}) copy-start(f32[512]{0:T(512)S(1)} %add_rsqrt_fusion.4) | copy-start | bytes 6148
  559.6 63.5 %copy-start.307 = (f32[512]{0:T(512)}, f32[512]{0:T(512)S(1)}, u32[]{:S(2)}) copy-start(f32[512]{0:T(512)S(1)} %add_rsqrt_fusion.7) | copy-start | bytes 6148
  559.6 58.5 %copy-start.326 = (f32[512]{0:T(512)}, f32[512]{0:T(512)S(1)}, u32[]{:S(2)}) copy-start(f32[512]{0:T(512)S(1)} %add_rsqrt_fusion.10) | copy-start | bytes 6148
  559.6 63.5 %copy-start.305 = (f32[512]{0:T(512)}, f32[512]{0:T(512)S(1)}, u32[]{:S(2)}) copy-start(f32[512]{0:T(512)S(1)} %add_rsqrt_fusion.1) | copy-start | bytes 6148
  573.1 25.8 %copy-start.394 = (f32[512,2048]{1,0:T(8,128)}, f32[512,2048]{1,0:T(8,128)S(1)}, u32[]{:S(2)}) copy-start(f32[512,2048]{1,0:T(8,128)S(1)} %fusion.290) | copy-start | bytes 12582916
  578.1 16.2 copy-start.148
  583.2 24.6 %copy-start.396 = (f32[512,2048]{1,0:T(8,128)}, f32[512,2048]{1,0:T(8,128)S(1)}, u32[]{:S(2)}) copy-start(f32[512,2048]{1,0:T(8,128)S(1)} %fusion.280) | copy-start | bytes 12582916
  594.4 22.5 copy-start.239
  594.4 23.8 copy-start.237
  777.7 261.2 %reduce-scatter.43.cloned.1.call-start = ((), (), s32[]{:S(2)}) async-start(), calls=%async_computation.26 | async-start | bytes 270336
  803.3 367.2 %reduce-scatter.39.cloned.1.call-start = ((), (), s32[]{:S(2)}) async-start(), calls=%async_computation.24 | async-start | bytes 270336
  805.7 496.6 %reduce-scatter.41.cloned.1.call-start = ((), (), s32[]{:S(2)}) async-start(), calls=%async_computation.25 | async-start | bytes 270336
  807.3 626.5 %reduce-scatter.37.cloned.1.call-start = ((), (), s32[]{:S(2)}) async-start(), calls=%async_computation.23 | async-start | bytes 270336
  808.3 759.0 %reduce-scatter.31.cloned.1.call-start = ((), (), s32[]{:S(2)}) async-start(), calls=%async_computation.20 | async-start | bytes 1081344 | tf_op jit(solution)/shard_map/reduce_scatter | solution.py:393
  811.6 889.3 %reduce-scatter.27.cloned.1.call-start = ((), (), s32[]{:S(2)}) async-start(), calls=%async_computation.18 | async-start | bytes 1081344 | tf_op jit(solution)/shard_map/reduce_scatter | solution.py:390
  817.6 11.0 copy-start.273
  817.6 11.0 copy-start.314
  832.3 11.9 copy-start.81
  832.3 1002.1 %reduce-scatter.25.cloned.1.call-start = ((), (), s32[]{:S(2)}) async-start(), calls=%async_computation.17 | async-start | bytes 1081344 | tf_op jit(solution)/shard_map/reduce_scatter | solution.py:388
  835.0 10.8 copy-start.31
  850.3 1119.6 %reduce-scatter.29.cloned.1.call-start = ((), (), s32[]{:S(2)}) async-start(), calls=%async_computation.19 | async-start | bytes 2162688 | tf_op jit(solution)/shard_map/reduce_scatter | solution.py:391
  875.9 1231.2 %reduce-scatter.23.cloned.1.call-start = ((), (), s32[]{:S(2)}) async-start(), calls=%async_computation.16 | async-start | bytes 3244032 | tf_op jit(solution)/shard_map/reduce_scatter | solution.py:386
  884.3 13.0 copy-start.41
  902.6 12.8 copy-start.39
  920.7 13.2 copy-start.37
  954.9 1291.7 %reduce-scatter.35.cloned.1.call-start = ((), (), s32[]{:S(2)}) async-start(), calls=%async_computation.22 | async-start | bytes 4325376 | tf_op jit(solution)/shard_map/reduce_scatter | solution.py:397
  968.3 1417.9 %reduce-scatter.33.cloned.1.call-start = ((), (), s32[]{:S(2)}) async-start(), calls=%async_computation.21 | async-start | bytes 4325376 | tf_op jit(solution)/shard_map/reduce_scatter | solution.py:395
  981.9 39.0 %copy-start.47 = (bf16[2,512,512]{1,2,0:T(8,128)(2,1)S(1)}, bf16[2,512,512]{1,2,0:T(8,128)(2,1)}, u32[]{:S(2)}) copy-start(bf16[2,512,512]{1,2,0:T(8,128)(2,1)} %all-gather.12.cloned.1.call-done) | copy-start | bytes 3145732
  981.9 40.9 %copy-start.194 = (bf16[2,512,512]{2,1,0:T(8,128)(2,1)S(1)}, bf16[2,512,512]{2,1,0:T(8,128)(2,1)}, u32[]{:S(2)}) copy-start(bf16[2,512,512]{2,1,0:T(8,128)(2,1)} %constant_dynamic-update-slice_fusion.14) | copy-start | bytes 3145732
  (367 other events, 1390.8 us)
Sparse Core Ops, SparseCore 0:
  11.0 56.3 all-gather.11
  70.2 54.0 all-gather.9
  127.2 55.2 all-gather.13
  185.2 55.6 all-gather.15
  777.9 129.5 reduce-scatter.44
  909.6 129.3 reduce-scatter.42
  1041.2 129.3 reduce-scatter.38
  1172.9 129.3 reduce-scatter.40
  1304.5 129.3 reduce-scatter.36
  1436.6 130.6 reduce-scatter.30
  1570.2 130.7 reduce-scatter.26
  1703.7 130.6 reduce-scatter.24
  1837.2 132.5 reduce-scatter.28
  1972.7 134.3 reduce-scatter.22
  2109.8 136.7 reduce-scatter.34
  2249.3 136.8 reduce-scatter.32
where the time goes:
time: 2400 us; the launch traced here: 2390 us
  waiting for transfers between devices  1350 us (56%)
  blocking collectives  391 us (16%)
  local copies, waits for them, and re-layouts  292 us (12%)
  matrix products  286 us (12%)
  other arithmetic  57.6 us (2%)
    unnamed x21, waiting for transfers between devices  395 us
    reduce_scatter x1, waiting for transfers between devices, on_device(): lax.psum_scatter(grad_totals[9], ('dp', 'fsdp'), scatter_dimension=1, til...  140 us
    reduce_scatter x1, waiting for transfers between devices, on_device(): lax.psum_scatter(grad_totals[11], ('dp', 'fsdp'), scatter_dimension=1, ti...  139 us
    reduce_scatter x1, waiting for transfers between devices, on_device(): lax.psum_scatter(grad_totals[0], ('dp', 'fsdp'), scatter_dimension=2, til...  137 us
    reduce_scatter x1, waiting for transfers between devices, on_device(): lax.psum_scatter(grad_totals[5], ('dp', 'fsdp'), scatter_dimension=2, til...  135 us
    reduce_scatter x1, waiting for transfers between devices, on_device(): lax.psum_scatter(grad_totals[4], ('dp', 'fsdp'), scatter_dimension=1, til...  134 us
    reduce_scatter x1, waiting for transfers between devices, on_device(): lax.psum_scatter(grad_totals[2], ('dp', 'fsdp'), scatter_dimension=1, til...  133 us
    reduce_scatter x1, waiting for transfers between devices, on_device(): lax.psum_scatter(grad_totals[7], ('dp', 'fsdp'), scatter_dimension=1, til...  132 us
  transfers between devices with their start and end apart: 16, of which 11 were waited for; matrix products, arithmetic and copies ran while one was open for 16% of the time, Pallas kernels for 0%

commit v1 on v0

v1 whole, which is shorter than its diff:
```python
import functools

import jax
import jax.numpy as jnp
from jax import lax
from jax.experimental import pallas as pl
from jax.experimental.pallas import tpu as pltpu
from jax.sharding import PartitionSpec as P

F32 = jnp.float32
BF16 = jnp.bfloat16
EPS = 1e-05
MASKED = -1e30
HEADS = 8
HEAD_DIM = 64
PAIR = 128
QUAD = 256
GELU_A = 0.7978845608028654
GELU_B = 0.044715


def mm(left, right, left_dim, right_dim):
    return lax.dot_general(
        left, right, (((left_dim,), (right_dim,)), ((), ())), preferred_element_type=F32
    )


def mm_nt(left, right):
    return mm(left, right, 1, 1)


def mm_nn(left, right):
    return mm(left, right, 1, 0)


def mm_tn(left, right):
    return mm(left, right, 0, 0)


def norm_stats(summed):
    centred = summed - jnp.mean(summed, axis=-1, keepdims=True)
    inverse = lax.rsqrt(jnp.mean(centred * centred, axis=-1, keepdims=True) + EPS)
    return centred * inverse, inverse


def norm_back(upstream, normed, inverse, gain):
    scaled = upstream * gain
    mean_scaled = jnp.mean(scaled, axis=-1, keepdims=True)
    mean_product = jnp.mean(scaled * normed, axis=-1, keepdims=True)
    return (scaled - mean_scaled - normed * mean_product) * inverse


def column_sum(values):
    return jnp.sum(values.astype(F32), axis=0, keepdims=True)


def lane_band(width, head):
    lane = lax.broadcasted_iota(jnp.int32, (1, width), 1)
    return (lane >= head * HEAD_DIM) & (lane < (head + 1) * HEAD_DIM)


def keep_head(values, head):
    return jnp.where(lane_band(values.shape[1], head), values, jnp.zeros_like(values))


def mask_bias(key_ids, query_ids, causal):
    slots = key_ids.shape[1]
    down = jnp.transpose(jnp.broadcast_to(key_ids, (slots, slots)))
    allowed = down == query_ids
    if causal:
        key_at = lax.broadcasted_iota(jnp.int32, (slots, slots), 0)
        query_at = lax.broadcasted_iota(jnp.int32, (slots, slots), 1)
        allowed = allowed & (key_at <= query_at)
    return jnp.where(allowed, 0.0, MASKED).astype(F32)


def attend_rows(query_ref, keys_ref, values_ref, bias_ref, shares_ref, mixture_ref, row, at):
    for quad in range(HEADS * HEAD_DIM // QUAD):
        lanes = slice(quad * QUAD, (quad + 1) * QUAD)
        values_quad = values_ref[at, lanes]
        parts, wide = [], []
        for inner in range(QUAD // HEAD_DIM):
            head = quad * (QUAD // HEAD_DIM) + inner
            first = head * HEAD_DIM // PAIR * PAIR
            pair = slice(first, first + PAIR)
            keys_head = keep_head(keys_ref[at, pair], head - first // HEAD_DIM)
            scores = mm_nt(keys_head, query_ref[at, pair]) + bias_ref[...]
            top = jnp.max(scores, axis=0, keepdims=True)
            raised = jnp.exp(scores - top)
            total = jnp.sum(raised, axis=0, keepdims=True)
            shares = (raised * (1.0 / total)).astype(BF16)
            shares_ref[row * HEADS + head] = shares
            parts.append(shares)
            wide.append(keep_head(values_quad, inner))
        mixture = mm_tn(jnp.concatenate(parts, 0), jnp.concatenate(wide, 0))
        mixture_ref[at, lanes] = mixture.astype(BF16)


def attend_rows_back(
    upstream_ref, query_ref, keys_ref, values_ref, shares_ref, gq_ref, gk_ref, gv_ref, row, at
):
    for quad in range(HEADS * HEAD_DIM // QUAD):
        lanes = slice(quad * QUAD, (quad + 1) * QUAD)
        query_quad = query_ref[at, lanes]
        keys_quad = keys_ref[at, lanes]
        up_quad = upstream_ref[at, lanes]
        grad_query = grad_keys = grad_values = None
        for inner in range(QUAD // HEAD_DIM):
            head = quad * (QUAD // HEAD_DIM) + inner
            first = head * HEAD_DIM // PAIR * PAIR
            pair = slice(first, first + PAIR)
            values_head = keep_head(values_ref[at, pair], head - first // HEAD_DIM)
            shares = shares_ref[row * HEADS + head]
            grad_shares = mm_nt(values_head, upstream_ref[at, pair])
            wide = shares.astype(F32)
            product = wide * grad_shares
            centre = jnp.sum(product, axis=0, keepdims=True)
            grad_scores = (product - wide * centre).astype(BF16)
            one = mm_nn(grad_scores, keep_head(query_quad, inner))
            two = mm_nn(shares, keep_head(up_quad, inner))
            three = mm_tn(grad_scores, keep_head(keys_quad, inner))
            grad_keys = one if grad_keys is None else grad_keys + one
            grad_values = two if grad_values is None else grad_values + two
            grad_query = three if grad_query is None else grad_query + three
        gq_ref[at, lanes] = (grad_query * HEAD_DIM**-0.5).astype(BF16)
        gk_ref[at, lanes] = grad_keys.astype(BF16)
        gv_ref[at, lanes] = grad_values.astype(BF16)


STEP_ROWS = 2

SELF_BQ, SELF_BV, SELF_BO, SELF_G, SELF_S = 0, 1, 2, 3, 4
CROSS_BQ, CROSS_BV, CROSS_BO, CROSS_G, CROSS_S = 5, 6, 7, 8, 9
FFN_BO, FFN_G, FFN_S, FFN_BI = 10, 11, 12, 13
TABLE = 24


def vrow(table_ref, index):
    return table_ref[index : index + 1, :]


def add_row(ref, index, values):
    ref[index : index + 1, :] += values


def self_forward_kernel(
    source_ref, ids_ref, weight_ref, table_ref,
    query_ref, keys_ref, values_ref, shares_ref, mixture_ref, summed_ref, bias_ref,
):
    slots = ids_ref.shape[2]
    source = source_ref[...]
    query = mm_nt(source, weight_ref[0]) + vrow(table_ref, SELF_BQ)
    query_ref[...] = (query * HEAD_DIM**-0.5).astype(BF16)
    keys_ref[...] = mm_nt(source, weight_ref[1]).astype(BF16)
    values_ref[...] = (mm_nt(source, weight_ref[2]) + vrow(table_ref, SELF_BV)).astype(BF16)

    def one_row(row, carry):
        at = pl.ds(pl.multiple_of(row * slots, slots), slots)
        ids = ids_ref[row]
        bias_ref[...] = mask_bias(ids[0:1], ids[0:1], True)
        attend_rows(query_ref, keys_ref, values_ref, bias_ref, shares_ref, mixture_ref, row, at)
        return carry

    lax.fori_loop(0, STEP_ROWS, one_row, 0)
    summed_ref[...] = (
        source.astype(F32) + mm_nt(mixture_ref[...], weight_ref[3]) + vrow(table_ref, SELF_BO)
    )


def middle_kernel(
    summed_one_ref, remote_ref, upstream_ref, ids_ref, weight_ref, win_ref, wout_ref, table_ref,
    result_ref, grad_remote_ref, sum_one_ref, dweight_ref, dwin_ref, dwout_ref, dtable_ref,
    low_ref, query_ref, keys_ref, values_ref, shares_ref, mixture_ref, bias_ref,
    normed_one_ref, normed_two_ref, hidden_ref, active_ref, slope_ref, accum_ref,
    gq_ref, gk_ref, gv_ref, low_two_ref, grad_low_ref, acc_ref, accin_ref, accout_ref, acct_ref,
):
    step = pl.program_id(0)
    slots = ids_ref.shape[2]
    chunks = win_ref.shape[0] // 512

    @pl.when(step == 0)
    def _():
        acc_ref[...] = jnp.zeros_like(acc_ref)
        accin_ref[...] = jnp.zeros_like(accin_ref)
        accout_ref[...] = jnp.zeros_like(accout_ref)
        acct_ref[...] = jnp.zeros_like(acct_ref)

    normed_one, inverse_one = norm_stats(summed_one_ref[...])
    normed_one_ref[...] = normed_one
    hidden_one = normed_one * vrow(table_ref, SELF_G) + vrow(table_ref, SELF_S)
    low_ref[...] = hidden_one.astype(BF16)
    query = mm_nt(low_ref[...], weight_ref[0]) + vrow(table_ref, CROSS_BQ)
    query_ref[...] = (query * HEAD_DIM**-0.5).astype(BF16)
    remote = remote_ref[...]
    keys_ref[...] = mm_nt(remote, weight_ref[1]).astype(BF16)
    values_ref[...] = (mm_nt(remote, weight_ref[2]) + vrow(table_ref, CROSS_BV)).astype(BF16)

    def one_row(row, carry):
        at = pl.ds(pl.multiple_of(row * slots, slots), slots)
        ids = ids_ref[row]
        bias_ref[...] = mask_bias(ids[1:2], ids[0:1], False)
        attend_rows(query_ref, keys_ref, values_ref, bias_ref, shares_ref, mixture_ref, row, at)
        return carry

    lax.fori_loop(0, STEP_ROWS, one_row, 0)
    hidden_one = normed_one_ref[...] * vrow(table_ref, SELF_G) + vrow(table_ref, SELF_S)
    summed_two = hidden_one + mm_nt(mixture_ref[...], weight_ref[3]) + vrow(table_ref, CROSS_BO)
    normed_two, inverse_two = norm_stats(summed_two)
    normed_two_ref[...] = normed_two
    hidden_two = normed_two * vrow(table_ref, CROSS_G) + vrow(table_ref, CROSS_S)
    hidden_ref[...] = hidden_two
    low_two_ref[...] = hidden_two.astype(BF16)

    accum_ref[...] = jnp.zeros_like(accum_ref)

    def ffn_chunk(chunk, carry):
        units = pl.ds(pl.multiple_of(chunk * 512, 512), 512)
        expanded = mm_nt(low_two_ref[...], win_ref[units, :]) + table_ref[pl.ds(FFN_BI + chunk, 1), :]
        square = expanded * expanded
        inner = expanded * (GELU_A + (GELU_A * GELU_B) * square)
        bent = jnp.tanh(inner)
        half = 0.5 * bent + 0.5
        active_ref[:, units] = (expanded * half).astype(BF16)
        slope = half + (0.5 * expanded) * (1.0 - bent * bent) * (
            GELU_A + (3.0 * GELU_A * GELU_B) * square
        )
        slope_ref[:, units] = slope.astype(BF16)
        accum_ref[...] += mm_nt(active_ref[:, units], wout_ref[:, units])
        return carry

    lax.fori_loop(0, chunks, ffn_chunk, 0)
    normed_three, inverse_three = norm_stats(
        hidden_ref[...] + accum_ref[...] + vrow(table_ref, FFN_BO)
    )
    result = normed_three * vrow(table_ref, FFN_G) + vrow(table_ref, FFN_S)
    result_ref[...] = result.astype(BF16)

    upstream = upstream_ref[...].astype(F32)
    add_row(acct_ref, FFN_G, column_sum(upstream * normed_three))
    add_row(acct_ref, FFN_S, column_sum(upstream))
    sum_three = norm_back(upstream, normed_three, inverse_three, vrow(table_ref, FFN_G))
    grad_low_ref[...] = sum_three.astype(BF16)
    add_row(acct_ref, FFN_BO, column_sum(grad_low_ref[...]))
    accum_ref[...] = sum_three

    def ffn_chunk_back(chunk, carry):
        units = pl.ds(pl.multiple_of(chunk * 512, 512), 512)
        grad_three = grad_low_ref[...]
        accout_ref[:, units] += mm_tn(grad_three, active_ref[:, units])
        grad_active = mm_nn(grad_three, wout_ref[:, units])
        grad_expanded = (grad_active * slope_ref[:, units].astype(F32)).astype(BF16)
        acct_ref[pl.ds(FFN_BI + chunk, 1), :] += column_sum(grad_expanded)
        accin_ref[units, :] += mm_tn(grad_expanded, low_two_ref[...])
        accum_ref[...] += mm_nn(grad_expanded, win_ref[units, :])
        return carry

    lax.fori_loop(0, chunks, ffn_chunk_back, 0)

    grad_hidden_two = accum_ref[...]
    normed_two = normed_two_ref[...]
    add_row(acct_ref, CROSS_G, column_sum(grad_hidden_two * normed_two))
    add_row(acct_ref, CROSS_S, column_sum(grad_hidden_two))
    sum_two = norm_back(grad_hidden_two, normed_two, inverse_two, vrow(table_ref, CROSS_G))
    accum_ref[...] = sum_two
    grad_low_ref[...] = sum_two.astype(BF16)
    grad_two = grad_low_ref[...]
    add_row(acct_ref, CROSS_BO, column_sum(grad_two))
    acc_ref[3] += mm_tn(grad_two, mixture_ref[...])
    mixture_ref[...] = mm_nn(grad_two, weight_ref[3]).astype(BF16)

    def one_row_back(row, carry):
        at = pl.ds(pl.multiple_of(row * slots, slots), slots)
        attend_rows_back(
            mixture_ref, query_ref, keys_ref, values_ref, shares_ref, gq_ref, gk_ref, gv_ref, row, at
        )
        return carry

    lax.fori_loop(0, STEP_ROWS, one_row_back, 0)
    grad_query, grad_keys, grad_values = gq_ref[...], gk_ref[...], gv_ref[...]
    add_row(acct_ref, CROSS_BQ, column_sum(grad_query))
    add_row(acct_ref, CROSS_BV, column_sum(grad_values))
    acc_ref[0] += mm_tn(grad_query, low_ref[...])
    acc_ref[1] += mm_tn(grad_keys, remote_ref[...])
    acc_ref[2] += mm_tn(grad_values, remote_ref[...])
    grad_remote_ref[...] = (
        mm_nn(grad_keys, weight_ref[1]) + mm_nn(grad_values, weight_ref[2])
    ).astype(BF16)

    grad_hidden_one = accum_ref[...] + mm_nn(grad_query, weight_ref[0])
    normed_one = normed_one_ref[...]
    add_row(acct_ref, SELF_G, column_sum(grad_hidden_one * normed_one))
    add_row(acct_ref, SELF_S, column_sum(grad_hidden_one))
    sum_one_ref[...] = norm_back(grad_hidden_one, normed_one, inverse_one, vrow(table_ref, SELF_G))

    @pl.when(step == pl.num_programs(0) - 1)
    def _():
        dweight_ref[...] = acc_ref[...].astype(BF16)
        dwin_ref[...] = accin_ref[...].astype(BF16)
        dwout_ref[...] = accout_ref[...].astype(BF16)
        dtable_ref[...] = acct_ref[...]


def self_backward_kernel(
    sum_one_ref, source_ref, mixture_ref, query_ref, keys_ref, values_ref, shares_ref, weight_ref,
    grad_source_ref, dweight_ref, dtable_ref,
    up_ref, gq_ref, gk_ref, gv_ref, acc_ref, acct_ref,
):
    step = pl.program_id(0)
    slots = shares_ref.shape[1]

    @pl.when(step == 0)
    def _():
        acc_ref[...] = jnp.zeros_like(acc_ref)
        acct_ref[...] = jnp.zeros_like(acct_ref)

    grad_one = sum_one_ref[...].astype(BF16)
    add_row(acct_ref, SELF_BO, column_sum(grad_one))
    acc_ref[3] += mm_tn(grad_one, mixture_ref[...])
    up_ref[...] = mm_nn(grad_one, weight_ref[3]).astype(BF16)

    def one_row_back(row, carry):
        at = pl.ds(pl.multiple_of(row * slots, slots), slots)
        attend_rows_back(
            up_ref, query_ref, keys_ref, values_ref, shares_ref, gq_ref, gk_ref, gv_ref, row, at
        )
        return carry

    lax.fori_loop(0, STEP_ROWS, one_row_back, 0)
    grad_query, grad_keys, grad_values = gq_ref[...], gk_ref[...], gv_ref[...]
    add_row(acct_ref, SELF_BQ, column_sum(grad_query))
    add_row(acct_ref, SELF_BV, column_sum(grad_values))
    source = source_ref[...]
    acc_ref[0] += mm_tn(grad_query, source)
    acc_ref[1] += mm_tn(grad_keys, source)
    acc_ref[2] += mm_tn(grad_values, source)
    grad_source_ref[...] = (
        sum_one_ref[...]
        + mm_nn(grad_query, weight_ref[0])
        + mm_nn(grad_keys, weight_ref[1])
        + mm_nn(grad_values, weight_ref[2])
    ).astype(BF16)

    @pl.when(step == pl.num_programs(0) - 1)
    def _():
        dweight_ref[...] = acc_ref[...].astype(BF16)
        dtable_ref[...] = acct_ref[...]


def whole(shape):
    return pl.BlockSpec(shape, lambda i: (0,) * len(shape), pipeline_mode=pl.Buffered(1))


def tokens_spec(block, width):
    return pl.BlockSpec((block, width), lambda i: (i, 0))


def params(limit):
    return pltpu.CompilerParams(vmem_limit_bytes=limit, dimension_semantics=("arbitrary",))


def layer(decoder_in, memory, out_grad, ids, weight_self, weight_cross, win, wout, table):
    rows, slots, width = decoder_in.shape
    hidden = win.shape[0]
    tokens = rows * slots
    block = STEP_ROWS * slots
    steps = rows // STEP_ROWS
    shares_block = (STEP_ROWS * HEADS, slots, slots)
    source = decoder_in.reshape(tokens, width)
    shape = jax.ShapeDtypeStruct
    low = shape((tokens, width), BF16)
    full = shape((tokens, width), F32)
    tok = tokens_spec(block, width)
    ids_spec = pl.BlockSpec((STEP_ROWS, 2, slots), lambda i: (i, 0, 0))
    shares_spec = pl.BlockSpec(shares_block, lambda i: (i, 0, 0))
    query, keys, values, shares, mixture, summed = pl.pallas_call(
        self_forward_kernel,
        grid=(steps,),
        in_specs=[tok, ids_spec, whole(weight_self.shape), whole(table.shape)],
        out_specs=[tok, tok, tok, shares_spec, tok, tok],
        out_shape=[low, low, low, shape((rows * HEADS, slots, slots), BF16), low, full],
        scratch_shapes=[pltpu.VMEM((slots, slots), F32)],
        compiler_params=params(56 << 20),
        name="self_forward",
    )(source, ids, weight_self, table)
    vm = pltpu.VMEM
    result, grad_remote, sum_one, dcross, dwin, dwout, dtable = pl.pallas_call(
        middle_kernel,
        grid=(steps,),
        in_specs=[tok, tok, tok, ids_spec, whole(weight_cross.shape), whole(win.shape), whole(wout.shape), whole(table.shape)],
        out_specs=[tok, tok, tok, whole(weight_cross.shape), whole(win.shape), whole(wout.shape), whole(table.shape)],
        out_shape=[low, low, full, shape(weight_cross.shape, BF16), shape(win.shape, BF16), shape(wout.shape, BF16), shape(table.shape, F32)],
        scratch_shapes=[
            vm((block, width), BF16), vm((block, width), BF16), vm((block, width), BF16), vm((block, width), BF16),
            vm(shares_block, BF16), vm((block, width), BF16), vm((slots, slots), F32),
            vm((block, width), F32), vm((block, width), F32), vm((block, width), F32),
            vm((block, hidden), BF16), vm((block, hidden), BF16), vm((block, width), F32),
            vm((block, width), BF16), vm((block, width), BF16), vm((block, width), BF16),
            vm((block, width), BF16), vm((block, width), BF16),
            vm(weight_cross.shape, F32), vm(win.shape, F32), vm(wout.shape, F32), vm(table.shape, F32),
        ],
        compiler_params=params(63 << 20),
        name="middle",
    )(summed, memory.reshape(tokens, width), out_grad.reshape(tokens, width), ids, weight_cross, win, wout, table)
    grad_source, dself, dtable_self = pl.pallas_call(
        self_backward_kernel,
        grid=(steps,),
        in_specs=[tok, tok, tok, tok, tok, tok, shares_spec, whole(weight_self.shape)],
        out_specs=[tok, whole(weight_self.shape), whole(table.shape)],
        out_shape=[low, shape(weight_self.shape, BF16), shape(table.shape, F32)],
        scratch_shapes=[
            vm((block, width), BF16), vm((block, width), BF16), vm((block, width), BF16), vm((block, width), BF16),
            vm(weight_self.shape, F32), vm(table.shape, F32),
        ],
        compiler_params=params(56 << 20),
        name="self_backward",
    )(sum_one, source, mixture, query, keys, values, shares, weight_self)
    as_rows = lambda array: array.reshape(rows, slots, width)
    return as_rows(result), as_rows(grad_source), as_rows(grad_remote), dself, dcross, dwin, dwout, dtable + dtable_self


def segment_ids(lengths, slot_count):
    places = jnp.arange(slot_count, dtype=jnp.int32)
    finish = jnp.cumsum(lengths, axis=-1)
    return jnp.sum((finish[:, None, :] <= places[None, :, None]).astype(jnp.int32), axis=-1)


def turn(array):
    return jnp.swapaxes(array, -1, -2)


AXES = ("dp", "fsdp")


def gather_plain(parts, count):
    (self_qkv, self_bias, self_out, self_norm, cross_q, cross_kv, cross_bias, cross_out, cross_norm,
     ffn_in, ffn_in_bias, ffn_out, ffn_out_bias, ffn_norm) = parts
    cols = self_out.shape[1]
    width = self_out.shape[0]
    chunks = ffn_out.shape[0] // width
    small = jnp.concatenate(
        [self_bias, self_norm, cross_bias, cross_norm, ffn_out_bias[None], ffn_norm,
         ffn_in_bias.reshape(chunks, cols)], axis=0)
    small = jnp.pad(turn(small), ((0, 0), (0, width - small.shape[0])))
    packed = jnp.concatenate([
        turn(self_qkv).reshape(-1, width), turn(self_out), turn(cross_q),
        turn(cross_kv).reshape(-1, width), turn(cross_out), turn(ffn_in),
        turn(ffn_out).reshape(cols, chunks, width).swapaxes(0, 1).reshape(-1, width), small], axis=0)
    whole_set = lax.all_gather(packed, AXES, axis=0, tiled=False)
    square = whole_set[:, : 8 * cols].reshape(count, 8, cols, width).swapaxes(0, 1)
    square = square.reshape(8, width, width)
    low = 8 * cols
    win = whole_set[:, low : low + chunks * cols].reshape(chunks * width, width)
    low += chunks * cols
    wout = whole_set[:, low : low + chunks * cols].reshape(count, chunks, cols, width)
    wout = wout.transpose(0, 2, 1, 3).reshape(width, chunks * width)
    low += chunks * cols
    table = whole_set[:, low:]
    first = table[:, :, :13].transpose(2, 0, 1).reshape(13, width)
    second = table[:, :, 13 : 13 + chunks].transpose(0, 2, 1).reshape(chunks, width)
    table = jnp.concatenate([first, second], axis=0).astype(F32)
    table = jnp.pad(table, ((0, TABLE - table.shape[0]), (0, 0)))
    return square[:4], square[4:], win, wout, table


def scatter_plain(dself, dcross, dwin, dwout, dtable, count):
    width = dself.shape[1]
    cols = width // count
    chunks = dwin.shape[0] // width
    squares = jnp.concatenate([dself, dcross], axis=0).reshape(8, count, cols, width).swapaxes(0, 1)
    first = dtable[:13].reshape(13, count, cols).transpose(1, 2, 0)
    second = dtable[13 : 13 + chunks].reshape(count, chunks, cols).transpose(0, 2, 1)
    small = jnp.concatenate([first, second], axis=2)
    small = jnp.pad(small, ((0, 0), (0, 0), (0, width - small.shape[2]))).astype(BF16)
    packed = jnp.concatenate([
        squares.reshape(count, 8 * cols, width), dwin.reshape(count, chunks * cols, width),
        dwout.reshape(count, cols, chunks, width).swapaxes(1, 2).reshape(count, -1, width), small],
        axis=1)
    mine = lax.psum_scatter(packed, AXES, scatter_dimension=0, tiled=False).astype(F32)
    square = turn(mine[: 8 * cols].reshape(8, cols, width))
    low = 8 * cols
    ffn_in = turn(mine[low : low + chunks * cols])
    low += chunks * cols
    ffn_out = mine[low : low + chunks * cols].reshape(chunks, cols, width).swapaxes(0, 1)
    ffn_out = turn(ffn_out.reshape(cols, chunks * width))
    low += chunks * cols
    small = turn(mine[low:, : 13 + chunks])
    return (square[:3], small[0:3], square[3], small[3:5], square[4], square[5:7], small[5:8], square[7],
            small[8:10], ffn_in, small[13:].reshape(-1), ffn_out, small[10], small[11:13])


def on_device(count, decoder_in, memory, out_grad, tgt_len, src_len, *parts):
    slots = decoder_in.shape[1]
    ids = jnp.stack([segment_ids(tgt_len, slots), segment_ids(src_len, slots)], axis=1).astype(F32)
    weights = gather_plain(parts, count)
    result, grad_source, grad_remote, *grads = layer(decoder_in, memory, out_grad, ids, *weights)
    return (result, grad_source, grad_remote, *scatter_plain(*grads, count))


def solution(mesh):
    count = mesh.shape["dp"] * mesh.shape["fsdp"]
    rows = P(AXES, None, None)
    lens = P(AXES, None)
    cube = P(None, None, AXES)
    flat = P(None, AXES)
    line = P(AXES)
    params_in = (cube, flat, flat, flat, flat, cube, flat, flat, flat, flat, line, flat, line, flat)
    return jax.shard_map(
        functools.partial(on_device, count),
        mesh=mesh,
        in_specs=(rows, rows, rows, lens, lens) + params_in,
        out_specs=(rows, rows, rows) + params_in,
        check_vma=False,
    )
```

time: 2400 us -> 451 us (0.19)
  waiting for transfers between devices: 1350 us -> 228 us
  blocking collectives: 391 us -> 0 us
  matrix products: 286 us -> 0 us
  local copies, waits for them, and re-layouts: 292 us -> 46.6 us
  Pallas kernels: 0 us -> 147 us
  other arithmetic: 57.6 us -> 12.9 us
    reduce_scatter x7 -> x1, waiting for transfers between devices: 951 us -> 149 us  [scatter_plain(): lax.psum_scatter(packed, AXES, scatter_dimension=0, tiled=False).astype(F32)]
    unnamed x21 -> x2, waiting for transfers between devices: 395 us -> 0.03 us
    all_gather x8 -> x0, blocking collectives: 317 us -> none  [the longest x1 43.5 us: on_device(): lax.all_gather(self_bias, ('dp', 'fsdp'), axis=1, tiled=True)]
    dot_general x132 -> x0, matrix products: 286 us -> none  [the longest x20 43.9 us: dense_back(): lax.dot_general(left, right, (((1,), (1,)), ((), ())), preferred_element_...]
    pallas_call x0 -> x3, Pallas kernels: none -> 147 us  [the longest x1 98.2 us: layer(): pl.pallas_call(middle_kernel, grid=(steps,), in_specs=[tok, tok, tok, ids...]
    convert_element_type x60 -> x0, local copies, waits for them, and re-layouts: 104 us -> none  [the longest x16 37.3 us: attend_backward(): grad_keys.reshape(keys.shape).astype(jnp.bfloat16)]
    all_gather x4 -> x1, waiting for transfers between devices: 0.03 us -> 79.7 us  [gather_plain(): whole_set = lax.all_gather(packed, AXES, axis=0, tiled=False)]
    unnamed x2 -> x0, blocking collectives: 74.4 us -> none
  transfers between devices with their start and end apart: 16 -> 2, of which waited for: 11 -> 2; matrix products, arithmetic and copies ran while one was open for 16% -> 1% of each run, Pallas kernels for 0% -> 0%
where the time goes in v1:
time: 451 us; the launch traced here: 449 us
  waiting for transfers between devices  228 us (51%)
  Pallas kernels  147 us (33%)
  local copies, waits for them, and re-layouts  46.6 us (10%)
  between operations  14.3 us (3%)
  other arithmetic  12.9 us (3%)
    reduce_scatter x1, waiting for transfers between devices, scatter_plain(): lax.psum_scatter(packed, AXES, scatter_dimension=0, tiled=False).astype(F32)  149 us
    pallas_call x1, Pallas kernels, layer(): pl.pallas_call(middle_kernel, grid=(steps,), in_specs=[tok, tok, tok, ids...  98.2 us
    all_gather x1, waiting for transfers between devices, gather_plain(): whole_set = lax.all_gather(packed, AXES, axis=0, tiled=False)  79.7 us
    pallas_call x1, Pallas kernels, layer(): pl.pallas_call(self_backward_kernel, grid=(steps,), in_specs=[tok, tok, t...  29.4 us
    pallas_call x1, Pallas kernels, layer(): pl.pallas_call(self_forward_kernel, grid=(steps,), in_specs=[tok, ids_spe...  19.6 us
    unnamed x24, local copies, waits for them, and re-layouts  12.9 us
  transfers between devices with their start and end apart: 2, of which 2 were waited for; matrix products, arithmetic and copies ran while one was open for 1% of the time, Pallas kernels for 0%

profile of v1, /device:TPU:0, one launch (start us, length us, event | category | flops | bytes accessed | tf_op | source)
XLA Modules:
  0.0 449.4 jit_solution(4064727896174150895)
XLA Ops:
  7.2 0.7 reshape.140
  8.0 1.5 concatenate.19
  9.6 0.9 reshape.138
  10.5 0.8 constant_dynamic-update-slice_fusion.6
  11.3 0.7 constant_dynamic-update-slice_fusion.5
  12.0 0.7 constant_dynamic-update-slice_fusion.4
  12.7 0.8 constant_dynamic-update-slice_fusion.3
  13.5 0.7 constant_dynamic-update-slice_fusion.2
  14.2 0.8 bitcast_dynamic-update-slice_fusion
  15.1 0.7 copy-done.3
  15.9 0.9 reduce_window_sum.17
  16.9 0.9 reduce_window_sum.18
  18.5 79.7 %all-gather.3.cloned.1.call-done = bf16[8704,512]{1,0:T(8,128)(2,1)} async-done(((bf16[272,512]{1,0:T(8,128)(2,1)}), bf16[8704,512]{1,0:T(8,128)(2,1)}) %all-gather.3.cloned.1.call-update) | async-done | bytes 8912912 | tf_op jit(solution)/shard_map/all_gather | solution.py:448
  98.2 1.0 slice_bitcast_fusion.1
  99.2 0.9 slice.121
  100.2 4.6 %slice.119 = bf16[32,128,512]{2,1,0:T(8,128)(2,1)} slice(bf16[32,272,512]{2,1,0:T(8,128)(2,1)} %bitcast.86), slice={[0:32], [0:128], [0:512]} | slice | bytes 8388608 | tf_op jit(solution)/shard_map/slice | solution.py:449
  104.8 4.0 fusion.7
  109.3 2.0 copy.88
  111.3 1.9 copy.104
  113.2 1.0 copy-done.1
  114.2 0.8 fusion.8
  115.0 1.5 copy.87
  116.5 1.5 copy.84
  118.6 19.6 %self_forward.1 = (bf16[2048,512]{1,0:T(8,128)(2,1)}, bf16[2048,512]{1,0:T(8,128)(2,1)}, bf16[2048,512]{1,0:T(8,128)(2,1)}, bf16[64,256,256]{2,1,0:T(8,128)(2,1)...) custom-call(bf16[2048,512]{1,0:T(8,128)(2,1)} %bitcast.88, f32[8,2,256]{2,1,0:T(2,128)} %add_convert_fusion.1.ids_ref, ...), custom_call_target="tpu_custom_call" | custom-call | tf_op jit(solution)/shard_map/self_forward/pallas_call | solution.py:375
  138.3 98.2 %middle.1 = (bf16[2048,512]{1,0:T(8,128)(2,1)}, bf16[2048,512]{1,0:T(8,128)(2,1)}, f32[2048,512]{1,0:T(8,128)}, bf16[4,512,512]{2,1,0:T(8,128)(2,1)}, bf16[2048,...) custom-call(f32[2048,512]{1,0:T(8,128)} %get-tuple-element.33.summed_one_ref, ...), custom_call_target="tpu_custom_call" | custom-call | tf_op jit(solution)/shard_map/middle/pallas_call | solution.py:386
  236.5 29.4 %self_backward.1 = (bf16[2048,512]{1,0:T(8,128)(2,1)}, bf16[4,512,512]{2,1,0:T(8,128)(2,1)}, f32[24,512]{1,0:T(8,128)}) custom-call(f32[2048,512]{1,0:T(8,128)} %get-tuple-element.35.sum_one_ref, bf16[2048,512]{1,0:T(8,128)(2,1)} %bitcast.89, bf16[2048,512]{1,0:T(8,128)(2,1)} %get-tuple-element.36.mixture_ref, ...), custom_call_target="tpu_custom_call" | custom-call | tf_op jit(solution)/shard_map/self_backward/pallas_call | solution.py:404
  265.9 0.8 add_convert_fusion
  267.3 2.0 pad_maximum_fusion.1
  269.2 2.6 copy.89
  271.8 3.3 reshape.155
  275.2 0.6 copy.90
  275.9 1.4 copy-done
  277.3 5.7 %pad_maximum_fusion = bf16[32,272,512]{2,1,0:T(8,128)(2,1)} fusion(bf16[32,16,512]{2,1,0:T(8,128)(2,1)S(1)} %fusion.2, bf16[32,64,512]{2,1,0:T(8,128)(2,1)S(1)} %bitcast.92, bf16[32,64,512]{2,1,0:T(8,128)(2,1)} %bitcast.98, bf16[32,128,512]{2,1,0:T(8,128)(2,1)S(1)} %bitcast.81), kind=kLoop, calls=%fused_computation | loop fusion | flops 35651584 | bytes 17825792 | tf_op jit(solution)/shard_map/concatenate | solution.py:474
  283.1 148.6 %reduce-scatter.2.cloned.1.call-done = bf16[1,272,512]{2,1,0:T(8,128)(2,1)} async-done(((bf16[32,272,512]{2,1,0:T(8,128)(2,1)}), bf16[1,272,512]{2,1,0:T(8,128)(2,1)}) %reduce-scatter.2.cloned.1.call-update) | async-done | bytes 278544 | tf_op jit(solution)/shard_map/reduce_scatter | solution.py:478
  431.6 0.9 slice.128
  432.6 0.6 slice.135
  433.2 0.6 slice.129
  433.9 0.6 slice_bitcast_fusion.2
  434.5 1.1 fusion.9
  435.6 0.7 slice_reduce_fusion
  436.5 0.9 slice.141
  437.4 0.7 copy.103
  438.0 0.7 slice_bitcast_fusion
  439.4 0.7 copy.97
  440.0 0.7 copy.95
  440.7 0.6 copy.99
  441.3 0.6 copy.98
  441.9 0.6 copy.96
  (36 shorter events, 3.8 us)
Async XLA Ops:
  7.2 91.0 %all-gather.3.cloned.1.call-start = ((), (), s32[]{:S(2)}) async-start(), calls=%async_computation.2 | async-start | bytes 9191424 | tf_op jit(solution)/shard_map/all_gather | solution.py:448
  15.1 0.7 copy-start.3
  15.8 415.8 %reduce-scatter.2.cloned.1.call-start = ((), (), s32[]{:S(2)}) async-start(), calls=%async_computation.1 | async-start | bytes 9191424 | tf_op jit(solution)/shard_map/reduce_scatter | solution.py:478
  111.3 2.9 copy-start.1
  236.5 29.4 %copy-start.4 = (f32[24,512]{1,0:T(8,128)S(1)}, f32[24,512]{1,0:T(8,128)}, u32[]{:S(2)}) copy-start(f32[24,512]{1,0:T(8,128)} %get-tuple-element.47) | copy-start | bytes 147460
  236.5 30.8 %copy-start.2 = (bf16[4,512,512]{2,1,0:T(8,128)(2,1)S(1)}, bf16[4,512,512]{2,1,0:T(8,128)(2,1)}, u32[]{:S(2)}) copy-start(bf16[4,512,512]{2,1,0:T(8,128)(2,1)} %get-tuple-element.44) | copy-start | bytes 6291460
  275.1 2.2 copy-start
Sparse Core Ops, SparseCore 0:
  15.9 82.2 all-gather.2
  283.2 148.4 reduce-scatter.1

commit v2 on v1

--- a/solution.py
+++ b/solution.py
@@ -143,74 +143,353 @@
     ref[index : index + 1, :] += values
 
 
-def self_forward_kernel(
-    source_ref, ids_ref, weight_ref, table_ref,
+MESH = pl.DeviceIdType.MESH
+ALL = slice(None)
+
+
+def place():
+    z = lax.axis_index("dp")
+    f = lax.axis_index("fsdp")
+    return z, f // 4, (f // 2) % 2, f % 2
+
+
+def device(z, y, x, core):
+    return (z, y * 4 + x * 2 + core)
+
+
+def greet():
+    z, y, x, core = place()
+    partners = [device(lax.rem(z + step, 4), y, x, core) for step in (1, 2, 3)]
+    partners += [device(z, y, 1 - x, core), device(z, 1 - y, x, core), device(z, y, x, 1 - core)]
+    barrier = pltpu.get_barrier_semaphore()
+    for partner in partners:
+        pl.semaphore_signal(barrier, inc=1, device_id=partner, device_id_type=MESH)
+    pl.semaphore_wait(barrier, len(partners))
+
+
+class Gather:
+    def __init__(self, ref, own, first, second, sems, base):
+        self.ref, self.own, self.first, self.second = ref, own, first, second
+        self.local, self.send, self.recv = sems
+        self.base = base
+        self.mats = slice(min(m.start for _, m in own), max(m.stop for _, m in own))
+
+    @staticmethod
+    def slots(own):
+        return 3 * len(own) + 5
+
+    def copy(self, slot, source, target, partner):
+        at = self.base + slot
+        return pltpu.make_async_remote_copy(
+            src_ref=source, dst_ref=target, send_sem=self.send.at[at], recv_sem=self.recv.at[at],
+            device_id=partner, device_id_type=MESH)
+
+    def at(self, half, z, y, x, core):
+        mats, rows, lanes = half
+        return self.ref.at[mats, z, y, x, core, rows, lanes]
+
+    def locals(self):
+        z, y, x, core = place()
+        return [
+            pltpu.make_async_copy(source, self.ref.at[mats, z, y, x, core], self.local.at[self.base + i])
+            for i, (source, mats) in enumerate(self.own)
+        ]
+
+    def hops(self, stage, incoming):
+        z, y, x, core = place()
+        full = (self.mats, ALL, ALL)
+        found = []
+        many = len(self.own)
+        if stage == 0:
+            for step in (1, 2, 3):
+                other = lax.rem(z + (4 - step if incoming else step), 4)
+                for i, (source, mats) in enumerate(self.own):
+                    target = self.ref.at[mats, other if incoming else z, y, x, core]
+                    found.append(self.copy((step - 1) * many + i, source, target, device(other, y, x, core)))
+        if stage == 1:
+            for slot, (py, px) in enumerate(((y, 1 - x), (1 - y, x))):
+                sent = self.at(full, ALL, y, x, core)
+                target = self.at(full, ALL, py, px, core) if incoming else sent
+                found.append(self.copy(3 * many + slot, sent, target, device(z, py, px, core)))
+        if stage == 2:
+            for slot, (half, by, bx, py, px) in enumerate((
+                (self.first, 1 - y, x, y, 1 - x), (self.second, y, 1 - x, 1 - y, x))):
+                sent = self.at(half, ALL, by, bx, core)
+                target = self.at(half, ALL, 1 - y, 1 - x, core) if incoming else sent
+                found.append(self.copy(3 * many + 2 + slot, sent, target, device(z, py, px, core)))
+        if stage == 3:
+            sent = self.at(full, ALL, ALL, ALL, core)
+            target = self.at(full, ALL, ALL, ALL, 1 - core) if incoming else sent
+            found.append(self.copy(3 * many + 4, sent, target, device(z, y, x, 1 - core)))
+        return found
+
+    def start(self, stage):
+        for hop in self.hops(stage, False):
+            hop.start()
+
+    def arrive(self, stage):
+        for hop in self.hops(stage, True):
+            hop.wait_recv()
+
+    def finish(self):
+        for stage in range(4):
+            for hop in self.hops(stage, False):
+                hop.wait_send()
+
+
+def gather_pieces(shards, targets, sems):
+    qkv, out_one, cross_q, cross_kv, out_two, win, wout, small = shards
+    ws, wc, win_all, wout_all, small_all = targets
+    one = lambda n: slice(n, n + 1)
+    plans = [
+        (ws, [(qkv.at[0:2], slice(0, 2))], (one(0), ALL, ALL), (one(1), ALL, ALL)),
+        (ws, [(qkv.at[2:3], one(2)), (out_one, one(3))], (one(2), ALL, ALL), (one(3), ALL, ALL)),
+        (small_all, [(small, one(0))], (ALL, ALL, slice(0, 128)), (ALL, ALL, slice(128, 256))),
+        (wc, [(cross_q, one(0)), (cross_kv, slice(1, 3)), (out_two, one(3))],
+         (slice(0, 2), ALL, ALL), (slice(2, 4), ALL, ALL)),
+        (win_all, [(win, one(0))], (ALL, slice(0, 32), ALL), (ALL, slice(32, 64), ALL)),
+        (wout_all, [(wout, one(0))], (ALL, ALL, slice(0, 1024)), (ALL, ALL, slice(1024, 2048))),
+    ]
+    pieces, base = [], 0
+    for ref, own, first, second in plans:
+        pieces.append(Gather(ref, own, first, second, sems, base))
+        base += Gather.slots(own)
+    return pieces
+
+
+GATHER_SLOTS = 64
+
+BLOCKS = (4, 2, 2, 2)
+
+
+def square(ref, index):
+    return ref[index].reshape(512, 512)
+
+
+def prepare_ids(tgt_ref, src_ref, ids_ref):
+    rows, sents = tgt_ref.shape
+    slots = ids_ref.shape[2]
+    before = lax.broadcasted_iota(jnp.int32, (sents, sents), 0)
+    after = lax.broadcasted_iota(jnp.int32, (sents, sents), 1)
+    ladder = (before <= after).astype(F32)
+    slot = lax.broadcasted_iota(jnp.int32, (sents, slots), 1).astype(F32)
+    for side, ref in enumerate((tgt_ref, src_ref)):
+        lengths = ref[...].astype(F32)
+        finish = lax.dot_general(
+            ladder, lengths, (((0,), (1,)), ((), ())),
+            precision=lax.Precision.HIGHEST, preferred_element_type=F32)
+        for row in range(rows):
+            ended = (finish[:, row : row + 1] <= slot).astype(F32)
+            ids_ref[row, side : side + 1, :] = jnp.sum(ended, axis=0, keepdims=True)
+
+
+def self_forward(
+    step, source_ref, ids_ref, weight_ref, table_ref,
     query_ref, keys_ref, values_ref, shares_ref, mixture_ref, summed_ref, bias_ref,
 ):
     slots = ids_ref.shape[2]
     source = source_ref[...]
-    query = mm_nt(source, weight_ref[0]) + vrow(table_ref, SELF_BQ)
+    query = mm_nt(source, square(weight_ref, 0)) + vrow(table_ref, SELF_BQ)
     query_ref[...] = (query * HEAD_DIM**-0.5).astype(BF16)
-    keys_ref[...] = mm_nt(source, weight_ref[1]).astype(BF16)
-    values_ref[...] = (mm_nt(source, weight_ref[2]) + vrow(table_ref, SELF_BV)).astype(BF16)
+    keys_ref[...] = mm_nt(source, square(weight_ref, 1)).astype(BF16)
+    values_ref[...] = (mm_nt(source, square(weight_ref, 2)) + vrow(table_ref, SELF_BV)).astype(BF16)
 
     def one_row(row, carry):
         at = pl.ds(pl.multiple_of(row * slots, slots), slots)
-        ids = ids_ref[row]
+        ids = ids_ref[step * STEP_ROWS + row]
         bias_ref[...] = mask_bias(ids[0:1], ids[0:1], True)
         attend_rows(query_ref, keys_ref, values_ref, bias_ref, shares_ref, mixture_ref, row, at)
         return carry
 
     lax.fori_loop(0, STEP_ROWS, one_row, 0)
     summed_ref[...] = (
-        source.astype(F32) + mm_nt(mixture_ref[...], weight_ref[3]) + vrow(table_ref, SELF_BO)
+        source.astype(F32) + mm_nt(mixture_ref[...], square(weight_ref, 3)) + vrow(table_ref, SELF_BO)
     )
 
 
-def middle_kernel(
-    summed_one_ref, remote_ref, upstream_ref, ids_ref, weight_ref, win_ref, wout_ref, table_ref,
-    result_ref, grad_remote_ref, sum_one_ref, dweight_ref, dwin_ref, dwout_ref, dtable_ref,
-    low_ref, query_ref, keys_ref, values_ref, shares_ref, mixture_ref, bias_ref,
-    normed_one_ref, normed_two_ref, hidden_ref, active_ref, slope_ref, accum_ref,
-    gq_ref, gk_ref, gv_ref, low_two_ref, grad_low_ref, acc_ref, accin_ref, accout_ref, acct_ref,
+def cross_forward(
+    step, summed_one_ref, remote_ref, ids_ref, weight_ref, table_ref,
+    query_ref, keys_ref, values_ref, shares_ref, mixture_ref, summed_ref, bias_ref, hidden_ref,
+):
+    slots = ids_ref.shape[2]
+    normed_one, _ = norm_stats(summed_one_ref[...])
+    hidden_one = normed_one * vrow(table_ref, SELF_G) + vrow(table_ref, SELF_S)
+    hidden_ref[...] = hidden_one
+    query = mm_nt(hidden_one.astype(BF16), square(weight_ref, 0)) + vrow(table_ref, CROSS_BQ)
+    query_ref[...] = (query * HEAD_DIM**-0.5).astype(BF16)
+    remote = remote_ref[...]
+    keys_ref[...] = mm_nt(remote, square(weight_ref, 1)).astype(BF16)
+    values_ref[...] = (mm_nt(remote, square(weight_ref, 2)) + vrow(table_ref, CROSS_BV)).astype(BF16)
+
+    def one_row(row, carry):
+        at = pl.ds(pl.multiple_of(row * slots, slots), slots)
+        ids = ids_ref[step * STEP_ROWS + row]
+        bias_ref[...] = mask_bias(ids[1:2], ids[0:1], False)
+        attend_rows(query_ref, keys_ref, values_ref, bias_ref, shares_ref, mixture_ref, row, at)
+        return carry
+
+    lax.fori_loop(0, STEP_ROWS, one_row, 0)
+    summed_ref[...] = (
+        hidden_ref[...] + mm_nt(mixture_ref[...], square(weight_ref, 3)) + vrow(table_ref, CROSS_BO)
+    )
+
+
+def table_from_columns(columns, table_ref):
+    turned = jnp.transpose(columns[:, :128])
+    table_ref[0:TABLE, :] = turned[0:TABLE]
+    parts = [columns[:, 128 + k : 129 + k].reshape(32, 1, 16, 1) for k in range(4)]
+    line = jnp.concatenate(parts, axis=1).reshape(2048, 1)
+    line = jnp.transpose(jnp.broadcast_to(line, (2048, 128)))
+    for k in range(4):
+        table_ref[FFN_BI + k : FFN_BI + k + 1, :] = line[0:1, k * 512 : (k + 1) * 512]
+
+
+def columns_from_table(rows):
+    rows = jnp.concatenate([rows, jnp.zeros((128 - TABLE, 512), F32)], axis=0)
+    columns = jnp.transpose(rows)
+    lane = lax.broadcasted_iota(jnp.int32, (512, 128), 1)
+    line = jnp.concatenate([columns[:, FFN_BI + k : FFN_BI + k + 1] for k in range(4)], axis=0)
+    line = line.reshape(32, 4, 16, 1)
+    second = jnp.zeros((512, 128), F32)
+    for k in range(4):
+        second = jnp.where(lane == k, line[:, k].reshape(512, 1), second)
+    return jnp.concatenate([columns, second], axis=1)
+
+
+FIRST_OUT = 12
+
+
+def first_kernel(gathers, steps, *refs):
+    step = pl.program_id(0)
+    if gathers:
+        (source_ref, remote_ref, tgt_ref, src_ref), shards, refs = refs[:4], refs[4:12], refs[12:]
+    else:
+        (source_ref, remote_ref, tgt_ref, src_ref, ws_ref, wc_ref, table_ref), refs = refs[:7], refs[7:]
+    (q1_ref, k1_ref, v1_ref, p1_ref, m1_ref, s1_ref,
+     q2_ref, k2_ref, v2_ref, p2_ref, m2_ref, s2_ref), refs = refs[:FIRST_OUT], refs[FIRST_OUT:]
+    if gathers:
+        (table_ref, ws_out, wc_out, win_out, wout_out), refs = refs[:5], refs[5:]
+        (ws_ref, wc_ref, small_ref, *sems, out_sem), refs = refs[:7], refs[7:]
+        pieces = gather_pieces(shards, (ws_ref, wc_ref, win_out, wout_out, small_ref), sems)
+        one, two, small, cross, inner, outer = pieces
+        saves = [pltpu.make_async_copy(ws_ref, ws_out, out_sem.at[0]), pltpu.make_async_copy(wc_ref, wc_out, out_sem.at[1])]
+    bias_ref, hidden_ref, keep_ref, ids_ref = refs
+
+    @pl.when(step == 0)
+    def _():
+        if gathers:
+            greet()
+            head = (one, two, small)
+            for piece in pieces:
+                for copy in piece.locals():
+                    copy.start()
+            for piece in head:
+                piece.start(0)
+        prepare_ids(tgt_ref, src_ref, ids_ref)
+        if gathers:
+            for piece in pieces:
+                for copy in piece.locals():
+                    copy.wait()
+            for piece in head:
+                piece.arrive(0)
+                piece.start(1)
+            cross.start(0)
+            inner.start(0)
+            for piece in head:
+                piece.arrive(1)
+                piece.start(2)
+            cross.arrive(0)
+            cross.start(1)
+            for piece in head:
+                piece.arrive(2)
+                piece.start(3)
+            for piece in head:
+                piece.arrive(3)
+            table_from_columns(small_ref[0].reshape(512, 256).astype(F32), table_ref)
+            saves[0].start()
+
+    @pl.when(step < steps)
+    def _():
+        self_forward(
+            step, source_ref, ids_ref, ws_ref, table_ref,
+            q1_ref, k1_ref, v1_ref, p1_ref, m1_ref, s1_ref, bias_ref)
+        keep_ref[step] = s1_ref[...]
+
+    @pl.when(step >= steps)
+    def _():
+        at = step - steps
+        cross_forward(
+            at, keep_ref.at[at], remote_ref, ids_ref, wc_ref, table_ref,
+            q2_ref, k2_ref, v2_ref, p2_ref, m2_ref, s2_ref, bias_ref, hidden_ref)
+
+    if gathers:
+        @pl.when(step == 0)
+        def _():
+            cross.arrive(1)
+            cross.start(2)
+            inner.arrive(0)
+            inner.start(1)
+            outer.start(0)
+
+        @pl.when(step == 1)
+        def _():
+            cross.arrive(2)
+            cross.start(3)
+
+        @pl.when(step == 2)
+        def _():
+            inner.arrive(1)
+            inner.start(2)
+            outer.arrive(0)
+            outer.start(1)
+
+        @pl.when(step == steps - 1)
+        def _():
+            cross.arrive(3)
+            saves[1].start()
+
+        @pl.when(step == steps)
+        def _():
+            inner.arrive(2)
+            inner.start(3)
+            outer.arrive(1)
+            outer.start(2)
+
+        @pl.when(step == 2 * steps - 2)
+        def _():
+            outer.arrive(2)
+            outer.start(3)
+
+        @pl.when(step == 2 * steps - 1)
+        def _():
+            inner.arrive(3)
+            outer.arrive(3)
+            for piece in pieces:
+                piece.finish()
+            for copy in saves:
+                copy.wait()
+
+
+def ffn_kernel(
+    summed_two_ref, upstream_ref, win_ref, wout_ref, table_ref,
+    result_ref, sum_two_ref, dwin_ref, dwout_ref, dtable_ref,
+    normed_two_ref, hidden_ref, active_ref, slope_ref, accum_ref,
+    low_two_ref, grad_low_ref, accin_ref, accout_ref, acct_ref,
 ):
     step = pl.program_id(0)
-    slots = ids_ref.shape[2]
     chunks = win_ref.shape[0] // 512
 
     @pl.when(step == 0)
     def _():
-        acc_ref[...] = jnp.zeros_like(acc_ref)
         accin_ref[...] = jnp.zeros_like(accin_ref)
         accout_ref[...] = jnp.zeros_like(accout_ref)
         acct_ref[...] = jnp.zeros_like(acct_ref)
 
-    normed_one, inverse_one = norm_stats(summed_one_ref[...])
-    normed_one_ref[...] = normed_one
-    hidden_one = normed_one * vrow(table_ref, SELF_G) + vrow(table_ref, SELF_S)
-    low_ref[...] = hidden_one.astype(BF16)
-    query = mm_nt(low_ref[...], weight_ref[0]) + vrow(table_ref, CROSS_BQ)
-    query_ref[...] = (query * HEAD_DIM**-0.5).astype(BF16)
-    remote = remote_ref[...]
-    keys_ref[...] = mm_nt(remote, weight_ref[1]).astype(BF16)
-    values_ref[...] = (mm_nt(remote, weight_ref[2]) + vrow(table_ref, CROSS_BV)).astype(BF16)
-
-    def one_row(row, carry):
-        at = pl.ds(pl.multiple_of(row * slots, slots), slots)
-        ids = ids_ref[row]
-        bias_ref[...] = mask_bias(ids[1:2], ids[0:1], False)
-        attend_rows(query_ref, keys_ref, values_ref, bias_ref, shares_ref, mixture_ref, row, at)
-        return carry
-
-    lax.fori_loop(0, STEP_ROWS, one_row, 0)
-    hidden_one = normed_one_ref[...] * vrow(table_ref, SELF_G) + vrow(table_ref, SELF_S)
-    summed_two = hidden_one + mm_nt(mixture_ref[...], weight_ref[3]) + vrow(table_ref, CROSS_BO)
-    normed_two, inverse_two = norm_stats(summed_two)
+    normed_two, inverse_two = norm_stats(summed_two_ref[...])
     normed_two_ref[...] = normed_two
     hidden_two = normed_two * vrow(table_ref, CROSS_G) + vrow(table_ref, CROSS_S)
     hidden_ref[...] = hidden_two
     low_two_ref[...] = hidden_two.astype(BF16)
-
     accum_ref[...] = jnp.zeros_like(accum_ref)
 
     def ffn_chunk(chunk, carry):
@@ -255,74 +534,67 @@
         return carry
 
     lax.fori_loop(0, chunks, ffn_chunk_back, 0)
-
     grad_hidden_two = accum_ref[...]
     normed_two = normed_two_ref[...]
     add_row(acct_ref, CROSS_G, column_sum(grad_hidden_two * normed_two))
     add_row(acct_ref, CROSS_S, column_sum(grad_hidden_two))
-    sum_two = norm_back(grad_hidden_two, normed_two, inverse_two, vrow(table_ref, CROSS_G))
-    accum_ref[...] = sum_two
-    grad_low_ref[...] = sum_two.astype(BF16)
-    grad_two = grad_low_ref[...]
+    sum_two_ref[...] = norm_back(grad_hidden_two, normed_two, inverse_two, vrow(table_ref, CROSS_G))
+
+    @pl.when(step == pl.num_programs(0) - 1)
+    def _():
+        dwin_ref[...] = accin_ref[...].astype(BF16)
+        dwout_ref[...] = accout_ref[...].astype(BF16)
+        dtable_ref[...] = acct_ref[...]
+
+
+def cross_backward(
+    sum_two_ref, summed_one_ref, remote_ref, mixture_ref, query_ref, keys_ref, values_ref, shares_ref,
+    weight_ref, table_ref, grad_remote_ref, sum_one_ref, up_ref, gq_ref, gk_ref, gv_ref, acc_ref, acct_ref,
+):
+    slots = shares_ref.shape[1]
+    grad_two = sum_two_ref[...].astype(BF16)
     add_row(acct_ref, CROSS_BO, column_sum(grad_two))
     acc_ref[3] += mm_tn(grad_two, mixture_ref[...])
-    mixture_ref[...] = mm_nn(grad_two, weight_ref[3]).astype(BF16)
+    up_ref[...] = mm_nn(grad_two, square(weight_ref, 3)).astype(BF16)
 
     def one_row_back(row, carry):
         at = pl.ds(pl.multiple_of(row * slots, slots), slots)
         attend_rows_back(
-            mixture_ref, query_ref, keys_ref, values_ref, shares_ref, gq_ref, gk_ref, gv_ref, row, at
-        )
+            up_ref, query_ref, keys_ref, values_ref, shares_ref, gq_ref, gk_ref, gv_ref, row, at)
         return carry
 
     lax.fori_loop(0, STEP_ROWS, one_row_back, 0)
+    normed_one, inverse_one = norm_stats(summed_one_ref[...])
+    low = (normed_one * vrow(table_ref, SELF_G) + vrow(table_ref, SELF_S)).astype(BF16)
     grad_query, grad_keys, grad_values = gq_ref[...], gk_ref[...], gv_ref[...]
     add_row(acct_ref, CROSS_BQ, column_sum(grad_query))
     add_row(acct_ref, CROSS_BV, column_sum(grad_values))
-    acc_ref[0] += mm_tn(grad_query, low_ref[...])
+    acc_ref[0] += mm_tn(grad_query, low)
     acc_ref[1] += mm_tn(grad_keys, remote_ref[...])
     acc_ref[2] += mm_tn(grad_values, remote_ref[...])
     grad_remote_ref[...] = (
-        mm_nn(grad_keys, weight_ref[1]) + mm_nn(grad_values, weight_ref[2])
+        mm_nn(grad_keys, square(weight_ref, 1)) + mm_nn(grad_values, square(weight_ref, 2))
     ).astype(BF16)
-
-    grad_hidden_one = accum_ref[...] + mm_nn(grad_query, weight_ref[0])
-    normed_one = normed_one_ref[...]
+    grad_hidden_one = sum_two_ref[...] + mm_nn(grad_query, square(weight_ref, 0))
     add_row(acct_ref, SELF_G, column_sum(grad_hidden_one * normed_one))
     add_row(acct_ref, SELF_S, column_sum(grad_hidden_one))
     sum_one_ref[...] = norm_back(grad_hidden_one, normed_one, inverse_one, vrow(table_ref, SELF_G))
 
-    @pl.when(step == pl.num_programs(0) - 1)
-    def _():
-        dweight_ref[...] = acc_ref[...].astype(BF16)
-        dwin_ref[...] = accin_ref[...].astype(BF16)
-        dwout_ref[...] = accout_ref[...].astype(BF16)
-        dtable_ref[...] = acct_ref[...]
-
-
-def self_backward_kernel(
+
+def self_backward(
     sum_one_ref, source_ref, mixture_ref, query_ref, keys_ref, values_ref, shares_ref, weight_ref,
-    grad_source_ref, dweight_ref, dtable_ref,
-    up_ref, gq_ref, gk_ref, gv_ref, acc_ref, acct_ref,
+    grad_source_ref, up_ref, gq_ref, gk_ref, gv_ref, acc_ref, acct_ref,
 ):
-    step = pl.program_id(0)
     slots = shares_ref.shape[1]
-
-    @pl.when(step == 0)
-    def _():
-        acc_ref[...] = jnp.zeros_like(acc_ref)
-        acct_ref[...] = jnp.zeros_like(acct_ref)
-
     grad_one = sum_one_ref[...].astype(BF16)
     add_row(acct_ref, SELF_BO, column_sum(grad_one))
     acc_ref[3] += mm_tn(grad_one, mixture_ref[...])
-    up_ref[...] = mm_nn(grad_one, weight_ref[3]).astype(BF16)
+    up_ref[...] = mm_nn(grad_one, square(weight_ref, 3)).astype(BF16)
 
     def one_row_back(row, carry):
         at = pl.ds(pl.multiple_of(row * slots, slots), slots)
         attend_rows_back(
-            up_ref, query_ref, keys_ref, values_ref, shares_ref, gq_ref, gk_ref, gv_ref, row, at
-        )
+            up_ref, query_ref, keys_ref, values_ref, shares_ref, gq_ref, gk_ref, gv_ref, row, at)
         return carry
 
     lax.fori_loop(0, STEP_ROWS, one_row_back, 0)
@@ -335,93 +607,367 @@
     acc_ref[2] += mm_tn(grad_values, source)
     grad_source_ref[...] = (
         sum_one_ref[...]
-        + mm_nn(grad_query, weight_ref[0])
-        + mm_nn(grad_keys, weight_ref[1])
-        + mm_nn(grad_values, weight_ref[2])
+        + mm_nn(grad_query, square(weight_ref, 0))
+        + mm_nn(grad_keys, square(weight_ref, 1))
+        + mm_nn(grad_values, square(weight_ref, 2))
     ).astype(BF16)
 
-    @pl.when(step == pl.num_programs(0) - 1)
-    def _():
-        dweight_ref[...] = acc_ref[...].astype(BF16)
-        dtable_ref[...] = acct_ref[...]
-
-
-def whole(shape):
+
+class Scatter:
+    def __init__(self, full, mine, halves, bufs, units, sems, base):
+        self.full, self.mine, self.halves, self.units = full, mine, halves, units
+        self.total, self.pair, self.far, self.near = bufs
+        self.local, self.send, self.recv = sems
+        self.base = base
+
+    def copy(self, slot, source, target, partner):
+        at = self.base + slot
+        return pltpu.make_async_remote_copy(
+            src_ref=source, dst_ref=target, send_sem=self.send.at[at], recv_sem=self.recv.at[at],
+            device_id=partner, device_id_type=MESH)
+
+    def hops(self, stage, incoming=False):
+        z, y, x, core = place()
+        if stage == 0:
+            return [self.copy(0, self.full.at[:, :, :, :, 1 - core], self.pair, device(z, y, x, 1 - core))]
+        sides = ((y, 1 - x), (1 - y, x))
+        if stage == 1:
+            return [
+                self.copy(1 + i, self.total.at[h[0], :, 1 - y, 1 - x, h[1], h[2]], self.far.at[i], device(z, *side, core))
+                for i, (side, h) in enumerate(zip(sides, self.halves))
+            ]
+        if stage == 2:
+            return [
+                self.copy(3 + i, self.total.at[:, :, side[0], side[1]], self.near.at[i], device(z, *side, core))
+                for i, side in enumerate(sides)
+            ]
+        found = []
+        for step in (1, 2, 3):
+            other = lax.rem(z + step, 4)
+            found.append(self.copy(4 + step, self.total.at[:, other, y, x], self.units.at[step], device(other, y, x, core)))
+        return found
+
+    def own(self):
+        z, y, x, _ = place()
+        return pltpu.make_async_copy(self.total.at[:, z, y, x], self.units.at[0], self.local.at[self.base])
+
+    def start(self, stage):
+        for hop in self.hops(stage):
+            hop.start()
+        if stage == 3:
+            self.own().start()
+
+    def arrive(self, stage):
+        for hop in self.hops(stage):
+            hop.wait_recv()
+        z, y, x, core = place()
+        if stage == 0:
+            mats = self.total.shape[0]
+            for mat in range(mats):
+                self.total[mat] = (self.mine(mat, core) + self.pair[mat].astype(F32)).astype(BF16)
+        if stage == 1:
+            for i, (h, at) in enumerate(zip(self.halves, ((1 - y, x), (y, 1 - x)))):
+                old = self.total[h[0], :, at[0], at[1], h[1], h[2]].astype(F32)
+                self.total[h[0], :, at[0], at[1], h[1], h[2]] = (old + self.far[i].astype(F32)).astype(BF16)
+        if stage == 2:
+            old = self.total[:, :, y, x].astype(F32)
+            self.total[:, :, y, x] = (
+                old + self.near[0].astype(F32) + self.near[1].astype(F32)).astype(BF16)
+
+    def finish(self):
+        for stage in range(4):
+            for hop in self.hops(stage):
+                hop.wait_send()
+        self.own().wait()
+
+
+SCATTER_SLOTS = 8
+
+
+def last_kernel(scatters, steps, *refs):
+    step = pl.program_id(0)
+    (sum_two_ref, s1_ref, remote_ref, m2_ref, q2_ref, k2_ref, v2_ref, p2_ref,
+     source_ref, m1_ref, q1_ref, k1_ref, v1_ref, p1_ref, ws_ref, wc_ref, table_ref), refs = refs[:17], refs[17:]
+    if scatters:
+        (dwin, dwout, dtable_in), refs = refs[:3], refs[3:]
+    (grad_remote_ref, grad_source_ref), refs = refs[:2], refs[2:]
+    if scatters:
+        units, refs = refs[:5], refs[5:]
+    else:
+        (dself_ref, dcross_ref, dtable_ref), refs = refs[:3], refs[3:]
+    (up_ref, gq_ref, gk_ref, gv_ref, keep_ref, accs_ref, accc_ref, acct_ref), refs = refs[:8], refs[8:]
+    if scatters:
+        (lows_ref, lowc_ref, lowt_ref, win_own, wout_own), refs = refs[:5], refs[5:]
+        bufs = [refs[4 * i : 4 * i + 4] for i in range(5)]
+        local, *sems = refs[20:]
+        sems = (local, *sems)
+        top = lambda ref: (lambda mat, core: ref[mat].astype(F32))
+        acc = lambda ref: (lambda mat, core: ref[mat, :, :, :, core])
+        mats = ((slice(0, 2), ALL, ALL), (slice(2, 4), ALL, ALL))
+        wide = lambda a, b: ((ALL, ALL, slice(0, a)), (ALL, ALL, slice(a, b)))
+        inner = Scatter(dwin, top(win_own), ((ALL, slice(0, 32), ALL), (ALL, slice(32, 64), ALL)), bufs[0], units[0], sems, 0)
+        outer = Scatter(dwout, top(wout_own), wide(1024, 2048), bufs[1], units[1], sems, 8)
+        cross = Scatter(lowc_ref, acc(accc_ref), mats, bufs[2], units[2], sems, 16)
+        own = Scatter(lows_ref, acc(accs_ref), mats, bufs[3], units[3], sems, 24)
+        small = Scatter(lowt_ref, lambda mat, core: lowt_ref[mat, :, :, :, core].astype(F32), wide(128, 256), bufs[4], units[4], sems, 32)
+        everything = (inner, outer, cross, own, small)
+        core = lax.axis_index("fsdp") % 2
+        fetch = [
+            pltpu.make_async_copy(dwin.at[:, :, :, :, core], win_own, local.at[1]),
+            pltpu.make_async_copy(dwout.at[:, :, :, :, core], wout_own, local.at[2]),
+        ]
+
+    @pl.when(step == 0)
+    def _():
+        if scatters:
+            greet()
+            inner.start(0)
+            outer.start(0)
+            for copy in fetch:
+                copy.start()
+        accs_ref[...] = jnp.zeros_like(accs_ref)
+        accc_ref[...] = jnp.zeros_like(accc_ref)
+        acct_ref[...] = jnp.zeros_like(acct_ref)
+
+    @pl.when(step < steps)
+    def _():
+        cross_backward(
+            sum_two_ref, s1_ref, remote_ref, m2_ref, q2_ref, k2_ref, v2_ref, p2_ref, wc_ref, table_ref,
+            grad_remote_ref, keep_ref.at[step], up_ref, gq_ref, gk_ref, gv_ref, Flat(accc_ref), acct_ref)
+
+    @pl.when(step >= steps)
+    def _():
+        self_backward(
+            keep_ref.at[step - steps], source_ref, m1_ref, q1_ref, k1_ref, v1_ref, p1_ref, ws_ref,
+            grad_source_ref, up_ref, gq_ref, gk_ref, gv_ref, Flat(accs_ref), acct_ref)
+
+    if not scatters:
+        @pl.when(step == 2 * steps - 1)
+        def _():
+            dself_ref[...] = accs_ref[...].astype(BF16)
+            dcross_ref[...] = accc_ref[...].astype(BF16)
+            dtable_ref[...] = acct_ref[...]
+        return
+
+    @pl.when(step == 0)
+    def _():
+        for copy in fetch:
+            copy.wait()
+        for piece in (inner, outer):
+            piece.arrive(0)
+            piece.start(1)
+
+    @pl.when(step == 1)
+    def _():
+        for piece in (inner, outer):
+            piece.arrive(1)
+            piece.start(2)
+
+    @pl.when(step == steps - 1)
+    def _():
+        for mat in range(4):
+            lowc_ref[mat] = accc_ref[mat].astype(BF16)
+        cross.start(0)
+        for piece in (inner, outer):
+            piece.arrive(2)
+            piece.start(3)
+
+    @pl.when(step == steps)
+    def _():
+        cross.arrive(0)
+        cross.start(1)
+
+    @pl.when(step == steps + 1)
+    def _():
+        cross.arrive(1)
+        cross.start(2)
+
+    @pl.when(step == 2 * steps - 2)
+    def _():
+        cross.arrive(2)
+        cross.start(3)
+
+    @pl.when(step == 2 * steps - 1)
+    def _():
+        for mat in range(4):
+            lows_ref[mat] = accs_ref[mat].astype(BF16)
+        own.start(0)
+        table = columns_from_table(acct_ref[...] + dtable_in[...]).astype(BF16)
+        lowt_ref[...] = table.reshape(lowt_ref.shape)
+        small.start(0)
+        for stage in range(3):
+            for piece in (own, small):
+                piece.arrive(stage)
+                piece.start(stage + 1)
+        for piece in everything:
+            piece.arrive(3)
+        for piece in everything:
+            piece.finish()
+
+
+class Flat:
+    def __init__(self, ref):
+        self.ref = ref
+
+    def __getitem__(self, index):
+        return self.ref[index].reshape(512, 512)
+
+    def __setitem__(self, index, values):
+        self.ref[index] = values.reshape(self.ref.shape[1:])
+
+
+def sum_kernel(win_ref, wout_ref, cross_ref, own_ref, small_ref, *outs):
+    total = lambda ref: (
+        ref[0].astype(F32) + ref[1].astype(F32) + ref[2].astype(F32) + ref[3].astype(F32))
+    (qkv, bias_one, out_one, norm_one, cross_q, cross_kv, bias_two, out_two, norm_two,
+     win, win_bias, wout, wout_bias, norm_three) = outs
+    own, cross = total(own_ref), total(cross_ref)
+    qkv[...] = own[0:3]
+    out_one[...] = own[3]
+    cross_q[...] = cross[0]
+    cross_kv[...] = cross[1:3]
+    out_two[...] = cross[3]
+    win[...] = total(win_ref)[0]
+    wout[...] = total(wout_ref)[0]
+    small = jnp.transpose(total(small_ref)[0])
+    bias_one[...] = small[SELF_BQ : SELF_BQ + 3]
+    norm_one[...] = small[SELF_G : SELF_G + 2]
+    bias_two[...] = small[CROSS_BQ : CROSS_BQ + 3]
+    norm_two[...] = small[CROSS_G : CROSS_G + 2]
+    wout_bias[...] = small[FFN_BO : FFN_BO + 1]
+    norm_three[...] = small[FFN_G : FFN_G + 2]
+    win_bias[...] = small[128:132]
+
+
+def fixed(shape):
     return pl.BlockSpec(shape, lambda i: (0,) * len(shape), pipeline_mode=pl.Buffered(1))
 
 
-def tokens_spec(block, width):
-    return pl.BlockSpec((block, width), lambda i: (i, 0))
-
-
-def params(limit):
-    return pltpu.CompilerParams(vmem_limit_bytes=limit, dimension_semantics=("arbitrary",))
-
-
-def layer(decoder_in, memory, out_grad, ids, weight_self, weight_cross, win, wout, table):
+def shape_of(*shape, dtype=BF16):
+    return jax.ShapeDtypeStruct(shape, dtype)
+
+
+def params(limit, collective=None):
+    if collective is None:
+        return pltpu.CompilerParams(vmem_limit_bytes=limit, dimension_semantics=("arbitrary",))
+    return pltpu.CompilerParams(
+        vmem_limit_bytes=limit, dimension_semantics=("arbitrary",), collective_id=collective,
+        has_side_effects=True)
+
+
+ANYWHERE = pl.BlockSpec(memory_space=pl.ANY)
+SQUARES = (4,) + BLOCKS + (16, 512)
+WIN_BLOCKS = (1,) + BLOCKS + (64, 512)
+WOUT_BLOCKS = (1,) + BLOCKS + (16, 2048)
+SMALL_BLOCKS = (1,) + BLOCKS + (16, 256)
+
+
+def layer(decoder_in, memory, out_grad, tgt_len, src_len, shards=None, weights=None):
     rows, slots, width = decoder_in.shape
-    hidden = win.shape[0]
     tokens = rows * slots
     block = STEP_ROWS * slots
     steps = rows // STEP_ROWS
     shares_block = (STEP_ROWS * HEADS, slots, slots)
     source = decoder_in.reshape(tokens, width)
-    shape = jax.ShapeDtypeStruct
-    low = shape((tokens, width), BF16)
-    full = shape((tokens, width), F32)
-    tok = tokens_spec(block, width)
-    ids_spec = pl.BlockSpec((STEP_ROWS, 2, slots), lambda i: (i, 0, 0))
-    shares_spec = pl.BlockSpec(shares_block, lambda i: (i, 0, 0))
-    query, keys, values, shares, mixture, summed = pl.pallas_call(
-        self_forward_kernel,
+    remote = memory.reshape(tokens, width)
+    low, full = shape_of(tokens, width), shape_of(tokens, width, dtype=F32)
+    vm = pltpu.VMEM
+    dma = pltpu.SemaphoreType.DMA
+    early = lambda i: jnp.minimum(i, steps - 1)
+    late = lambda i: jnp.maximum(i - steps, 0)
+    tok = lambda when: pl.BlockSpec((block, width), lambda i: (when(i), 0))
+    shares = lambda when: pl.BlockSpec(shares_block, lambda i: (when(i), 0, 0))
+    half_out = lambda when: [tok(when), tok(when), tok(when), shares(when), tok(when), tok(when)]
+    shares_shape = shape_of(rows * HEADS, slots, slots)
+    half_shape = [low, low, low, shares_shape, low, full]
+    table_shape = shape_of(TABLE, width, dtype=F32)
+    table_spec = fixed((TABLE, width))
+    ins = [source, remote, tgt_len, src_len]
+    in_specs = [tok(early), tok(late), fixed(tgt_len.shape), fixed(src_len.shape)]
+    out_shape, out_specs = half_shape * 2, half_out(early) + half_out(late)
+    scratch = []
+    if shards is not None:
+        ins += list(shards)
+        in_specs += [ANYWHERE] * 8
+        out_shape += [table_shape, shape_of(*SQUARES), shape_of(*SQUARES), shape_of(*WIN_BLOCKS), shape_of(*WOUT_BLOCKS)]
+        out_specs += [table_spec] + [ANYWHERE] * 4
+        scratch += [vm(SQUARES, BF16), vm(SQUARES, BF16), vm(SMALL_BLOCKS, BF16)]
+        scratch += [dma((GATHER_SLOTS,)), dma((GATHER_SLOTS,)), dma((GATHER_SLOTS,)), dma((2,))]
+    else:
+        ws, wc, win, wout, table = weights
+        ws, wc = ws.reshape(SQUARES), wc.reshape(SQUARES)
+        ins += [ws, wc, table]
+        in_specs += [fixed(SQUARES), fixed(SQUARES), table_spec]
+    scratch += [vm((slots, slots), F32), vm((block, width), F32), vm((steps, block, width), F32), vm((rows, 2, slots), F32)]
+    outs = pl.pallas_call(
+        functools.partial(first_kernel, shards is not None, steps),
+        grid=(2 * steps,), in_specs=in_specs, out_specs=out_specs, out_shape=out_shape, scratch_shapes=scratch,
+        compiler_params=params(60 << 20, None if shards is None else 1), name="first",
+    )(*ins)
+    q1, k1, v1, p1, m1, s1, q2, k2, v2, p2, m2, s2 = outs[:FIRST_OUT]
+    if shards is not None:
+        table, ws, wc, win, wout = outs[FIRST_OUT:]
+        win = win.reshape(-1, width)
+        wout = wout.reshape(width, -1)
+    hidden = win.shape[0]
+    now = lambda i: i
+    result, sum_two, dwin, dwout, dtable = pl.pallas_call(
+        ffn_kernel,
         grid=(steps,),
-        in_specs=[tok, ids_spec, whole(weight_self.shape), whole(table.shape)],
-        out_specs=[tok, tok, tok, shares_spec, tok, tok],
-        out_shape=[low, low, low, shape((rows * HEADS, slots, slots), BF16), low, full],
-        scratch_shapes=[pltpu.VMEM((slots, slots), F32)],
-        compiler_params=params(56 << 20),
-        name="self_forward",
-    )(source, ids, weight_self, table)
-    vm = pltpu.VMEM
-    result, grad_remote, sum_one, dcross, dwin, dwout, dtable = pl.pallas_call(
-        middle_kernel,
-        grid=(steps,),
-        in_specs=[tok, tok, tok, ids_spec, whole(weight_cross.shape), whole(win.shape), whole(wout.shape), whole(table.shape)],
-        out_specs=[tok, tok, tok, whole(weight_cross.shape), whole(win.shape), whole(wout.shape), whole(table.shape)],
-        out_shape=[low, low, full, shape(weight_cross.shape, BF16), shape(win.shape, BF16), shape(wout.shape, BF16), shape(table.shape, F32)],
+        in_specs=[tok(now), tok(now), fixed(win.shape), fixed(wout.shape), table_spec],
+        out_specs=[tok(now), tok(now), fixed(win.shape), fixed(wout.shape), table_spec],
+        out_shape=[low, full, shape_of(*win.shape), shape_of(*wout.shape), table_shape],
         scratch_shapes=[
-            vm((block, width), BF16), vm((block, width), BF16), vm((block, width), BF16), vm((block, width), BF16),
-            vm(shares_block, BF16), vm((block, width), BF16), vm((slots, slots), F32),
-            vm((block, width), F32), vm((block, width), F32), vm((block, width), F32),
-            vm((block, hidden), BF16), vm((block, hidden), BF16), vm((block, width), F32),
-            vm((block, width), BF16), vm((block, width), BF16), vm((block, width), BF16),
-            vm((block, width), BF16), vm((block, width), BF16),
-            vm(weight_cross.shape, F32), vm(win.shape, F32), vm(wout.shape, F32), vm(table.shape, F32),
+            vm((block, width), F32), vm((block, width), F32), vm((block, hidden), BF16), vm((block, hidden), BF16),
+            vm((block, width), F32), vm((block, width), BF16), vm((block, width), BF16),
+            vm(win.shape, F32), vm(wout.shape, F32), vm((TABLE, width), F32),
         ],
-        compiler_params=params(63 << 20),
-        name="middle",
-    )(summed, memory.reshape(tokens, width), out_grad.reshape(tokens, width), ids, weight_cross, win, wout, table)
-    grad_source, dself, dtable_self = pl.pallas_call(
-        self_backward_kernel,
-        grid=(steps,),
-        in_specs=[tok, tok, tok, tok, tok, tok, shares_spec, whole(weight_self.shape)],
-        out_specs=[tok, whole(weight_self.shape), whole(table.shape)],
-        out_shape=[low, shape(weight_self.shape, BF16), shape(table.shape, F32)],
-        scratch_shapes=[
-            vm((block, width), BF16), vm((block, width), BF16), vm((block, width), BF16), vm((block, width), BF16),
-            vm(weight_self.shape, F32), vm(table.shape, F32),
-        ],
-        compiler_params=params(56 << 20),
-        name="self_backward",
-    )(sum_one, source, mixture, query, keys, values, shares, weight_self)
+        compiler_params=params(60 << 20), name="feed_forward",
+    )(s2, out_grad.reshape(tokens, width), win, wout, table)
+
+    ins = [sum_two, s1, remote, m2, q2, k2, v2, p2, source, m1, q1, k1, v1, p1, ws, wc, table]
+    in_specs = [tok(early)] * 7 + [shares(early)] + [tok(late)] * 5 + [shares(late)]
+    in_specs += [fixed(SQUARES), fixed(SQUARES), table_spec]
+    out_shape, out_specs = [low, low], [tok(early), tok(late)]
+    scratch = [vm((block, width), BF16)] * 4 + [
+        vm((steps, block, width), F32), vm(SQUARES, F32), vm(SQUARES, F32), vm((TABLE, width), F32)]
+    if shards is not None:
+        ins += [dwin.reshape(WIN_BLOCKS), dwout.reshape(WOUT_BLOCKS), dtable]
+        in_specs += [ANYWHERE, ANYWHERE, table_spec]
+        every = (WIN_BLOCKS, WOUT_BLOCKS, SQUARES, SQUARES, SMALL_BLOCKS)
+        out_shape += [shape_of(4, s[0], s[5], s[6]) for s in every]
+        out_specs += [ANYWHERE] * 5
+        scratch += [vm(SQUARES, BF16), vm(SQUARES, BF16), vm(SMALL_BLOCKS, BF16)]
+        scratch += [vm(s[:4] + s[5:], BF16) for s in every[:2]]
+        cut = ((0, 2, 1), (0, 1, 2), (2, 1, 1), (2, 1, 1), (0, 1, 2))
+        for s, (m, r, l) in zip(every, cut):
+            mats = s[0] // max(m, 1)
+            scratch += [
+                vm(s[:4] + s[5:], BF16), vm(s[:4] + s[5:], BF16),
+                vm((2, mats, 4, s[5] // r, s[6] // l), BF16), vm((2, s[0], 4, s[5], s[6]), BF16)]
+        slots_all = 5 * SCATTER_SLOTS
+        scratch += [dma((slots_all,)), dma((slots_all,)), dma((slots_all,))]
+    else:
+        out_shape += [shape_of(*SQUARES), shape_of(*SQUARES), table_shape]
+        out_specs += [fixed(SQUARES), fixed(SQUARES), table_spec]
+    grad_remote, grad_source, *tail = pl.pallas_call(
+        functools.partial(last_kernel, shards is not None, steps),
+        grid=(2 * steps,), in_specs=in_specs, out_specs=out_specs, out_shape=out_shape, scratch_shapes=scratch,
+        compiler_params=params(63 << 20, None if shards is None else 2), name="last",
+    )(*ins)
     as_rows = lambda array: array.reshape(rows, slots, width)
-    return as_rows(result), as_rows(grad_source), as_rows(grad_remote), dself, dcross, dwin, dwout, dtable + dtable_self
-
-
-def segment_ids(lengths, slot_count):
-    places = jnp.arange(slot_count, dtype=jnp.int32)
-    finish = jnp.cumsum(lengths, axis=-1)
-    return jnp.sum((finish[:, None, :] <= places[None, :, None]).astype(jnp.int32), axis=-1)
+    if shards is None:
+        dself, dcross, dtable_last = tail
+        grads = (dself.reshape(4, 512, 512), dcross.reshape(4, 512, 512), dwin, dwout, dtable + dtable_last)
+    else:
+        f = lambda *shape: shape_of(*shape, dtype=F32)
+        grads = pl.pallas_call(
+            sum_kernel,
+            out_shape=[f(3, 16, 512), f(3, 16), f(16, 512), f(2, 16), f(16, 512), f(2, 16, 512), f(3, 16), f(16, 512),
+                       f(2, 16), f(64, 512), f(4, 16), f(16, 2048), f(1, 16), f(2, 16)],
+            compiler_params=pltpu.CompilerParams(vmem_limit_bytes=16 << 20), name="sum_planes",
+        )(*tail)
+    return as_rows(result), as_rows(grad_source), as_rows(grad_remote), grads
 
 
 def turn(array):
@@ -488,16 +1034,37 @@
             small[8:10], ffn_in, small[13:].reshape(-1), ffn_out, small[10], small[11:13])
 
 
-def on_device(count, decoder_in, memory, out_grad, tgt_len, src_len, *parts):
-    slots = decoder_in.shape[1]
-    ids = jnp.stack([segment_ids(tgt_len, slots), segment_ids(src_len, slots)], axis=1).astype(F32)
-    weights = gather_plain(parts, count)
-    result, grad_source, grad_remote, *grads = layer(decoder_in, memory, out_grad, ids, *weights)
-    return (result, grad_source, grad_remote, *scatter_plain(*grads, count))
+def small_block(parts):
+    (_, self_bias, _, self_norm, _, _, cross_bias, _, cross_norm, _, ffn_in_bias, _, ffn_out_bias, ffn_norm) = parts
+    cols = ffn_out_bias.shape[0]
+    first = jnp.concatenate(
+        [self_bias, self_norm, cross_bias, cross_norm, ffn_out_bias[None], ffn_norm,
+         jnp.zeros((128 - 13, cols), BF16), ffn_in_bias.reshape(-1, cols)], axis=0)
+    return turn(jnp.pad(first, ((0, 256 - first.shape[0]), (0, 0))))
+
+
+def on_device(count, direct, decoder_in, memory, out_grad, tgt_len, src_len, *parts):
+    if not direct:
+        weights = gather_plain(parts, count)
+        result, grad_source, grad_remote, grads = layer(
+            decoder_in, memory, out_grad, tgt_len, src_len, weights=weights)
+        return (result, grad_source, grad_remote, *scatter_plain(*grads, count))
+    (self_qkv, _, self_out, _, cross_q, cross_kv, _, cross_out, _, ffn_in, _, ffn_out, _, _) = parts
+    shards = [turn(part) for part in (self_qkv, self_out, cross_q, cross_kv, cross_out, ffn_in, ffn_out)]
+    shards.append(small_block(parts))
+    shards = [part.reshape((-1,) + part.shape[-2:]) for part in shards]
+    result, grad_source, grad_remote, grads = layer(
+        decoder_in, memory, out_grad, tgt_len, src_len, shards=shards)
+    (qkv, bias_one, out_one, norm_one, query, pair, bias_two, out_two, norm_two, win, win_bias, wout, wout_bias,
+     norm_three) = grads
+    return (result, grad_source, grad_remote, turn(qkv), bias_one, turn(out_one), norm_one, turn(query), turn(pair),
+            bias_two, turn(out_two), norm_two, turn(win), win_bias.reshape(-1), turn(wout), wout_bias.reshape(-1),
+            norm_three)
 
 
 def solution(mesh):
     count = mesh.shape["dp"] * mesh.shape["fsdp"]
+    direct = mesh.shape["dp"] == 4 and mesh.shape["fsdp"] == 8
     rows = P(AXES, None, None)
     lens = P(AXES, None)
     cube = P(None, None, AXES)
@@ -505,7 +1072,7 @@
     line = P(AXES)
     params_in = (cube, flat, flat, flat, flat, cube, flat, flat, flat, flat, line, flat, line, flat)
     return jax.shard_map(
-        functools.partial(on_device, count),
+        functools.partial(on_device, count, direct),
         mesh=mesh,
         in_specs=(rows, rows, rows, lens, lens) + params_in,
         out_specs=(rows, rows, rows) + params_in,

time: 451 us -> 229 us (0.51)
  waiting for transfers between devices: 228 us -> 0 us
  Pallas kernels: 147 us -> 212 us
  local copies, waits for them, and re-layouts: 46.6 us -> 15.7 us
  between operations: 14.3 us -> 0.7 us
  other arithmetic: 12.9 us -> 0 us
    reduce_scatter x1 -> x0, waiting for transfers between devices: 149 us -> none  [scatter_plain(): lax.psum_scatter(packed, AXES, scatter_dimension=0, tiled=False).astype(F32)]
    all_gather x1 -> x0, waiting for transfers between devices: 79.7 us -> none  [gather_plain(): whole_set = lax.all_gather(packed, AXES, axis=0, tiled=False)]
    pallas_call x3 -> x4, Pallas kernels: 147 us -> 212 us  [the longest x1 86 us: layer(): pl.pallas_call(functools.partial(last_kernel, shards is not None, steps),...]
    slice x17 -> x0, local copies, waits for them, and re-layouts: 17.4 us -> none  [the longest x1 4.63 us: gather_plain(): whole_set[:, :8 * cols].reshape(count, 8, cols, width).swapaxes(0, 1)]
    reshape x12 -> x4, local copies, waits for them, and re-layouts: 10.2 us -> 2.04 us  [the longest x2 0.84 us: small_block(): ffn_in_bias.reshape(-1, cols)]
    concatenate x3 -> x0, other arithmetic: 7.79 us -> none  [the longest x1 5.7 us: scatter_plain(): jnp.concatenate([squares.reshape(count, 8 * cols, width), dwin.reshape(co...]
    unnamed x24 -> x19, local copies, waits for them, and re-layouts: 12.9 us -> 12.8 us
  transfers between devices with their start and end apart: 2 -> 0, of which waited for: 2 -> 0; matrix products, arithmetic and copies ran while one was open for 1% -> 0% of each run, Pallas kernels for 0% -> 0%
where the time goes in v2:
time: 229 us
  Pallas kernels  212 us (93%)
  local copies, waits for them, and re-layouts  15.7 us (7%)
    pallas_call x1, Pallas kernels, layer(): pl.pallas_call(functools.partial(last_kernel, shards is not None, steps),...  86 us
    pallas_call x1, Pallas kernels, layer(): pl.pallas_call(functools.partial(first_kernel, shards is not None, steps)...  69.4 us
    pallas_call x1, Pallas kernels, layer(): pl.pallas_call(ffn_kernel, grid=(steps,), in_specs=[tok(now), tok(now), f...  56 us
    unnamed x19, local copies, waits for them, and re-layouts  12.8 us

profile of v2, /device:TPU:0, one launch (start us, length us, event | category | flops | bytes accessed | tf_op | source)
XLA Modules:
  0.0 228.6 jit_solution(15136584990250034271)
XLA Ops:
  0.7 0.7 reshape.98
  1.4 0.1 copy.42
  1.5 0.8 copy.36
  2.3 0.7 copy.37
  3.0 0.8 copy.38
  3.8 0.7 copy.39
  4.5 0.7 copy.40
  5.3 0.7 copy.41
  6.0 0.1 concatenate.3
  6.1 0.6 pad_bitcast_fusion.refs_11_
  6.7 69.4 %first.1 = (bf16[2048,512]{1,0:T(8,128)(2,1)}, bf16[2048,512]{1,0:T(8,128)(2,1)}, bf16[2048,512]{1,0:T(8,128)(2,1)}, bf16[64,256,256]{2,1,0:T(8,128)(2,1)}, bf16...) custom-call(bf16[2048,512]{1,0:T(8,128)(2,1)} %bitcast.40, ...), custom_call_target="tpu_custom_call" | custom-call | tf_op jit(solution)/shard_map/first/pallas_call | solution.py:902
  76.1 56.0 %feed_forward.1 = (bf16[2048,512]{1,0:T(8,128)(2,1)}, f32[2048,512]{1,0:T(8,128)}, bf16[2048,512]{1,0:T(8,128)(2,1)}, bf16[512,2048]{1,0:T(8,128)(2,1)}, f32[24,512]{1,0:T(8,128)}) custom-call(f32[2048,512]{1,0:T(8,128)} %get-tuple-element.60.summed_two_ref, bf16[2048,512]{1,0:T(8,128)(2,1)} %bitcast.44, bf16[2048,512]{1,0:T(8,128)(2,1)} %bitcast.47, ...), custom_call_target="tpu_custom_call" | custom-call | tf_op jit(solution)/shard_map/feed_forward/pallas_call | solution.py:914
  132.1 86.0 %last.1 = (bf16[2048,512]{1,0:T(8,128)(2,1)}, bf16[2048,512]{1,0:T(8,128)(2,1)}, bf16[4,1,64,512]{3,2,1,0:T(8,128)(2,1)}, bf16[4,1,16,2048]{3,2,1,0:T(8,128)(2,1...) custom-call(f32[2048,512]{1,0:T(8,128)} %get-tuple-element.65.refs_0_, ...), custom_call_target="tpu_custom_call" | custom-call | tf_op jit(solution)/shard_map/last/pallas_call | solution.py:953
  218.1 0.0 copy-start
  218.1 0.9 copy-done
  219.1 0.0 copy-start.1
  219.1 0.9 copy-done.1
  220.0 0.0 copy-start.2
  220.0 0.9 copy-done.2
  221.0 0.0 copy-start.3
  221.0 0.9 copy-done.3
  221.9 0.0 copy-start.4
  221.9 0.8 copy-done.4
  222.7 0.8 sum_planes.1
  223.5 0.6 reshape.108
  224.1 0.0 copy-start.5
  224.1 3.2 %copy.45 = bf16[8,256,512]{2,1,0:T(8,128)(2,1)} copy(bf16[8,256,512]{2,1,0:T(8,128)(2,1)} %bitcast.50) | data formatting | bytes 4194304
  227.3 0.0 copy-done.5
  227.3 1.3 copy.46
  (1 shorter events, 0.0 us)
Async XLA Ops:
  218.1 1.0 copy-start
  219.1 0.9 copy-start.1
  220.0 0.9 copy-start.2
  221.0 0.9 copy-start.3
  221.9 0.8 copy-start.4
  224.1 3.2 %copy-start.5 = (bf16[2048,512]{1,0:T(8,128)(2,1)S(1)}, bf16[2048,512]{1,0:T(8,128)(2,1)}, u32[]{:S(2)}) copy-start(bf16[2048,512]{1,0:T(8,128)(2,1)} %get-tuple-element.83) | copy-start | bytes 6291460

commit v3 on v2

--- a/solution.py
+++ b/solution.py
@@ -74,7 +74,7 @@
     return jnp.where(allowed, 0.0, MASKED).astype(F32)
 
 
-def attend_rows(query_ref, keys_ref, values_ref, bias_ref, shares_ref, mixture_ref, row, at):
+def attend_rows(query_ref, keys_ref, values_ref, bias_ref, shares_ref, mixture_ref, row, at, into):
     for quad in range(HEADS * HEAD_DIM // QUAD):
         lanes = slice(quad * QUAD, (quad + 1) * QUAD)
         values_quad = values_ref[at, lanes]
@@ -93,11 +93,11 @@
             parts.append(shares)
             wide.append(keep_head(values_quad, inner))
         mixture = mm_tn(jnp.concatenate(parts, 0), jnp.concatenate(wide, 0))
-        mixture_ref[at, lanes] = mixture.astype(BF16)
+        mixture_ref[into, lanes] = mixture.astype(BF16)
 
 
 def attend_rows_back(
-    upstream_ref, query_ref, keys_ref, values_ref, shares_ref, gq_ref, gk_ref, gv_ref, row, at
+    upstream_ref, query_ref, keys_ref, values_ref, shares_ref, gq_ref, gk_ref, gv_ref, row, at, into
 ):
     for quad in range(HEADS * HEAD_DIM // QUAD):
         lanes = slice(quad * QUAD, (quad + 1) * QUAD)
@@ -122,9 +122,9 @@
             grad_keys = one if grad_keys is None else grad_keys + one
             grad_values = two if grad_values is None else grad_values + two
             grad_query = three if grad_query is None else grad_query + three
-        gq_ref[at, lanes] = (grad_query * HEAD_DIM**-0.5).astype(BF16)
-        gk_ref[at, lanes] = grad_keys.astype(BF16)
-        gv_ref[at, lanes] = grad_values.astype(BF16)
+        gq_ref[into, lanes] = (grad_query * HEAD_DIM**-0.5).astype(BF16)
+        gk_ref[into, lanes] = grad_keys.astype(BF16)
+        gv_ref[into, lanes] = grad_values.astype(BF16)
 
 
 STEP_ROWS = 2
@@ -157,14 +157,20 @@
     return (z, y * 4 + x * 2 + core)
 
 
-def greet():
+def partners():
     z, y, x, core = place()
-    partners = [device(lax.rem(z + step, 4), y, x, core) for step in (1, 2, 3)]
-    partners += [device(z, y, 1 - x, core), device(z, 1 - y, x, core), device(z, y, x, 1 - core)]
+    found = [device(lax.rem(z + step, 4), y, x, core) for step in (1, 2, 3)]
+    return found + [device(z, y, 1 - x, core), device(z, 1 - y, x, core), device(z, y, x, 1 - core)]
+
+
+def hail():
     barrier = pltpu.get_barrier_semaphore()
-    for partner in partners:
+    for partner in partners():
         pl.semaphore_signal(barrier, inc=1, device_id=partner, device_id_type=MESH)
-    pl.semaphore_wait(barrier, len(partners))
+
+
+def await_hails():
+    pl.semaphore_wait(pltpu.get_barrier_semaphore(), 6)
 
 
 class Gather:
@@ -241,14 +247,18 @@
     qkv, out_one, cross_q, cross_kv, out_two, win, wout, small = shards
     ws, wc, win_all, wout_all, small_all = targets
     one = lambda n: slice(n, n + 1)
+    lanes = lambda n: ((ALL, ALL, slice(0, n)), (ALL, ALL, slice(n, 2 * n)))
+    single = lambda n: ((one(n), ALL, slice(0, 256)), (one(n), ALL, slice(256, 512)))
     plans = [
-        (ws, [(qkv.at[0:2], slice(0, 2))], (one(0), ALL, ALL), (one(1), ALL, ALL)),
-        (ws, [(qkv.at[2:3], one(2)), (out_one, one(3))], (one(2), ALL, ALL), (one(3), ALL, ALL)),
-        (small_all, [(small, one(0))], (ALL, ALL, slice(0, 128)), (ALL, ALL, slice(128, 256))),
+        (small_all, [(small, one(0))], *lanes(128)),
+        (ws, [(qkv.at[0:1], one(0))], *single(0)),
+        (ws, [(qkv.at[1:2], one(1))], *single(1)),
+        (ws, [(qkv.at[2:3], one(2))], *single(2)),
+        (ws, [(out_one, one(3))], *single(3)),
         (wc, [(cross_q, one(0)), (cross_kv, slice(1, 3)), (out_two, one(3))],
          (slice(0, 2), ALL, ALL), (slice(2, 4), ALL, ALL)),
         (win_all, [(win, one(0))], (ALL, slice(0, 32), ALL), (ALL, slice(32, 64), ALL)),
-        (wout_all, [(wout, one(0))], (ALL, ALL, slice(0, 1024)), (ALL, ALL, slice(1024, 2048))),
+        (wout_all, [(wout, one(0))], *lanes(1024)),
     ]
     pieces, base = [], 0
     for ref, own, first, second in plans:
@@ -257,7 +267,7 @@
     return pieces
 
 
-GATHER_SLOTS = 64
+GATHER_SLOTS = 80
 
 BLOCKS = (4, 2, 2, 2)
 
@@ -266,7 +276,7 @@
     return ref[index].reshape(512, 512)
 
 
-def prepare_ids(tgt_ref, src_ref, ids_ref):
+def prepare_masks(tgt_ref, src_ref, ids_ref, bias_ref):
     rows, sents = tgt_ref.shape
     slots = ids_ref.shape[2]
     before = lax.broadcasted_iota(jnp.int32, (sents, sents), 0)
@@ -282,36 +292,41 @@
             ended = (finish[:, row : row + 1] <= slot).astype(F32)
             ids_ref[row, side : side + 1, :] = jnp.sum(ended, axis=0, keepdims=True)
 
+    def one_row(row, carry):
+        ids = ids_ref[row]
+        bias_ref[0, row] = mask_bias(ids[0:1], ids[0:1], True)
+        bias_ref[1, row] = mask_bias(ids[1:2], ids[0:1], False)
+        return carry
+
+    lax.fori_loop(0, rows, one_row, 0)
+
+
+def tokens_of(block, size):
+    start = block * size
+    return pl.ds(start if isinstance(start, int) else pl.multiple_of(start, size), size)
+
 
 def self_forward(
-    step, source_ref, ids_ref, weight_ref, table_ref,
-    query_ref, keys_ref, values_ref, shares_ref, mixture_ref, summed_ref, bias_ref,
+    step, source_ref, weight_ref, table_ref, query_ref, keys_ref, values_ref,
+    shares_ref, mixture_ref, summed_ref, bias_ref,
 ):
-    slots = ids_ref.shape[2]
-    source = source_ref[...]
-    query = mm_nt(source, square(weight_ref, 0)) + vrow(table_ref, SELF_BQ)
-    query_ref[...] = (query * HEAD_DIM**-0.5).astype(BF16)
-    keys_ref[...] = mm_nt(source, square(weight_ref, 1)).astype(BF16)
-    values_ref[...] = (mm_nt(source, square(weight_ref, 2)) + vrow(table_ref, SELF_BV)).astype(BF16)
-
-    def one_row(row, carry):
-        at = pl.ds(pl.multiple_of(row * slots, slots), slots)
-        ids = ids_ref[step * STEP_ROWS + row]
-        bias_ref[...] = mask_bias(ids[0:1], ids[0:1], True)
-        attend_rows(query_ref, keys_ref, values_ref, bias_ref, shares_ref, mixture_ref, row, at)
-        return carry
-
-    lax.fori_loop(0, STEP_ROWS, one_row, 0)
+    slots = shares_ref.shape[1]
+    block = STEP_ROWS * slots
+    for row in range(STEP_ROWS):
+        attend_rows(
+            query_ref, keys_ref, values_ref, bias_ref.at[0, step * STEP_ROWS + row], shares_ref, mixture_ref, row,
+            tokens_of(step * STEP_ROWS + row, slots), tokens_of(row, slots))
     summed_ref[...] = (
-        source.astype(F32) + mm_nt(mixture_ref[...], square(weight_ref, 3)) + vrow(table_ref, SELF_BO)
+        source_ref[tokens_of(step, block), :].astype(F32)
+        + mm_nt(mixture_ref[...], square(weight_ref, 3)) + vrow(table_ref, SELF_BO)
     )
 
 
 def cross_forward(
-    step, summed_one_ref, remote_ref, ids_ref, weight_ref, table_ref,
+    step, summed_one_ref, remote_ref, weight_ref, table_ref,
     query_ref, keys_ref, values_ref, shares_ref, mixture_ref, summed_ref, bias_ref, hidden_ref,
 ):
-    slots = ids_ref.shape[2]
+    slots = shares_ref.shape[1]
     normed_one, _ = norm_stats(summed_one_ref[...])
     hidden_one = normed_one * vrow(table_ref, SELF_G) + vrow(table_ref, SELF_S)
     hidden_ref[...] = hidden_one
@@ -321,14 +336,10 @@
     keys_ref[...] = mm_nt(remote, square(weight_ref, 1)).astype(BF16)
     values_ref[...] = (mm_nt(remote, square(weight_ref, 2)) + vrow(table_ref, CROSS_BV)).astype(BF16)
 
-    def one_row(row, carry):
-        at = pl.ds(pl.multiple_of(row * slots, slots), slots)
-        ids = ids_ref[step * STEP_ROWS + row]
-        bias_ref[...] = mask_bias(ids[1:2], ids[0:1], False)
-        attend_rows(query_ref, keys_ref, values_ref, bias_ref, shares_ref, mixture_ref, row, at)
-        return carry
-
-    lax.fori_loop(0, STEP_ROWS, one_row, 0)
+    for row in range(STEP_ROWS):
+        at = tokens_of(row, slots)
+        attend_rows(
+            query_ref, keys_ref, values_ref, bias_ref.at[1, step * STEP_ROWS + row], shares_ref, mixture_ref, row, at, at)
     summed_ref[...] = (
         hidden_ref[...] + mm_nt(mixture_ref[...], square(weight_ref, 3)) + vrow(table_ref, CROSS_BO)
     )
@@ -356,118 +367,188 @@
     return jnp.concatenate([columns, second], axis=1)
 
 
-FIRST_OUT = 12
+def small_columns(parts, lines_ref, small_ref):
+    lines_ref[...] = jnp.zeros_like(lines_ref)
+    at = 0
+    for part in parts[:-1]:
+        lines_ref[at : at + part.shape[0], 0:16] = part[...].astype(F32)
+        at += part.shape[0]
+    line = parts[-1][...].astype(F32)
+    for k in range(4):
+        lines_ref[128 + k : 129 + k, 0:16] = line[:, k * 16 : k * 16 + 16]
+    small_ref[0, :, 0:128] = jnp.transpose(lines_ref[0:128, :])[0:16].astype(BF16)
+    small_ref[0, :, 128:256] = jnp.transpose(lines_ref[128:256, :])[0:16].astype(BF16)
+
+
+FIRST_OUT = 11
 
 
 def first_kernel(gathers, steps, *refs):
     step = pl.program_id(0)
+    (source_ref, remote_ref, tgt_ref, src_ref), refs = refs[:4], refs[4:]
     if gathers:
-        (source_ref, remote_ref, tgt_ref, src_ref), shards, refs = refs[:4], refs[4:12], refs[12:]
+        shards, smalls, refs = refs[:7], refs[7:14], refs[14:]
     else:
-        (source_ref, remote_ref, tgt_ref, src_ref, ws_ref, wc_ref, table_ref), refs = refs[:7], refs[7:]
-    (q1_ref, k1_ref, v1_ref, p1_ref, m1_ref, s1_ref,
-     q2_ref, k2_ref, v2_ref, p2_ref, m2_ref, s2_ref), refs = refs[:FIRST_OUT], refs[FIRST_OUT:]
+        (ws_ref, wc_ref, table_ref), refs = refs[:3], refs[3:]
+    (q1_out, k1_out, v1_out, m1_ref, s1_ref, q2_ref, k2_ref, v2_ref, m2_ref, s2_ref, shares_ref), refs = (
+        refs[:FIRST_OUT], refs[FIRST_OUT:])
     if gathers:
         (table_ref, ws_out, wc_out, win_out, wout_out), refs = refs[:5], refs[5:]
-        (ws_ref, wc_ref, small_ref, *sems, out_sem), refs = refs[:7], refs[7:]
-        pieces = gather_pieces(shards, (ws_ref, wc_ref, win_out, wout_out, small_ref), sems)
-        one, two, small, cross, inner, outer = pieces
-        saves = [pltpu.make_async_copy(ws_ref, ws_out, out_sem.at[0]), pltpu.make_async_copy(wc_ref, wc_out, out_sem.at[1])]
-    bias_ref, hidden_ref, keep_ref, ids_ref = refs
+        (ws_ref, wc_ref, small_ref, own_ref, lines_ref, *sems), refs = refs[:8], refs[8:]
+        pieces = gather_pieces((*shards, own_ref), (ws_ref, wc_ref, win_out, wout_out, small_ref), sems)
+        small, query, keys, values, mixed, cross, inner, outer = pieces
+        head = (small, query, keys, values, mixed)
+    bias_ref, hidden_ref, keep_ref, ids_ref, q1_ref, k1_ref, v1_ref, out_sem = refs
+    saves = [
+        pltpu.make_async_copy(ref, out, out_sem.at[i])
+        for i, (ref, out) in enumerate(((q1_ref, q1_out), (k1_ref, k1_out), (v1_ref, v1_out)))
+    ]
+    if gathers:
+        saves.append(pltpu.make_async_copy(ws_ref, ws_out, out_sem.at[3]))
+        late_save = pltpu.make_async_copy(wc_ref, wc_out, out_sem.at[4])
+    tokens = source_ref.shape[0]
+
+    def project(index, out_ref, row, factor):
+        for part in range(4):
+            at = tokens_of(part, tokens // 4)
+            found = mm_nt(source_ref[at, :], square(ws_ref, index))
+            if row is not None:
+                found = found + vrow(table_ref, row)
+            if factor is not None:
+                found = found * factor
+            out_ref[at, :] = found.astype(BF16)
+
+    def project_query():
+        project(0, q1_ref, SELF_BQ, HEAD_DIM**-0.5)
+
+    def project_keys():
+        project(1, k1_ref, None, None)
+
+    def project_values():
+        project(2, v1_ref, SELF_BV, None)
 
     @pl.when(step == 0)
     def _():
-        if gathers:
-            greet()
-            head = (one, two, small)
+        if not gathers:
+            prepare_masks(tgt_ref, src_ref, ids_ref, bias_ref)
+            project_query()
+            project_keys()
+            project_values()
+        else:
+            hail()
+            small_columns(smalls, lines_ref, own_ref)
             for piece in pieces:
                 for copy in piece.locals():
                     copy.start()
+            await_hails()
             for piece in head:
                 piece.start(0)
-        prepare_ids(tgt_ref, src_ref, ids_ref)
-        if gathers:
-            for piece in pieces:
+            prepare_masks(tgt_ref, src_ref, ids_ref, bias_ref)
+            for piece in head:
                 for copy in piece.locals():
                     copy.wait()
-            for piece in head:
-                piece.arrive(0)
-                piece.start(1)
+
+            def move(piece, stage):
+                piece.arrive(stage)
+                if stage < 3:
+                    piece.start(stage + 1)
+
+            move(small, 0)
+            move(query, 0)
+            move(keys, 0)
+            move(small, 1)
+            move(query, 1)
+            move(values, 0)
+            move(keys, 1)
+            move(small, 2)
+            move(query, 2)
+            move(mixed, 0)
             cross.start(0)
+            move(values, 1)
+            move(keys, 2)
+            move(small, 3)
+            table_from_columns(small_ref[0].reshape(512, 256).astype(F32), table_ref)
+            move(mixed, 1)
+            move(query, 3)
+            project_query()
+            move(values, 2)
             inner.start(0)
-            for piece in head:
-                piece.arrive(1)
-                piece.start(2)
+            move(keys, 3)
+            project_keys()
+            move(mixed, 2)
+            for piece in (cross, inner, outer):
+                for copy in piece.locals():
+                    copy.wait()
             cross.arrive(0)
             cross.start(1)
-            for piece in head:
-                piece.arrive(2)
-                piece.start(3)
-            for piece in head:
-                piece.arrive(3)
-            table_from_columns(small_ref[0].reshape(512, 256).astype(F32), table_ref)
-            saves[0].start()
-
-    @pl.when(step < steps)
+            outer.start(0)
+            move(values, 3)
+            project_values()
+            move(mixed, 3)
+        for copy in saves:
+            copy.start()
+
+    @pl.when((step >= 1) & (step <= steps))
     def _():
         self_forward(
-            step, source_ref, ids_ref, ws_ref, table_ref,
-            q1_ref, k1_ref, v1_ref, p1_ref, m1_ref, s1_ref, bias_ref)
-        keep_ref[step] = s1_ref[...]
-
-    @pl.when(step >= steps)
-    def _():
-        at = step - steps
+            step - 1, source_ref, ws_ref, table_ref, q1_ref, k1_ref, v1_ref,
+            shares_ref, m1_ref, s1_ref, bias_ref)
+        keep_ref[step - 1] = s1_ref[...]
+
+    @pl.when(step > steps)
+    def _():
+        at = step - steps - 1
         cross_forward(
-            at, keep_ref.at[at], remote_ref, ids_ref, wc_ref, table_ref,
-            q2_ref, k2_ref, v2_ref, p2_ref, m2_ref, s2_ref, bias_ref, hidden_ref)
+            at, keep_ref.at[at], remote_ref, wc_ref, table_ref,
+            q2_ref, k2_ref, v2_ref, shares_ref, m2_ref, s2_ref, bias_ref, hidden_ref)
 
     if gathers:
-        @pl.when(step == 0)
+        @pl.when(step == 1)
         def _():
             cross.arrive(1)
             cross.start(2)
             inner.arrive(0)
             inner.start(1)
-            outer.start(0)
-
-        @pl.when(step == 1)
+
+        @pl.when(step == steps - 1)
         def _():
             cross.arrive(2)
             cross.start(3)
-
-        @pl.when(step == 2)
+            outer.arrive(0)
+            outer.start(1)
+
+        @pl.when(step == steps)
+        def _():
+            cross.arrive(3)
+            late_save.start()
+
+        @pl.when(step == steps + 1)
         def _():
             inner.arrive(1)
             inner.start(2)
-            outer.arrive(0)
-            outer.start(1)
-
-        @pl.when(step == steps - 1)
+
+        @pl.when(step == steps + 2)
         def _():
-            cross.arrive(3)
-            saves[1].start()
-
-        @pl.when(step == steps)
-        def _():
+            outer.arrive(1)
+            outer.start(2)
             inner.arrive(2)
             inner.start(3)
-            outer.arrive(1)
-            outer.start(2)
-
-        @pl.when(step == 2 * steps - 2)
+
+        @pl.when(step == 2 * steps - 1)
         def _():
             outer.arrive(2)
             outer.start(3)
 
-        @pl.when(step == 2 * steps - 1)
-        def _():
+    @pl.when(step == 2 * steps)
+    def _():
+        if gathers:
             inner.arrive(3)
             outer.arrive(3)
             for piece in pieces:
                 piece.finish()
-            for copy in saves:
-                copy.wait()
+            late_save.wait()
+        for copy in saves:
+            copy.wait()
 
 
 def ffn_kernel(
@@ -492,24 +573,29 @@
     low_two_ref[...] = hidden_two.astype(BF16)
     accum_ref[...] = jnp.zeros_like(accum_ref)
 
-    def ffn_chunk(chunk, carry):
-        units = pl.ds(pl.multiple_of(chunk * 512, 512), 512)
-        expanded = mm_nt(low_two_ref[...], win_ref[units, :]) + table_ref[pl.ds(FFN_BI + chunk, 1), :]
+    def expand(chunk):
+        units = slice(chunk * 512, chunk * 512 + 512)
+        return mm_nt(low_two_ref[...], win_ref[units, :]) + table_ref[FFN_BI + chunk : FFN_BI + chunk + 1, :]
+
+    def bend(chunk, expanded):
+        units = slice(chunk * 512, chunk * 512 + 512)
         square = expanded * expanded
-        inner = expanded * (GELU_A + (GELU_A * GELU_B) * square)
-        bent = jnp.tanh(inner)
+        bent = jnp.tanh(expanded * (GELU_A + (GELU_A * GELU_B) * square))
         half = 0.5 * bent + 0.5
-        active_ref[:, units] = (expanded * half).astype(BF16)
-        slope = half + (0.5 * expanded) * (1.0 - bent * bent) * (
-            GELU_A + (3.0 * GELU_A * GELU_B) * square
-        )
+        active = expanded * half
+        active_ref[:, units] = active.astype(BF16)
+        slope = half + (active * (1.0 - half)) * (2.0 * GELU_A + (6.0 * GELU_A * GELU_B) * square)
         slope_ref[:, units] = slope.astype(BF16)
-        accum_ref[...] += mm_nt(active_ref[:, units], wout_ref[:, units])
-        return carry
-
-    lax.fori_loop(0, chunks, ffn_chunk, 0)
+
+    ahead = expand(0)
+    for chunk in range(chunks):
+        expanded = ahead
+        if chunk + 1 < chunks:
+            ahead = expand(chunk + 1)
+        bend(chunk, expanded)
+    contracted = mm_nt(active_ref[...], wout_ref[...])
     normed_three, inverse_three = norm_stats(
-        hidden_ref[...] + accum_ref[...] + vrow(table_ref, FFN_BO)
+        hidden_ref[...] + contracted + vrow(table_ref, FFN_BO)
     )
     result = normed_three * vrow(table_ref, FFN_G) + vrow(table_ref, FFN_S)
     result_ref[...] = result.astype(BF16)
@@ -522,18 +608,16 @@
     add_row(acct_ref, FFN_BO, column_sum(grad_low_ref[...]))
     accum_ref[...] = sum_three
 
-    def ffn_chunk_back(chunk, carry):
-        units = pl.ds(pl.multiple_of(chunk * 512, 512), 512)
-        grad_three = grad_low_ref[...]
+    grad_three = grad_low_ref[...]
+    for chunk in range(chunks):
+        units = slice(chunk * 512, chunk * 512 + 512)
+        grad_active = mm_nn(grad_three, wout_ref[:, units])
         accout_ref[:, units] += mm_tn(grad_three, active_ref[:, units])
-        grad_active = mm_nn(grad_three, wout_ref[:, units])
         grad_expanded = (grad_active * slope_ref[:, units].astype(F32)).astype(BF16)
-        acct_ref[pl.ds(FFN_BI + chunk, 1), :] += column_sum(grad_expanded)
+        slope_ref[:, units] = grad_expanded
+        acct_ref[FFN_BI + chunk : FFN_BI + chunk + 1, :] += column_sum(grad_expanded)
         accin_ref[units, :] += mm_tn(grad_expanded, low_two_ref[...])
-        accum_ref[...] += mm_nn(grad_expanded, win_ref[units, :])
-        return carry
-
-    lax.fori_loop(0, chunks, ffn_chunk_back, 0)
+    accum_ref[...] += mm_nn(slope_ref[...], win_ref[...])
     grad_hidden_two = accum_ref[...]
     normed_two = normed_two_ref[...]
     add_row(acct_ref, CROSS_G, column_sum(grad_hidden_two * normed_two))
@@ -548,74 +632,60 @@
 
 
 def cross_backward(
-    sum_two_ref, summed_one_ref, remote_ref, mixture_ref, query_ref, keys_ref, values_ref, shares_ref,
-    weight_ref, table_ref, grad_remote_ref, sum_one_ref, up_ref, gq_ref, gk_ref, gv_ref, acc_ref, acct_ref,
+    step, sum_two_ref, summed_one_ref, remote_ref, mixture_ref, query_ref, keys_ref, values_ref, shares_ref,
+    weight_ref, table_ref, first_mixture_ref, sum_one_ref, up_ref, gq_ref, gk_ref, gv_ref,
+    acc_ref, acc_out_ref, acct_ref,
 ):
     slots = shares_ref.shape[1]
+    block = tokens_of(step, STEP_ROWS * slots)
     grad_two = sum_two_ref[...].astype(BF16)
     add_row(acct_ref, CROSS_BO, column_sum(grad_two))
+    up_ref[...] = mm_nn(grad_two, square(weight_ref, 3)).astype(BF16)
     acc_ref[3] += mm_tn(grad_two, mixture_ref[...])
-    up_ref[...] = mm_nn(grad_two, square(weight_ref, 3)).astype(BF16)
-
-    def one_row_back(row, carry):
-        at = pl.ds(pl.multiple_of(row * slots, slots), slots)
+    def one_row(row, carry):
         attend_rows_back(
-            up_ref, query_ref, keys_ref, values_ref, shares_ref, gq_ref, gk_ref, gv_ref, row, at)
+            up_ref, query_ref, keys_ref, values_ref, shares_ref, gq_ref, gk_ref, gv_ref, row,
+            tokens_of(row, slots), tokens_of(step * STEP_ROWS + row, slots))
         return carry
-
-    lax.fori_loop(0, STEP_ROWS, one_row_back, 0)
+    lax.fori_loop(0, STEP_ROWS, one_row, 0)
     normed_one, inverse_one = norm_stats(summed_one_ref[...])
     low = (normed_one * vrow(table_ref, SELF_G) + vrow(table_ref, SELF_S)).astype(BF16)
-    grad_query, grad_keys, grad_values = gq_ref[...], gk_ref[...], gv_ref[...]
+    grad_query, grad_keys, grad_values = gq_ref[block, :], gk_ref[block, :], gv_ref[block, :]
     add_row(acct_ref, CROSS_BQ, column_sum(grad_query))
     add_row(acct_ref, CROSS_BV, column_sum(grad_values))
+    grad_hidden_one = sum_two_ref[...] + mm_nn(grad_query, square(weight_ref, 0))
+    add_row(acct_ref, SELF_G, column_sum(grad_hidden_one * normed_one))
+    add_row(acct_ref, SELF_S, column_sum(grad_hidden_one))
+    sum_one = norm_back(grad_hidden_one, normed_one, inverse_one, vrow(table_ref, SELF_G))
+    sum_one_ref[...] = sum_one
     acc_ref[0] += mm_tn(grad_query, low)
     acc_ref[1] += mm_tn(grad_keys, remote_ref[...])
     acc_ref[2] += mm_tn(grad_values, remote_ref[...])
-    grad_remote_ref[...] = (
-        mm_nn(grad_keys, square(weight_ref, 1)) + mm_nn(grad_values, square(weight_ref, 2))
-    ).astype(BF16)
-    grad_hidden_one = sum_two_ref[...] + mm_nn(grad_query, square(weight_ref, 0))
-    add_row(acct_ref, SELF_G, column_sum(grad_hidden_one * normed_one))
-    add_row(acct_ref, SELF_S, column_sum(grad_hidden_one))
-    sum_one_ref[...] = norm_back(grad_hidden_one, normed_one, inverse_one, vrow(table_ref, SELF_G))
+    grad_one = sum_one.astype(BF16)
+    add_row(acct_ref, SELF_BO, column_sum(grad_one))
+    acc_out_ref[0] += mm_tn(grad_one, first_mixture_ref[...])
 
 
 def self_backward(
-    sum_one_ref, source_ref, mixture_ref, query_ref, keys_ref, values_ref, shares_ref, weight_ref,
-    grad_source_ref, up_ref, gq_ref, gk_ref, gv_ref, acc_ref, acct_ref,
+    step, sum_one_ref, query_ref, keys_ref, values_ref, shares_ref, weight_ref,
+    up_ref, gq_ref, gk_ref, gv_ref, acct_ref,
 ):
     slots = shares_ref.shape[1]
-    grad_one = sum_one_ref[...].astype(BF16)
-    add_row(acct_ref, SELF_BO, column_sum(grad_one))
-    acc_ref[3] += mm_tn(grad_one, mixture_ref[...])
-    up_ref[...] = mm_nn(grad_one, square(weight_ref, 3)).astype(BF16)
-
-    def one_row_back(row, carry):
-        at = pl.ds(pl.multiple_of(row * slots, slots), slots)
+    block = tokens_of(step, STEP_ROWS * slots)
+    up_ref[...] = mm_nn(sum_one_ref[...].astype(BF16), square(weight_ref, 3)).astype(BF16)
+    def one_row(row, carry):
         attend_rows_back(
-            up_ref, query_ref, keys_ref, values_ref, shares_ref, gq_ref, gk_ref, gv_ref, row, at)
+            up_ref, query_ref, keys_ref, values_ref, shares_ref, gq_ref, gk_ref, gv_ref, row,
+            tokens_of(row, slots), tokens_of(step * STEP_ROWS + row, slots))
         return carry
-
-    lax.fori_loop(0, STEP_ROWS, one_row_back, 0)
-    grad_query, grad_keys, grad_values = gq_ref[...], gk_ref[...], gv_ref[...]
-    add_row(acct_ref, SELF_BQ, column_sum(grad_query))
-    add_row(acct_ref, SELF_BV, column_sum(grad_values))
-    source = source_ref[...]
-    acc_ref[0] += mm_tn(grad_query, source)
-    acc_ref[1] += mm_tn(grad_keys, source)
-    acc_ref[2] += mm_tn(grad_values, source)
-    grad_source_ref[...] = (
-        sum_one_ref[...]
-        + mm_nn(grad_query, square(weight_ref, 0))
-        + mm_nn(grad_keys, square(weight_ref, 1))
-        + mm_nn(grad_values, square(weight_ref, 2))
-    ).astype(BF16)
+    lax.fori_loop(0, STEP_ROWS, one_row, 0)
+    add_row(acct_ref, SELF_BQ, column_sum(gq_ref[block, :]))
+    add_row(acct_ref, SELF_BV, column_sum(gv_ref[block, :]))
 
 
 class Scatter:
-    def __init__(self, full, mine, halves, bufs, units, sems, base):
-        self.full, self.mine, self.halves, self.units = full, mine, halves, units
+    def __init__(self, theirs, halves, bufs, units, sems, base):
+        self.theirs, self.halves, self.units = theirs, halves, units
         self.total, self.pair, self.far, self.near = bufs
         self.local, self.send, self.recv = sems
         self.base = base
@@ -629,7 +699,7 @@
     def hops(self, stage, incoming=False):
         z, y, x, core = place()
         if stage == 0:
-            return [self.copy(0, self.full.at[:, :, :, :, 1 - core], self.pair, device(z, y, x, 1 - core))]
+            return [self.copy(0, self.theirs, self.pair, device(z, y, x, 1 - core))]
         sides = ((y, 1 - x), (1 - y, x))
         if stage == 1:
             return [
@@ -651,6 +721,11 @@
         z, y, x, _ = place()
         return pltpu.make_async_copy(self.total.at[:, z, y, x], self.units.at[0], self.local.at[self.base])
 
+    def divide(self, mat, ref, index):
+        _, _, _, core = place()
+        self.theirs[mat] = ref[index, :, :, :, 1 - core].astype(BF16)
+        self.total[mat] = ref[index, :, :, :, core].astype(BF16)
+
     def start(self, stage):
         for hop in self.hops(stage):
             hop.start()
@@ -662,9 +737,8 @@
             hop.wait_recv()
         z, y, x, core = place()
         if stage == 0:
-            mats = self.total.shape[0]
-            for mat in range(mats):
-                self.total[mat] = (self.mine(mat, core) + self.pair[mat].astype(F32)).astype(BF16)
+            for mat in range(self.total.shape[0]):
+                self.total[mat] = (self.total[mat].astype(F32) + self.pair[mat].astype(F32)).astype(BF16)
         if stage == 1:
             for i, (h, at) in enumerate(zip(self.halves, ((1 - y, x), (y, 1 - x)))):
                 old = self.total[h[0], :, at[0], at[1], h[1], h[2]].astype(F32)
@@ -686,123 +760,188 @@
 
 def last_kernel(scatters, steps, *refs):
     step = pl.program_id(0)
-    (sum_two_ref, s1_ref, remote_ref, m2_ref, q2_ref, k2_ref, v2_ref, p2_ref,
-     source_ref, m1_ref, q1_ref, k1_ref, v1_ref, p1_ref, ws_ref, wc_ref, table_ref), refs = refs[:17], refs[17:]
+    (sum_two_ref, s1_ref, remote_ref, m2_ref, q2_ref, k2_ref, v2_ref, shares_ref, m1_ref,
+     source_ref, q1_ref, k1_ref, v1_ref, ws_ref, wc_ref, table_ref), refs = refs[:16], refs[16:]
     if scatters:
         (dwin, dwout, dtable_in), refs = refs[:3], refs[3:]
-    (grad_remote_ref, grad_source_ref), refs = refs[:2], refs[2:]
+    (grad_remote_out, grad_source_out), refs = refs[:2], refs[2:]
     if scatters:
-        units, refs = refs[:5], refs[5:]
+        units, refs = refs[:8], refs[8:]
     else:
         (dself_ref, dcross_ref, dtable_ref), refs = refs[:3], refs[3:]
-    (up_ref, gq_ref, gk_ref, gv_ref, keep_ref, accs_ref, accc_ref, acct_ref), refs = refs[:8], refs[8:]
+    (up_ref, gq_ref, gk_ref, gv_ref, gk2_ref, gv2_ref, keep_ref, acco_ref, accc_ref, acct_ref, out_sem), refs = (
+        refs[:11], refs[11:])
     if scatters:
-        (lows_ref, lowc_ref, lowt_ref, win_own, wout_own), refs = refs[:5], refs[5:]
-        bufs = [refs[4 * i : 4 * i + 4] for i in range(5)]
-        local, *sems = refs[20:]
-        sems = (local, *sems)
-        top = lambda ref: (lambda mat, core: ref[mat].astype(F32))
-        acc = lambda ref: (lambda mat, core: ref[mat, :, :, :, core])
+        (halfc_ref, halfo_ref, halfq_ref, halfk_ref, halfv_ref, halft_ref, low_ref, lowt_ref), refs = refs[:8], refs[8:]
+        bufs = [refs[4 * i : 4 * i + 4] for i in range(8)]
+        sems = refs[32:]
+        local = sems[0]
+        lanes = lambda n: ((ALL, ALL, slice(0, n)), (ALL, ALL, slice(n, 2 * n)))
         mats = ((slice(0, 2), ALL, ALL), (slice(2, 4), ALL, ALL))
-        wide = lambda a, b: ((ALL, ALL, slice(0, a)), (ALL, ALL, slice(a, b)))
-        inner = Scatter(dwin, top(win_own), ((ALL, slice(0, 32), ALL), (ALL, slice(32, 64), ALL)), bufs[0], units[0], sems, 0)
-        outer = Scatter(dwout, top(wout_own), wide(1024, 2048), bufs[1], units[1], sems, 8)
-        cross = Scatter(lowc_ref, acc(accc_ref), mats, bufs[2], units[2], sems, 16)
-        own = Scatter(lows_ref, acc(accs_ref), mats, bufs[3], units[3], sems, 24)
-        small = Scatter(lowt_ref, lambda mat, core: lowt_ref[mat, :, :, :, core].astype(F32), wide(128, 256), bufs[4], units[4], sems, 32)
-        everything = (inner, outer, cross, own, small)
+        rows = ((ALL, slice(0, 32), ALL), (ALL, slice(32, 64), ALL))
         core = lax.axis_index("fsdp") % 2
+        plans = [
+            (dwin.at[:, :, :, :, 1 - core], rows), (dwout.at[:, :, :, :, 1 - core], lanes(1024)), (halfc_ref, mats),
+            (halfo_ref, lanes(256)), (halfq_ref, lanes(256)), (halfk_ref, lanes(256)), (halfv_ref, lanes(256)),
+            (halft_ref, lanes(128)),
+        ]
+        everything = [
+            Scatter(theirs, halves, bufs[i], units[i], sems, i * SCATTER_SLOTS)
+            for i, (theirs, halves) in enumerate(plans)
+        ]
+        inner, outer, cross, mixed, query, keys, values, small = everything
         fetch = [
-            pltpu.make_async_copy(dwin.at[:, :, :, :, core], win_own, local.at[1]),
-            pltpu.make_async_copy(dwout.at[:, :, :, :, core], wout_own, local.at[2]),
+            pltpu.make_async_copy(dwin.at[:, :, :, :, core], bufs[0][0], local.at[1]),
+            pltpu.make_async_copy(dwout.at[:, :, :, :, core], bufs[1][0], local.at[2]),
         ]
 
     @pl.when(step == 0)
     def _():
         if scatters:
-            greet()
+            hail()
+        acco_ref[...] = jnp.zeros_like(acco_ref)
+        accc_ref[...] = jnp.zeros_like(accc_ref)
+        acct_ref[...] = jnp.zeros_like(acct_ref)
+        if scatters:
+            await_hails()
             inner.start(0)
             outer.start(0)
             for copy in fetch:
                 copy.start()
-        accs_ref[...] = jnp.zeros_like(accs_ref)
-        accc_ref[...] = jnp.zeros_like(accc_ref)
-        acct_ref[...] = jnp.zeros_like(acct_ref)
 
     @pl.when(step < steps)
     def _():
         cross_backward(
-            sum_two_ref, s1_ref, remote_ref, m2_ref, q2_ref, k2_ref, v2_ref, p2_ref, wc_ref, table_ref,
-            grad_remote_ref, keep_ref.at[step], up_ref, gq_ref, gk_ref, gv_ref, Flat(accc_ref), acct_ref)
-
-    @pl.when(step >= steps)
+            step, sum_two_ref, s1_ref, remote_ref, m2_ref, q2_ref, k2_ref, v2_ref, shares_ref, wc_ref, table_ref, m1_ref,
+            keep_ref.at[step], up_ref, gq_ref, gk2_ref, gv2_ref, Flat(accc_ref), Flat(acco_ref), acct_ref)
+
+    @pl.when((step >= steps) & (step < 2 * steps))
     def _():
         self_backward(
-            keep_ref.at[step - steps], source_ref, m1_ref, q1_ref, k1_ref, v1_ref, p1_ref, ws_ref,
-            grad_source_ref, up_ref, gq_ref, gk_ref, gv_ref, Flat(accs_ref), acct_ref)
+            step - steps, keep_ref.at[step - steps], q1_ref, k1_ref, v1_ref, shares_ref, ws_ref,
+            up_ref, gq_ref, gk_ref, gv_ref, acct_ref)
+
+    tokens = source_ref.shape[0]
+
+    def weight_grad(ref):
+        return mm_tn(ref[...], source_ref[...]).astype(BF16)
+
+    def source_grad(block):
+        at = tokens_of(block, tokens // steps)
+        found = (
+            keep_ref[block]
+            + mm_nn(gq_ref[at, :], square(ws_ref, 0))
+            + mm_nn(gk_ref[at, :], square(ws_ref, 1))
+            + mm_nn(gv_ref[at, :], square(ws_ref, 2))
+        )
+        gq_ref[at, :] = found.astype(BF16)
+        copy = pltpu.make_async_copy(gq_ref.at[at, :], grad_source_out.at[at, :], out_sem.at[block])
+        copy.start()
+        return copy
+
+    def remote_grad(block):
+        at = tokens_of(block, tokens // steps)
+        found = mm_nn(gk2_ref[at, :], square(wc_ref, 1)) + mm_nn(gv2_ref[at, :], square(wc_ref, 2))
+        gk2_ref[at, :] = found.astype(BF16)
+        copy = pltpu.make_async_copy(gk2_ref.at[at, :], grad_remote_out.at[at, :], out_sem.at[steps + block])
+        copy.start()
+        return copy
 
     if not scatters:
-        @pl.when(step == 2 * steps - 1)
+        @pl.when(step == 2 * steps)
         def _():
-            dself_ref[...] = accs_ref[...].astype(BF16)
+            for index, ref in enumerate((gq_ref, gk_ref, gv_ref)):
+                dself_ref[index] = weight_grad(ref).reshape(dself_ref.shape[1:])
+            dself_ref[3] = acco_ref[0].astype(BF16)
             dcross_ref[...] = accc_ref[...].astype(BF16)
             dtable_ref[...] = acct_ref[...]
+            copies = [source_grad(block) for block in range(steps)] + [remote_grad(block) for block in range(steps)]
+            for copy in copies:
+                copy.wait()
         return
 
-    @pl.when(step == 0)
+    def move(piece, stage):
+        piece.arrive(stage)
+        piece.start(stage + 1)
+
+    @pl.when(step == 1)
     def _():
         for copy in fetch:
             copy.wait()
-        for piece in (inner, outer):
-            piece.arrive(0)
-            piece.start(1)
-
-    @pl.when(step == 1)
-    def _():
-        for piece in (inner, outer):
-            piece.arrive(1)
-            piece.start(2)
+        move(inner, 0)
+        move(outer, 0)
+
+    @pl.when(step == steps - 2)
+    def _():
+        move(inner, 1)
+        move(outer, 1)
 
     @pl.when(step == steps - 1)
     def _():
         for mat in range(4):
-            lowc_ref[mat] = accc_ref[mat].astype(BF16)
+            cross.divide(mat, accc_ref, mat)
+        mixed.divide(0, acco_ref, 0)
         cross.start(0)
-        for piece in (inner, outer):
-            piece.arrive(2)
-            piece.start(3)
+        mixed.start(0)
 
     @pl.when(step == steps)
     def _():
-        cross.arrive(0)
-        cross.start(1)
+        move(inner, 2)
+        move(outer, 2)
+        move(cross, 0)
+        move(mixed, 0)
 
     @pl.when(step == steps + 1)
     def _():
-        cross.arrive(1)
-        cross.start(2)
-
-    @pl.when(step == 2 * steps - 2)
-    def _():
-        cross.arrive(2)
-        cross.start(3)
+        move(cross, 1)
+        move(mixed, 1)
 
     @pl.when(step == 2 * steps - 1)
     def _():
-        for mat in range(4):
-            lows_ref[mat] = accs_ref[mat].astype(BF16)
-        own.start(0)
+        move(cross, 2)
+        move(mixed, 2)
+
+    @pl.when(step == 2 * steps)
+    def _():
+        low_ref[0] = weight_grad(gq_ref).reshape(low_ref.shape[1:])
+        query.divide(0, low_ref, 0)
+        query.start(0)
+        low_ref[0] = weight_grad(gk_ref).reshape(low_ref.shape[1:])
+        keys.divide(0, low_ref, 0)
+        keys.start(0)
         table = columns_from_table(acct_ref[...] + dtable_in[...]).astype(BF16)
         lowt_ref[...] = table.reshape(lowt_ref.shape)
+        small.divide(0, lowt_ref, 0)
         small.start(0)
-        for stage in range(3):
-            for piece in (own, small):
-                piece.arrive(stage)
-                piece.start(stage + 1)
+        move(query, 0)
+        low_ref[0] = weight_grad(gv_ref).reshape(low_ref.shape[1:])
+        values.divide(0, low_ref, 0)
+        values.start(0)
+        move(keys, 0)
+        move(small, 0)
+        copies = [source_grad(0)]
+        move(query, 1)
+        move(values, 0)
+        copies.append(source_grad(1))
+        move(keys, 1)
+        move(small, 1)
+        copies.append(source_grad(2))
+        move(values, 1)
+        move(query, 2)
+        copies.append(source_grad(3))
+        copies.append(remote_grad(0))
+        move(keys, 2)
+        move(small, 2)
+        copies.append(remote_grad(1))
+        move(values, 2)
+        copies.append(remote_grad(2))
+        copies.append(remote_grad(3))
         for piece in everything:
             piece.arrive(3)
         for piece in everything:
             piece.finish()
+        for copy in copies:
+            copy.wait()
 
 
 class Flat:
@@ -816,20 +955,31 @@
         self.ref[index] = values.reshape(self.ref.shape[1:])
 
 
-def sum_kernel(win_ref, wout_ref, cross_ref, own_ref, small_ref, *outs):
+def sum_kernel(*refs):
+    units, (remote_in, source_in), refs = refs[:8], refs[8:10], refs[10:]
+    (qkv, bias_one, out_one, norm_one, cross_q, cross_kv, bias_two, out_two, norm_two,
+     win, win_bias, wout, wout_bias, norm_three, remote_out, source_out), refs = refs[:16], refs[16:]
+    held, sems = refs[:10], refs[10]
+    copies = [
+        pltpu.make_async_copy(ref, buf, sems.at[i])
+        for i, (ref, buf) in enumerate(zip((*units, remote_in, source_in), held))
+    ]
+    for copy in copies:
+        copy.start()
+    for copy in copies[:8]:
+        copy.wait()
     total = lambda ref: (
         ref[0].astype(F32) + ref[1].astype(F32) + ref[2].astype(F32) + ref[3].astype(F32))
-    (qkv, bias_one, out_one, norm_one, cross_q, cross_kv, bias_two, out_two, norm_two,
-     win, win_bias, wout, wout_bias, norm_three) = outs
-    own, cross = total(own_ref), total(cross_ref)
-    qkv[...] = own[0:3]
-    out_one[...] = own[3]
+    win[...] = total(held[0])[0]
+    wout[...] = total(held[1])[0]
+    cross = total(held[2])
     cross_q[...] = cross[0]
     cross_kv[...] = cross[1:3]
     out_two[...] = cross[3]
-    win[...] = total(win_ref)[0]
-    wout[...] = total(wout_ref)[0]
-    small = jnp.transpose(total(small_ref)[0])
+    out_one[...] = total(held[3])[0]
+    for index in range(3):
+        qkv[index] = total(held[4 + index])[0]
+    small = jnp.transpose(total(held[7])[0])
     bias_one[...] = small[SELF_BQ : SELF_BQ + 3]
     norm_one[...] = small[SELF_G : SELF_G + 2]
     bias_two[...] = small[CROSS_BQ : CROSS_BQ + 3]
@@ -837,6 +987,15 @@
     wout_bias[...] = small[FFN_BO : FFN_BO + 1]
     norm_three[...] = small[FFN_G : FFN_G + 2]
     win_bias[...] = small[128:132]
+    leaving = [
+        pltpu.make_async_copy(buf, ref, sems.at[10 + i])
+        for i, (ref, buf) in enumerate(zip((remote_out, source_out), held[8:]))
+    ]
+    for arrived, copy in zip(copies[8:], leaving):
+        arrived.wait()
+        copy.start()
+    for copy in leaving:
+        copy.wait()
 
 
 def fixed(shape):
@@ -860,6 +1019,9 @@
 WIN_BLOCKS = (1,) + BLOCKS + (64, 512)
 WOUT_BLOCKS = (1,) + BLOCKS + (16, 2048)
 SMALL_BLOCKS = (1,) + BLOCKS + (16, 256)
+
+
+ONE_BLOCKS = (1,) + BLOCKS + (16, 512)
 
 
 def layer(decoder_in, memory, out_grad, tgt_len, src_len, shards=None, weights=None):
@@ -873,44 +1035,46 @@
     low, full = shape_of(tokens, width), shape_of(tokens, width, dtype=F32)
     vm = pltpu.VMEM
     dma = pltpu.SemaphoreType.DMA
-    early = lambda i: jnp.minimum(i, steps - 1)
-    late = lambda i: jnp.maximum(i - steps, 0)
+    part = lambda first: (lambda i: jnp.clip(i - first, 0, steps - 1))
     tok = lambda when: pl.BlockSpec((block, width), lambda i: (when(i), 0))
     shares = lambda when: pl.BlockSpec(shares_block, lambda i: (when(i), 0, 0))
-    half_out = lambda when: [tok(when), tok(when), tok(when), shares(when), tok(when), tok(when)]
-    shares_shape = shape_of(rows * HEADS, slots, slots)
-    half_shape = [low, low, low, shares_shape, low, full]
+    shares_shape = shape_of(2 * rows * HEADS, slots, slots)
     table_shape = shape_of(TABLE, width, dtype=F32)
     table_spec = fixed((TABLE, width))
     ins = [source, remote, tgt_len, src_len]
-    in_specs = [tok(early), tok(late), fixed(tgt_len.shape), fixed(src_len.shape)]
-    out_shape, out_specs = half_shape * 2, half_out(early) + half_out(late)
+    early, late = part(1), part(1 + steps)
+    in_specs = [fixed(source.shape), tok(late), fixed(tgt_len.shape), fixed(src_len.shape)]
+    out_shape = [low, low, low, low, full] * 2 + [shares_shape]
+    out_specs = [ANYWHERE] * 3 + [tok(early)] * 2 + [tok(late)] * 5
+    out_specs += [shares(lambda i: jnp.clip(i - 1, 0, 2 * steps - 1))]
     scratch = []
     if shards is not None:
-        ins += list(shards)
-        in_specs += [ANYWHERE] * 8
+        big, small = shards
+        ins += [*big, *small]
+        in_specs += [ANYWHERE] * 7 + [fixed(array.shape) for array in small]
         out_shape += [table_shape, shape_of(*SQUARES), shape_of(*SQUARES), shape_of(*WIN_BLOCKS), shape_of(*WOUT_BLOCKS)]
         out_specs += [table_spec] + [ANYWHERE] * 4
-        scratch += [vm(SQUARES, BF16), vm(SQUARES, BF16), vm(SMALL_BLOCKS, BF16)]
-        scratch += [dma((GATHER_SLOTS,)), dma((GATHER_SLOTS,)), dma((GATHER_SLOTS,)), dma((2,))]
+        scratch += [vm(SQUARES, BF16), vm(SQUARES, BF16), vm(SMALL_BLOCKS, BF16), vm((1, 16, 256), BF16), vm((256, 128), F32)]
+        scratch += [dma((GATHER_SLOTS,)), dma((GATHER_SLOTS,)), dma((GATHER_SLOTS,))]
     else:
         ws, wc, win, wout, table = weights
         ws, wc = ws.reshape(SQUARES), wc.reshape(SQUARES)
         ins += [ws, wc, table]
         in_specs += [fixed(SQUARES), fixed(SQUARES), table_spec]
-    scratch += [vm((slots, slots), F32), vm((block, width), F32), vm((steps, block, width), F32), vm((rows, 2, slots), F32)]
+    scratch += [vm((2, rows, slots, slots), F32), vm((block, width), F32), vm((steps, block, width), F32), vm((rows, 2, slots), F32)]
+    scratch += [vm((tokens, width), BF16)] * 3 + [dma((5,))]
     outs = pl.pallas_call(
         functools.partial(first_kernel, shards is not None, steps),
-        grid=(2 * steps,), in_specs=in_specs, out_specs=out_specs, out_shape=out_shape, scratch_shapes=scratch,
+        grid=(1 + 2 * steps,), in_specs=in_specs, out_specs=out_specs, out_shape=out_shape, scratch_shapes=scratch,
         compiler_params=params(60 << 20, None if shards is None else 1), name="first",
     )(*ins)
-    q1, k1, v1, p1, m1, s1, q2, k2, v2, p2, m2, s2 = outs[:FIRST_OUT]
+    q1, k1, v1, m1, s1, q2, k2, v2, m2, s2, both = outs[:FIRST_OUT]
     if shards is not None:
         table, ws, wc, win, wout = outs[FIRST_OUT:]
         win = win.reshape(-1, width)
         wout = wout.reshape(width, -1)
     hidden = win.shape[0]
-    now = lambda i: i
+    now = part(0)
     result, sum_two, dwin, dwout, dtable = pl.pallas_call(
         ffn_kernel,
         grid=(steps,),
@@ -925,34 +1089,35 @@
         compiler_params=params(60 << 20), name="feed_forward",
     )(s2, out_grad.reshape(tokens, width), win, wout, table)
 
-    ins = [sum_two, s1, remote, m2, q2, k2, v2, p2, source, m1, q1, k1, v1, p1, ws, wc, table]
-    in_specs = [tok(early)] * 7 + [shares(early)] + [tok(late)] * 5 + [shares(late)]
+    early, late = part(0), part(steps)
+    ins = [sum_two, s1, remote, m2, q2, k2, v2, both, m1, source, q1, k1, v1, ws, wc, table]
+    in_specs = [tok(early)] * 7 + [shares(lambda i: jnp.where(i < steps, i + steps, jnp.minimum(i - steps, steps - 1)))]
+    in_specs += [tok(early), fixed(source.shape)] + [tok(late)] * 3
     in_specs += [fixed(SQUARES), fixed(SQUARES), table_spec]
-    out_shape, out_specs = [low, low], [tok(early), tok(late)]
-    scratch = [vm((block, width), BF16)] * 4 + [
-        vm((steps, block, width), F32), vm(SQUARES, F32), vm(SQUARES, F32), vm((TABLE, width), F32)]
+    out_shape, out_specs = [low, low], [ANYWHERE, ANYWHERE]
+    scratch = [vm((block, width), BF16)] + [vm((tokens, width), BF16)] * 5 + [
+        vm((steps, block, width), F32), vm(ONE_BLOCKS, F32), vm(SQUARES, F32), vm((TABLE, width), F32), dma((2 * steps,))]
     if shards is not None:
         ins += [dwin.reshape(WIN_BLOCKS), dwout.reshape(WOUT_BLOCKS), dtable]
         in_specs += [ANYWHERE, ANYWHERE, table_spec]
-        every = (WIN_BLOCKS, WOUT_BLOCKS, SQUARES, SQUARES, SMALL_BLOCKS)
-        out_shape += [shape_of(4, s[0], s[5], s[6]) for s in every]
-        out_specs += [ANYWHERE] * 5
-        scratch += [vm(SQUARES, BF16), vm(SQUARES, BF16), vm(SMALL_BLOCKS, BF16)]
-        scratch += [vm(s[:4] + s[5:], BF16) for s in every[:2]]
-        cut = ((0, 2, 1), (0, 1, 2), (2, 1, 1), (2, 1, 1), (0, 1, 2))
+        every = (WIN_BLOCKS, WOUT_BLOCKS, SQUARES, ONE_BLOCKS, ONE_BLOCKS, ONE_BLOCKS, ONE_BLOCKS, SMALL_BLOCKS)
+        unit_shapes = [(4, s[0], s[5], s[6]) for s in every]
+        out_shape += [shape_of(*s) for s in unit_shapes]
+        out_specs += [ANYWHERE] * 8
+        scratch += [vm(s[:4] + s[5:], BF16) for s in every[2:]]
+        scratch += [vm(ONE_BLOCKS, BF16), vm(SMALL_BLOCKS, BF16)]
+        cut = ((1, 2, 1), (1, 1, 2), (2, 1, 1)) + ((1, 1, 2),) * 5
         for s, (m, r, l) in zip(every, cut):
-            mats = s[0] // max(m, 1)
             scratch += [
                 vm(s[:4] + s[5:], BF16), vm(s[:4] + s[5:], BF16),
-                vm((2, mats, 4, s[5] // r, s[6] // l), BF16), vm((2, s[0], 4, s[5], s[6]), BF16)]
-        slots_all = 5 * SCATTER_SLOTS
-        scratch += [dma((slots_all,)), dma((slots_all,)), dma((slots_all,))]
+                vm((2, s[0] // m, 4, s[5] // r, s[6] // l), BF16), vm((2, s[0], 4, s[5], s[6]), BF16)]
+        scratch += [dma((8 * SCATTER_SLOTS,))] * 3
     else:
         out_shape += [shape_of(*SQUARES), shape_of(*SQUARES), table_shape]
         out_specs += [fixed(SQUARES), fixed(SQUARES), table_spec]
     grad_remote, grad_source, *tail = pl.pallas_call(
         functools.partial(last_kernel, shards is not None, steps),
-        grid=(2 * steps,), in_specs=in_specs, out_specs=out_specs, out_shape=out_shape, scratch_shapes=scratch,
+        grid=(2 * steps + 1,), in_specs=in_specs, out_specs=out_specs, out_shape=out_shape, scratch_shapes=scratch,
         compiler_params=params(63 << 20, None if shards is None else 2), name="last",
     )(*ins)
     as_rows = lambda array: array.reshape(rows, slots, width)
@@ -961,12 +1126,16 @@
         grads = (dself.reshape(4, 512, 512), dcross.reshape(4, 512, 512), dwin, dwout, dtable + dtable_last)
     else:
         f = lambda *shape: shape_of(*shape, dtype=F32)
-        grads = pl.pallas_call(
+        in_vm = pl.BlockSpec(memory_space=pltpu.VMEM)
+        *grads, grad_remote, grad_source = pl.pallas_call(
             sum_kernel,
+            in_specs=[pl.BlockSpec(memory_space=pltpu.HBM)] * 10,
+            out_specs=[in_vm] * 14 + [pl.BlockSpec(memory_space=pltpu.HBM)] * 2,
             out_shape=[f(3, 16, 512), f(3, 16), f(16, 512), f(2, 16), f(16, 512), f(2, 16, 512), f(3, 16), f(16, 512),
-                       f(2, 16), f(64, 512), f(4, 16), f(16, 2048), f(1, 16), f(2, 16)],
-            compiler_params=pltpu.CompilerParams(vmem_limit_bytes=16 << 20), name="sum_planes",
-        )(*tail)
+                       f(2, 16), f(64, 512), f(4, 16), f(16, 2048), f(1, 16), f(2, 16), low, low],
+            scratch_shapes=[vm(s, BF16) for s in unit_shapes] + [vm((tokens, width), BF16)] * 2 + [dma((12,))],
+            compiler_params=pltpu.CompilerParams(vmem_limit_bytes=63 << 20), name="sum_planes",
+        )(*tail, grad_remote, grad_source)
     return as_rows(result), as_rows(grad_source), as_rows(grad_remote), grads
 
 
@@ -1034,25 +1203,18 @@
             small[8:10], ffn_in, small[13:].reshape(-1), ffn_out, small[10], small[11:13])
 
 
-def small_block(parts):
-    (_, self_bias, _, self_norm, _, _, cross_bias, _, cross_norm, _, ffn_in_bias, _, ffn_out_bias, ffn_norm) = parts
-    cols = ffn_out_bias.shape[0]
-    first = jnp.concatenate(
-        [self_bias, self_norm, cross_bias, cross_norm, ffn_out_bias[None], ffn_norm,
-         jnp.zeros((128 - 13, cols), BF16), ffn_in_bias.reshape(-1, cols)], axis=0)
-    return turn(jnp.pad(first, ((0, 256 - first.shape[0]), (0, 0))))
-
-
 def on_device(count, direct, decoder_in, memory, out_grad, tgt_len, src_len, *parts):
     if not direct:
         weights = gather_plain(parts, count)
         result, grad_source, grad_remote, grads = layer(
             decoder_in, memory, out_grad, tgt_len, src_len, weights=weights)
         return (result, grad_source, grad_remote, *scatter_plain(*grads, count))
-    (self_qkv, _, self_out, _, cross_q, cross_kv, _, cross_out, _, ffn_in, _, ffn_out, _, _) = parts
-    shards = [turn(part) for part in (self_qkv, self_out, cross_q, cross_kv, cross_out, ffn_in, ffn_out)]
-    shards.append(small_block(parts))
-    shards = [part.reshape((-1,) + part.shape[-2:]) for part in shards]
+    (self_qkv, self_bias, self_out, self_norm, cross_q, cross_kv, cross_bias, cross_out, cross_norm,
+     ffn_in, ffn_in_bias, ffn_out, ffn_out_bias, ffn_norm) = parts
+    big = [turn(part) for part in (self_qkv, self_out, cross_q, cross_kv, cross_out, ffn_in, ffn_out)]
+    big = [part.reshape((-1,) + part.shape[-2:]) for part in big]
+    small = [self_bias, self_norm, cross_bias, cross_norm, ffn_out_bias.reshape(1, -1), ffn_norm, ffn_in_bias.reshape(1, -1)]
+    shards = big, small
     result, grad_source, grad_remote, grads = layer(
         decoder_in, memory, out_grad, tgt_len, src_len, shards=shards)
     (qkv, bias_one, out_one, norm_one, query, pair, bias_two, out_two, norm_two, win, win_bias, wout, wout_bias,

time: 229 us -> 186 us (0.81)
  Pallas kernels: 212 us -> 184 us
  local copies, waits for them, and re-layouts: 15.7 us -> 1.22 us
    pallas_call x1, Pallas kernels: 56 us -> 42.8 us  [layer(): pl.pallas_call(ffn_kernel, grid=(steps,), in_specs=[tok(now), tok(now), f...]
    unnamed x19 -> x0, local copies, waits for them, and re-layouts: 12.8 us -> none
    pallas_call x1, Pallas kernels: 86 us -> 74.3 us  [layer(): pl.pallas_call(functools.partial(last_kernel, shards is not None, steps),...]
    pallas_call x1, Pallas kernels: 69.4 us -> 62.2 us  [layer(): pl.pallas_call(functools.partial(first_kernel, shards is not None, steps)...]
    pallas_call x1, Pallas kernels: 0.84 us -> 4.87 us  [layer(): pl.pallas_call(sum_kernel, in_specs=[pl.BlockSpec(memory_space=pltpu.HBM)...]
where the time goes in v3:
time: 186 us
  Pallas kernels  184 us (99%)
    pallas_call x1, Pallas kernels, layer(): pl.pallas_call(functools.partial(last_kernel, shards is not None, steps),...  74.3 us
    pallas_call x1, Pallas kernels, layer(): pl.pallas_call(functools.partial(first_kernel, shards is not None, steps)...  62.2 us
    pallas_call x1, Pallas kernels, layer(): pl.pallas_call(ffn_kernel, grid=(steps,), in_specs=[tok(now), tok(now), f...  42.8 us
    pallas_call x1, Pallas kernels, layer(): pl.pallas_call(sum_kernel, in_specs=[pl.BlockSpec(memory_space=pltpu.HBM)...  4.87 us

profile of v3, /device:TPU:0, one launch (start us, length us, event | category | flops | bytes accessed | tf_op | source)
XLA Modules:
  0.0 186.0 jit_solution(18238751227901909061)
XLA Ops:
  0.7 62.2 %first.1 = (bf16[2048,512]{1,0:T(8,128)(2,1)}, bf16[2048,512]{1,0:T(8,128)(2,1)}, bf16[2048,512]{1,0:T(8,128)(2,1)}, bf16[2048,512]{1,0:T(8,128)(2,1)}, f32[2048...) custom-call(bf16[2048,512]{1,0:T(8,128)(2,1)} %bitcast.37, ...), custom_call_target="tpu_custom_call" | custom-call | tf_op jit(solution)/shard_map/first/pallas_call | solution.py:1066
  62.9 42.8 %feed_forward.1 = (bf16[2048,512]{1,0:T(8,128)(2,1)}, f32[2048,512]{1,0:T(8,128)}, bf16[2048,512]{1,0:T(8,128)(2,1)}, bf16[512,2048]{1,0:T(8,128)(2,1)}, f32[24,512]{1,0:T(8,128)}) custom-call(f32[2048,512]{1,0:T(8,128)} %get-tuple-element.64.summed_two_ref, bf16[2048,512]{1,0:T(8,128)(2,1)} %bitcast.41, bf16[2048,512]{1,0:T(8,128)(2,1)} %bitcast.44, ...), custom_call_target="tpu_custom_call" | custom-call | tf_op jit(solution)/shard_map/feed_forward/pallas_call | solution.py:1078
  105.6 74.3 %last.1 = (bf16[2048,512]{1,0:T(8,128)(2,1)}, bf16[2048,512]{1,0:T(8,128)(2,1)}, bf16[4,1,64,512]{3,2,1,0:T(8,128)(2,1)}, bf16[4,1,16,2048]{3,2,1,0:T(8,128)(2,1...) custom-call(f32[2048,512]{1,0:T(8,128)} %get-tuple-element.69.refs_0, ...), custom_call_target="tpu_custom_call" | custom-call | tf_op jit(solution)/shard_map/last/pallas_call | solution.py:1118
  179.9 4.9 %sum_planes.1 = (f32[3,16,512]{2,1,0:T(8,128)}, f32[3,16]{1,0:T(4,128)}, f32[16,512]{1,0:T(8,128)}, f32[2,16]{1,0:T(2,128)}, f32[16,512]{1,0:T(8,128)}, /*index=...) custom-call(bf16[4,1,64,512]{3,2,1,0:T(8,128)(2,1)} %get-tuple-eleme, ...), custom_call_target="tpu_custom_call" | custom-call | tf_op jit(solution)/shard_map/sum_planes/pallas_call | solution.py:1130
  184.8 1.2 reshape.108

commit v4 on v3

--- a/solution.py
+++ b/solution.py
@@ -409,14 +409,17 @@
     tokens = source_ref.shape[0]
 
     def project(index, out_ref, row, factor):
-        for part in range(4):
-            at = tokens_of(part, tokens // 4)
+        def one_part(part, carry):
+            at = tokens_of(part, tokens // steps)
             found = mm_nt(source_ref[at, :], square(ws_ref, index))
             if row is not None:
                 found = found + vrow(table_ref, row)
             if factor is not None:
                 found = found * factor
             out_ref[at, :] = found.astype(BF16)
+            return carry
+
+        lax.fori_loop(0, steps, one_part, 0, unroll=True)
 
     def project_query():
         project(0, q1_ref, SELF_BQ, HEAD_DIM**-0.5)
@@ -552,18 +555,19 @@
 
 
 def ffn_kernel(
-    summed_two_ref, upstream_ref, win_ref, wout_ref, table_ref,
+    summed_two_ref, upstream_ref, win_any, wout_any, table_ref,
     result_ref, sum_two_ref, dwin_ref, dwout_ref, dtable_ref,
     normed_two_ref, hidden_ref, active_ref, slope_ref, accum_ref,
-    low_two_ref, grad_low_ref, accin_ref, accout_ref, acct_ref,
+    low_two_ref, grad_low_ref, accin_ref, accout_ref, acct_ref, win_ref, wout_ref, in_sem,
 ):
     step = pl.program_id(0)
     chunks = win_ref.shape[0] // 512
+    bring = (pltpu.make_async_copy(win_any, win_ref, in_sem.at[0]), pltpu.make_async_copy(wout_any, wout_ref, in_sem.at[1]))
 
     @pl.when(step == 0)
     def _():
-        accin_ref[...] = jnp.zeros_like(accin_ref)
-        accout_ref[...] = jnp.zeros_like(accout_ref)
+        for copy in bring:
+            copy.start()
         acct_ref[...] = jnp.zeros_like(acct_ref)
 
     normed_two, inverse_two = norm_stats(summed_two_ref[...])
@@ -571,7 +575,11 @@
     hidden_two = normed_two * vrow(table_ref, CROSS_G) + vrow(table_ref, CROSS_S)
     hidden_ref[...] = hidden_two
     low_two_ref[...] = hidden_two.astype(BF16)
-    accum_ref[...] = jnp.zeros_like(accum_ref)
+
+    @pl.when(step == 0)
+    def _():
+        for copy in bring:
+            copy.wait()
 
     def expand(chunk):
         units = slice(chunk * 512, chunk * 512 + 512)
@@ -612,11 +620,15 @@
     for chunk in range(chunks):
         units = slice(chunk * 512, chunk * 512 + 512)
         grad_active = mm_nn(grad_three, wout_ref[:, units])
-        accout_ref[:, units] += mm_tn(grad_three, active_ref[:, units])
+        total = jnp.where(step == 0, 0.0, accout_ref[:, units]) + mm_tn(grad_three, active_ref[:, units])
+        accout_ref[:, units] = total
+        dwout_ref[:, units] = total.astype(BF16)
         grad_expanded = (grad_active * slope_ref[:, units].astype(F32)).astype(BF16)
         slope_ref[:, units] = grad_expanded
         acct_ref[FFN_BI + chunk : FFN_BI + chunk + 1, :] += column_sum(grad_expanded)
-        accin_ref[units, :] += mm_tn(grad_expanded, low_two_ref[...])
+        total = jnp.where(step == 0, 0.0, accin_ref[units, :]) + mm_tn(grad_expanded, low_two_ref[...])
+        accin_ref[units, :] = total
+        dwin_ref[units, :] = total.astype(BF16)
     accum_ref[...] += mm_nn(slope_ref[...], win_ref[...])
     grad_hidden_two = accum_ref[...]
     normed_two = normed_two_ref[...]
@@ -626,8 +638,6 @@
 
     @pl.when(step == pl.num_programs(0) - 1)
     def _():
-        dwin_ref[...] = accin_ref[...].astype(BF16)
-        dwout_ref[...] = accout_ref[...].astype(BF16)
         dtable_ref[...] = acct_ref[...]
 
 
@@ -641,13 +651,11 @@
     grad_two = sum_two_ref[...].astype(BF16)
     add_row(acct_ref, CROSS_BO, column_sum(grad_two))
     up_ref[...] = mm_nn(grad_two, square(weight_ref, 3)).astype(BF16)
-    acc_ref[3] += mm_tn(grad_two, mixture_ref[...])
-    def one_row(row, carry):
+    acc_ref[3] = jnp.where(step == 0, 0.0, acc_ref[3]) + mm_tn(grad_two, mixture_ref[...])
+    for row in range(STEP_ROWS):
         attend_rows_back(
             up_ref, query_ref, keys_ref, values_ref, shares_ref, gq_ref, gk_ref, gv_ref, row,
             tokens_of(row, slots), tokens_of(step * STEP_ROWS + row, slots))
-        return carry
-    lax.fori_loop(0, STEP_ROWS, one_row, 0)
     normed_one, inverse_one = norm_stats(summed_one_ref[...])
     low = (normed_one * vrow(table_ref, SELF_G) + vrow(table_ref, SELF_S)).astype(BF16)
     grad_query, grad_keys, grad_values = gq_ref[block, :], gk_ref[block, :], gv_ref[block, :]
@@ -658,12 +666,12 @@
     add_row(acct_ref, SELF_S, column_sum(grad_hidden_one))
     sum_one = norm_back(grad_hidden_one, normed_one, inverse_one, vrow(table_ref, SELF_G))
     sum_one_ref[...] = sum_one
-    acc_ref[0] += mm_tn(grad_query, low)
-    acc_ref[1] += mm_tn(grad_keys, remote_ref[...])
-    acc_ref[2] += mm_tn(grad_values, remote_ref[...])
+    acc_ref[0] = jnp.where(step == 0, 0.0, acc_ref[0]) + mm_tn(grad_query, low)
+    acc_ref[1] = jnp.where(step == 0, 0.0, acc_ref[1]) + mm_tn(grad_keys, remote_ref[...])
+    acc_ref[2] = jnp.where(step == 0, 0.0, acc_ref[2]) + mm_tn(grad_values, remote_ref[...])
     grad_one = sum_one.astype(BF16)
     add_row(acct_ref, SELF_BO, column_sum(grad_one))
-    acc_out_ref[0] += mm_tn(grad_one, first_mixture_ref[...])
+    acc_out_ref[0] = jnp.where(step == 0, 0.0, acc_out_ref[0]) + mm_tn(grad_one, first_mixture_ref[...])
 
 
 def self_backward(
@@ -673,12 +681,10 @@
     slots = shares_ref.shape[1]
     block = tokens_of(step, STEP_ROWS * slots)
     up_ref[...] = mm_nn(sum_one_ref[...].astype(BF16), square(weight_ref, 3)).astype(BF16)
-    def one_row(row, carry):
+    for row in range(STEP_ROWS):
         attend_rows_back(
             up_ref, query_ref, keys_ref, values_ref, shares_ref, gq_ref, gk_ref, gv_ref, row,
             tokens_of(row, slots), tokens_of(step * STEP_ROWS + row, slots))
-        return carry
-    lax.fori_loop(0, STEP_ROWS, one_row, 0)
     add_row(acct_ref, SELF_BQ, column_sum(gq_ref[block, :]))
     add_row(acct_ref, SELF_BV, column_sum(gv_ref[block, :]))
 
@@ -738,11 +744,11 @@
         z, y, x, core = place()
         if stage == 0:
             for mat in range(self.total.shape[0]):
-                self.total[mat] = (self.total[mat].astype(F32) + self.pair[mat].astype(F32)).astype(BF16)
+                self.total[mat] = self.total[mat] + self.pair[mat]
         if stage == 1:
             for i, (h, at) in enumerate(zip(self.halves, ((1 - y, x), (y, 1 - x)))):
-                old = self.total[h[0], :, at[0], at[1], h[1], h[2]].astype(F32)
-                self.total[h[0], :, at[0], at[1], h[1], h[2]] = (old + self.far[i].astype(F32)).astype(BF16)
+                old = self.total[h[0], :, at[0], at[1], h[1], h[2]]
+                self.total[h[0], :, at[0], at[1], h[1], h[2]] = old + self.far[i]
         if stage == 2:
             old = self.total[:, :, y, x].astype(F32)
             self.total[:, :, y, x] = (
@@ -761,7 +767,7 @@
 def last_kernel(scatters, steps, *refs):
     step = pl.program_id(0)
     (sum_two_ref, s1_ref, remote_ref, m2_ref, q2_ref, k2_ref, v2_ref, shares_ref, m1_ref,
-     source_ref, q1_ref, k1_ref, v1_ref, ws_ref, wc_ref, table_ref), refs = refs[:16], refs[16:]
+     source_any, q1_ref, k1_ref, v1_ref, ws_any, wc_ref, table_ref), refs = refs[:16], refs[16:]
     if scatters:
         (dwin, dwout, dtable_in), refs = refs[:3], refs[3:]
     (grad_remote_out, grad_source_out), refs = refs[:2], refs[2:]
@@ -769,8 +775,11 @@
         units, refs = refs[:8], refs[8:]
     else:
         (dself_ref, dcross_ref, dtable_ref), refs = refs[:3], refs[3:]
-    (up_ref, gq_ref, gk_ref, gv_ref, gk2_ref, gv2_ref, keep_ref, acco_ref, accc_ref, acct_ref, out_sem), refs = (
-        refs[:11], refs[11:])
+    (up_ref, g_ref, gk2_ref, gv2_ref, keep_ref, acco_ref, accc_ref, acct_ref, out_sem, source_ref, ws_ref, in_sem), refs = (
+        refs[:12], refs[12:])
+    bring = (
+        pltpu.make_async_copy(ws_any, ws_ref, in_sem.at[0]), pltpu.make_async_copy(source_any, source_ref, in_sem.at[1]))
+    gq_ref, gk_ref, gv_ref = (g_ref.at[i] for i in range(3))
     if scatters:
         (halfc_ref, halfo_ref, halfq_ref, halfk_ref, halfv_ref, halft_ref, low_ref, lowt_ref), refs = refs[:8], refs[8:]
         bufs = [refs[4 * i : 4 * i + 4] for i in range(8)]
@@ -799,8 +808,6 @@
     def _():
         if scatters:
             hail()
-        acco_ref[...] = jnp.zeros_like(acco_ref)
-        accc_ref[...] = jnp.zeros_like(accc_ref)
         acct_ref[...] = jnp.zeros_like(acct_ref)
         if scatters:
             await_hails()
@@ -808,6 +815,8 @@
             outer.start(0)
             for copy in fetch:
                 copy.start()
+        for copy in bring:
+            copy.start()
 
     @pl.when(step < steps)
     def _():
@@ -815,6 +824,11 @@
             step, sum_two_ref, s1_ref, remote_ref, m2_ref, q2_ref, k2_ref, v2_ref, shares_ref, wc_ref, table_ref, m1_ref,
             keep_ref.at[step], up_ref, gq_ref, gk2_ref, gv2_ref, Flat(accc_ref), Flat(acco_ref), acct_ref)
 
+    @pl.when(step == steps)
+    def _():
+        for copy in bring:
+            copy.wait()
+
     @pl.when((step >= steps) & (step < 2 * steps))
     def _():
         self_backward(
@@ -823,8 +837,14 @@
 
     tokens = source_ref.shape[0]
 
-    def weight_grad(ref):
-        return mm_tn(ref[...], source_ref[...]).astype(BF16)
+    def weight_grad(index):
+        return mm_tn(g_ref[index], source_ref[...]).astype(BF16)
+
+    def results(block):
+        at = tokens_of(block, tokens // steps)
+        return (
+            pltpu.make_async_copy(gq_ref.at[at, :], grad_source_out.at[at, :], out_sem.at[block]),
+            pltpu.make_async_copy(gk2_ref.at[at, :], grad_remote_out.at[at, :], out_sem.at[steps + block]))
 
     def source_grad(block):
         at = tokens_of(block, tokens // steps)
@@ -835,36 +855,35 @@
             + mm_nn(gv_ref[at, :], square(ws_ref, 2))
         )
         gq_ref[at, :] = found.astype(BF16)
-        copy = pltpu.make_async_copy(gq_ref.at[at, :], grad_source_out.at[at, :], out_sem.at[block])
-        copy.start()
-        return copy
+        results(block)[0].start()
 
     def remote_grad(block):
         at = tokens_of(block, tokens // steps)
         found = mm_nn(gk2_ref[at, :], square(wc_ref, 1)) + mm_nn(gv2_ref[at, :], square(wc_ref, 2))
         gk2_ref[at, :] = found.astype(BF16)
-        copy = pltpu.make_async_copy(gk2_ref.at[at, :], grad_remote_out.at[at, :], out_sem.at[steps + block])
-        copy.start()
-        return copy
+        results(block)[1].start()
 
     if not scatters:
         @pl.when(step == 2 * steps)
         def _():
-            for index, ref in enumerate((gq_ref, gk_ref, gv_ref)):
-                dself_ref[index] = weight_grad(ref).reshape(dself_ref.shape[1:])
+            for index in range(3):
+                dself_ref[index] = weight_grad(index).reshape(dself_ref.shape[1:])
             dself_ref[3] = acco_ref[0].astype(BF16)
             dcross_ref[...] = accc_ref[...].astype(BF16)
             dtable_ref[...] = acct_ref[...]
-            copies = [source_grad(block) for block in range(steps)] + [remote_grad(block) for block in range(steps)]
-            for copy in copies:
-                copy.wait()
+            for block in range(steps):
+                source_grad(block)
+                remote_grad(block)
+            for block in range(steps):
+                for copy in results(block):
+                    copy.wait()
         return
 
     def move(piece, stage):
         piece.arrive(stage)
         piece.start(stage + 1)
 
-    @pl.when(step == 1)
+    @pl.when(step == 0)
     def _():
         for copy in fetch:
             copy.wait()
@@ -886,13 +905,13 @@
 
     @pl.when(step == steps)
     def _():
+        move(cross, 0)
+        move(mixed, 0)
+
+    @pl.when(step == steps + 1)
+    def _():
         move(inner, 2)
         move(outer, 2)
-        move(cross, 0)
-        move(mixed, 0)
-
-    @pl.when(step == steps + 1)
-    def _():
         move(cross, 1)
         move(mixed, 1)
 
@@ -903,45 +922,50 @@
 
     @pl.when(step == 2 * steps)
     def _():
-        low_ref[0] = weight_grad(gq_ref).reshape(low_ref.shape[1:])
-        query.divide(0, low_ref, 0)
-        query.start(0)
-        low_ref[0] = weight_grad(gk_ref).reshape(low_ref.shape[1:])
-        keys.divide(0, low_ref, 0)
-        keys.start(0)
+        parts = (query, keys, values)
+
+        def one_matrix(index, carry):
+            low_ref[0] = weight_grad(index).reshape(low_ref.shape[1:])
+            for at, piece in enumerate(parts):
+                @pl.when(index == at)
+                def _():
+                    piece.divide(0, low_ref, 0)
+                    piece.start(0)
+                    if at > 0:
+                        move(parts[at - 1], 0)
+            return carry
+
+        lax.fori_loop(0, 3, one_matrix, 0)
         table = columns_from_table(acct_ref[...] + dtable_in[...]).astype(BF16)
         lowt_ref[...] = table.reshape(lowt_ref.shape)
         small.divide(0, lowt_ref, 0)
         small.start(0)
-        move(query, 0)
-        low_ref[0] = weight_grad(gv_ref).reshape(low_ref.shape[1:])
-        values.divide(0, low_ref, 0)
-        values.start(0)
-        move(keys, 0)
-        move(small, 0)
-        copies = [source_grad(0)]
-        move(query, 1)
-        move(values, 0)
-        copies.append(source_grad(1))
-        move(keys, 1)
-        move(small, 1)
-        copies.append(source_grad(2))
-        move(values, 1)
-        move(query, 2)
-        copies.append(source_grad(3))
-        copies.append(remote_grad(0))
-        move(keys, 2)
-        move(small, 2)
-        copies.append(remote_grad(1))
-        move(values, 2)
-        copies.append(remote_grad(2))
-        copies.append(remote_grad(3))
+        moves = (
+            (((values, 0), (query, 1)), ((keys, 1), (small, 0))),
+            ((), ((values, 1),)),
+            (((query, 2), (small, 1)), ((keys, 2),)),
+            (((values, 2), (small, 2)), ()),
+        )
+
+        def one_block(block, carry):
+            for half, work in enumerate((source_grad, remote_grad)):
+                work(block)
+                for at in range(4):
+                    if moves[at][half]:
+                        @pl.when(block == at)
+                        def _():
+                            for piece, stage in moves[at][half]:
+                                move(piece, stage)
+            return carry
+
+        lax.fori_loop(0, steps, one_block, 0)
         for piece in everything:
             piece.arrive(3)
         for piece in everything:
             piece.finish()
-        for copy in copies:
-            copy.wait()
+        for block in range(steps):
+            for copy in results(block):
+                copy.wait()
 
 
 class Flat:
@@ -986,7 +1010,8 @@
     norm_two[...] = small[CROSS_G : CROSS_G + 2]
     wout_bias[...] = small[FFN_BO : FFN_BO + 1]
     norm_three[...] = small[FFN_G : FFN_G + 2]
-    win_bias[...] = small[128:132]
+    for k in range(4):
+        win_bias[:, k * 16 : k * 16 + 16] = small[128 + k : 129 + k]
     leaving = [
         pltpu.make_async_copy(buf, ref, sems.at[10 + i])
         for i, (ref, buf) in enumerate(zip((remote_out, source_out), held[8:]))
@@ -1078,13 +1103,14 @@
     result, sum_two, dwin, dwout, dtable = pl.pallas_call(
         ffn_kernel,
         grid=(steps,),
-        in_specs=[tok(now), tok(now), fixed(win.shape), fixed(wout.shape), table_spec],
+        in_specs=[tok(now), tok(now), ANYWHERE, ANYWHERE, table_spec],
         out_specs=[tok(now), tok(now), fixed(win.shape), fixed(wout.shape), table_spec],
         out_shape=[low, full, shape_of(*win.shape), shape_of(*wout.shape), table_shape],
         scratch_shapes=[
             vm((block, width), F32), vm((block, width), F32), vm((block, hidden), BF16), vm((block, hidden), BF16),
             vm((block, width), F32), vm((block, width), BF16), vm((block, width), BF16),
             vm(win.shape, F32), vm(wout.shape, F32), vm((TABLE, width), F32),
+            vm(win.shape, BF16), vm(wout.shape, BF16), dma((2,)),
         ],
         compiler_params=params(60 << 20), name="feed_forward",
     )(s2, out_grad.reshape(tokens, width), win, wout, table)
@@ -1092,11 +1118,12 @@
     early, late = part(0), part(steps)
     ins = [sum_two, s1, remote, m2, q2, k2, v2, both, m1, source, q1, k1, v1, ws, wc, table]
     in_specs = [tok(early)] * 7 + [shares(lambda i: jnp.where(i < steps, i + steps, jnp.minimum(i - steps, steps - 1)))]
-    in_specs += [tok(early), fixed(source.shape)] + [tok(late)] * 3
-    in_specs += [fixed(SQUARES), fixed(SQUARES), table_spec]
+    in_specs += [tok(early), ANYWHERE] + [tok(late)] * 3
+    in_specs += [ANYWHERE, fixed(SQUARES), table_spec]
     out_shape, out_specs = [low, low], [ANYWHERE, ANYWHERE]
-    scratch = [vm((block, width), BF16)] + [vm((tokens, width), BF16)] * 5 + [
-        vm((steps, block, width), F32), vm(ONE_BLOCKS, F32), vm(SQUARES, F32), vm((TABLE, width), F32), dma((2 * steps,))]
+    scratch = [vm((block, width), BF16), vm((3, tokens, width), BF16)] + [vm((tokens, width), BF16)] * 2 + [
+        vm((steps, block, width), F32), vm(ONE_BLOCKS, F32), vm(SQUARES, F32), vm((TABLE, width), F32), dma((2 * steps,)),
+        vm((tokens, width), BF16), vm(SQUARES, BF16), dma((2,))]
     if shards is not None:
         ins += [dwin.reshape(WIN_BLOCKS), dwout.reshape(WOUT_BLOCKS), dtable]
         in_specs += [ANYWHERE, ANYWHERE, table_spec]
@@ -1132,7 +1159,7 @@
             in_specs=[pl.BlockSpec(memory_space=pltpu.HBM)] * 10,
             out_specs=[in_vm] * 14 + [pl.BlockSpec(memory_space=pltpu.HBM)] * 2,
             out_shape=[f(3, 16, 512), f(3, 16), f(16, 512), f(2, 16), f(16, 512), f(2, 16, 512), f(3, 16), f(16, 512),
-                       f(2, 16), f(64, 512), f(4, 16), f(16, 2048), f(1, 16), f(2, 16), low, low],
+                       f(2, 16), f(64, 512), f(1, 64), f(16, 2048), f(1, 16), f(2, 16), low, low],
             scratch_shapes=[vm(s, BF16) for s in unit_shapes] + [vm((tokens, width), BF16)] * 2 + [dma((12,))],
             compiler_params=pltpu.CompilerParams(vmem_limit_bytes=63 << 20), name="sum_planes",
         )(*tail, grad_remote, grad_source)

time: 186 us -> 181 us (0.973)
  Pallas kernels: 184 us -> 180 us
    pallas_call x1, Pallas kernels: 74.3 us -> 70 us  [layer(): pl.pallas_call(functools.partial(last_kernel, shards is not None, steps),...]
where the time goes in v4:
time: 181 us
  Pallas kernels  180 us (99%)
    pallas_call x1, Pallas kernels, layer(): pl.pallas_call(functools.partial(last_kernel, shards is not None, steps),...  70 us
    pallas_call x1, Pallas kernels, layer(): pl.pallas_call(functools.partial(first_kernel, shards is not None, steps)...  62.2 us
    pallas_call x1, Pallas kernels, layer(): pl.pallas_call(ffn_kernel, grid=(steps,), in_specs=[tok(now), tok(now), A...  42.9 us
    pallas_call x1, Pallas kernels, layer(): pl.pallas_call(sum_kernel, in_specs=[pl.BlockSpec(memory_space=pltpu.HBM)...  4.87 us

profile of v4, /device:TPU:0, one launch (start us, length us, event | category | flops | bytes accessed | tf_op | source)
XLA Modules:
  0.0 180.8 jit_solution(12491457728383630382)
XLA Ops:
  0.7 62.2 %first.1 = (bf16[2048,512]{1,0:T(8,128)(2,1)}, bf16[2048,512]{1,0:T(8,128)(2,1)}, bf16[2048,512]{1,0:T(8,128)(2,1)}, bf16[2048,512]{1,0:T(8,128)(2,1)}, f32[2048...) custom-call(bf16[2048,512]{1,0:T(8,128)(2,1)} %bitcast.38, ...), custom_call_target="tpu_custom_call" | custom-call | tf_op jit(solution)/shard_map/first/pallas_call | solution.py:1091
  62.9 42.9 %feed_forward.1 = (bf16[2048,512]{1,0:T(8,128)(2,1)}, f32[2048,512]{1,0:T(8,128)}, bf16[2048,512]{1,0:T(8,128)(2,1)}, bf16[512,2048]{1,0:T(8,128)(2,1)}, f32[24,512]{1,0:T(8,128)}) custom-call(f32[2048,512]{1,0:T(8,128)} %get-tuple-element.64.summed_two_ref, bf16[2048,512]{1,0:T(8,128)(2,1)} %bitcast.42, bf16[2048,512]{1,0:T(8,128)(2,1)} %bitcast.45, ...), custom_call_target="tpu_custom_call" | custom-call | tf_op jit(solution)/shard_map/feed_forward/pallas_call | solution.py:1103
  105.8 70.0 %last.1 = (bf16[2048,512]{1,0:T(8,128)(2,1)}, bf16[2048,512]{1,0:T(8,128)(2,1)}, bf16[4,1,64,512]{3,2,1,0:T(8,128)(2,1)}, bf16[4,1,16,2048]{3,2,1,0:T(8,128)(2,1...) custom-call(f32[2048,512]{1,0:T(8,128)} %get-tuple-element.69.refs_0, ...), custom_call_target="tpu_custom_call" | custom-call | tf_op jit(solution)/shard_map/last/pallas_call | solution.py:1145
  175.8 4.9 %sum_planes.1 = (f32[3,16,512]{2,1,0:T(8,128)}, f32[3,16]{1,0:T(4,128)}, f32[16,512]{1,0:T(8,128)}, f32[2,16]{1,0:T(2,128)}, f32[16,512]{1,0:T(8,128)}, /*index=...) custom-call(bf16[4,1,64,512]{3,2,1,0:T(8,128)(2,1)} %get-tuple-eleme, ...), custom_call_target="tpu_custom_call" | custom-call | tf_op jit(solution)/shard_map/sum_planes/pallas_call | solution.py:1157

commit v5 on v4

--- a/solution.py
+++ b/solution.py
@@ -462,29 +462,28 @@
             move(small, 1)
             move(query, 1)
             move(values, 0)
+            cross.start(0)
             move(keys, 1)
             move(small, 2)
             move(query, 2)
             move(mixed, 0)
-            cross.start(0)
             move(values, 1)
+            inner.start(0)
             move(keys, 2)
             move(small, 3)
             table_from_columns(small_ref[0].reshape(512, 256).astype(F32), table_ref)
             move(mixed, 1)
             move(query, 3)
+            move(values, 2)
+            move(keys, 3)
             project_query()
-            move(values, 2)
-            inner.start(0)
-            move(keys, 3)
-            project_keys()
-            move(mixed, 2)
             for piece in (cross, inner, outer):
                 for copy in piece.locals():
                     copy.wait()
-            cross.arrive(0)
-            cross.start(1)
+            move(cross, 0)
             outer.start(0)
+            move(mixed, 2)
+            project_keys()
             move(values, 3)
             project_values()
             move(mixed, 3)

time: 181 us -> 179 us (0.989)
  Pallas kernels: 180 us -> 178 us
    pallas_call x1, Pallas kernels: 70 us -> 68.1 us  [layer(): pl.pallas_call(functools.partial(last_kernel, shards is not None, steps),...]
where the time goes in v5:
time: 179 us
  Pallas kernels  178 us (99%)
    pallas_call x1, Pallas kernels, layer(): pl.pallas_call(functools.partial(last_kernel, shards is not None, steps),...  68.1 us
    pallas_call x1, Pallas kernels, layer(): pl.pallas_call(functools.partial(first_kernel, shards is not None, steps)...  62.2 us
    pallas_call x1, Pallas kernels, layer(): pl.pallas_call(ffn_kernel, grid=(steps,), in_specs=[tok(now), tok(now), A...  42.9 us
    pallas_call x1, Pallas kernels, layer(): pl.pallas_call(sum_kernel, in_specs=[pl.BlockSpec(memory_space=pltpu.HBM)...  4.87 us

profile of v5, /device:TPU:0, one launch (start us, length us, event | category | flops | bytes accessed | tf_op | source)
XLA Modules:
  0.0 178.9 jit_solution(13873055779455425393)
XLA Ops:
  0.7 62.2 %first.1 = (bf16[2048,512]{1,0:T(8,128)(2,1)}, bf16[2048,512]{1,0:T(8,128)(2,1)}, bf16[2048,512]{1,0:T(8,128)(2,1)}, bf16[2048,512]{1,0:T(8,128)(2,1)}, f32[2048...) custom-call(bf16[2048,512]{1,0:T(8,128)(2,1)} %bitcast.38, ...), custom_call_target="tpu_custom_call" | custom-call | tf_op jit(solution)/shard_map/first/pallas_call | solution.py:1090
  62.8 42.9 %feed_forward.1 = (bf16[2048,512]{1,0:T(8,128)(2,1)}, f32[2048,512]{1,0:T(8,128)}, bf16[2048,512]{1,0:T(8,128)(2,1)}, bf16[512,2048]{1,0:T(8,128)(2,1)}, f32[24,512]{1,0:T(8,128)}) custom-call(f32[2048,512]{1,0:T(8,128)} %get-tuple-element.64.summed_two_ref, bf16[2048,512]{1,0:T(8,128)(2,1)} %bitcast.42, bf16[2048,512]{1,0:T(8,128)(2,1)} %bitcast.45, ...), custom_call_target="tpu_custom_call" | custom-call | tf_op jit(solution)/shard_map/feed_forward/pallas_call | solution.py:1102
  105.7 68.1 %last.1 = (bf16[2048,512]{1,0:T(8,128)(2,1)}, bf16[2048,512]{1,0:T(8,128)(2,1)}, bf16[4,1,64,512]{3,2,1,0:T(8,128)(2,1)}, bf16[4,1,16,2048]{3,2,1,0:T(8,128)(2,1...) custom-call(f32[2048,512]{1,0:T(8,128)} %get-tuple-element.69.refs_0, ...), custom_call_target="tpu_custom_call" | custom-call | tf_op jit(solution)/shard_map/last/pallas_call | solution.py:1144
  173.9 4.9 %sum_planes.1 = (f32[3,16,512]{2,1,0:T(8,128)}, f32[3,16]{1,0:T(4,128)}, f32[16,512]{1,0:T(8,128)}, f32[2,16]{1,0:T(2,128)}, f32[16,512]{1,0:T(8,128)}, /*index=...) custom-call(bf16[4,1,64,512]{3,2,1,0:T(8,128)(2,1)} %get-tuple-eleme, ...), custom_call_target="tpu_custom_call" | custom-call | tf_op jit(solution)/shard_map/sum_planes/pallas_call | solution.py:1156
